TPU v7x, 32 devices: a whole 2x2x4 slice. The times are simulated.
32 devices in a mesh: rows: 8 (over z, y), cols: 4 (over x, core).
Axes of the slice: x: 2, y: 2, z: 4, core: 2. Of those that a mesh axis runs over, the one named last changes fastest.
Arguments:
- sources: bfloat16 [262144, 128], P(('rows', 'cols')), may hold values from -6 to 6
- tiles: bfloat16 [16384, 128, 128], P(('rows', 'cols')), may hold values from -0.1875 to 0.1875
- block_list: int32 [16384, 2], P(('rows', 'cols')), may hold values from 0 to 2047, as said below
- inverses: bfloat16 [2048, 128, 128], P(('rows', 'cols')), may hold values from -0.5 to 0.5
- slot_cluster: int32 [2048], replicated, may hold values from 0 to 2047, as said below
Outputs:
- near: bfloat16 [262144, 128], P(('rows', 'cols'))
- preconditioned: bfloat16 [262144, 128], P(('rows', 'cols'))
Inputs may be any that keep to these rules, and one draw needn't show every extreme that they name: `block_list`: the blocks held on rows index r have row clusters among r*256 to (r+1)*256 - 1; each such cluster is the row of exactly 8 of that group's blocks, one of them its diagonal block; every column cluster lies within 128 clusters of its row cluster. For each device of its group, each device holds exactly 128 blocks whose row cluster that device owns, where device d owns clusters d*64 to (d+1)*64 - 1. `slot_cluster`: A permutation of the clusters. Device d owns clusters d*64 to (d+1)*64 - 1 and the slots with the same numbers; no device's slots hold more than 2 of one device's clusters, and this bound is reached.
All inputs are finite; a program needn't handle non-finite values.
Results may differ from a plain program's by a relative error of at most 0.005.
Values may be sent and summed in bfloat16 or wider, within the bound.
No kernel may reach another device: no remote copies, remote signals or barrier semaphores. Data moves between devices by JAX's collectives and lax.ppermute only.
A program may use at most 192 MiB of HBM per device.

v0:
```python
import math

import jax
import jax.numpy as jnp
from jax import lax
from jax.sharding import PartitionSpec as P


def extended(value, sides, width):
    for axis, dim in sides:
        devices, length = (lax.axis_size(axis), value.shape[dim])
        up = [(i, (i + 1) % devices) for i in range(devices - 1)]
        down = [(j, i) for i, j in up]
        last = lax.slice_in_dim(value, length - width, length, axis=dim)
        first = lax.slice_in_dim(value, 0, width, axis=dim)
        before = lax.ppermute(last, axis, up)
        after = lax.ppermute(first, axis, down)
        value = jnp.concatenate([before, value, after], axis=dim)
    return value


def ranks_within(labels, order_key):
    same_label = labels[:, None] == labels[None, :]
    earlier = order_key[:, None] > order_key[None, :]
    return jnp.sum((same_label & earlier).astype(jnp.int32), axis=1)


def accumulate(tiles, local_rows, local_cols, band_blocks, count):
    tile_count = tiles.shape[0]
    cluster_size = tiles.shape[1]
    columns = band_blocks.shape[2]
    step = math.gcd(tile_count, 64)

    def add_block(turn, totals):
        block_tiles = lax.dynamic_slice_in_dim(tiles, turn * step, step, 0)
        rows_here = lax.dynamic_slice_in_dim(local_rows, turn * step, step, 0)
        cols_here = lax.dynamic_slice_in_dim(local_cols, turn * step, step, 0)
        picked = band_blocks[cols_here]
        product = jnp.einsum(
            "tij,tjr->tir", block_tiles, picked, preferred_element_type=jnp.float32
        )
        return totals.at[rows_here].add(product)

    return lax.fori_loop(
        0, tile_count // step, add_block, jnp.zeros((count, cluster_size, columns), jnp.float32)
    )


def per_device(sources, tiles, block_list, inverses, slot_cluster):
    cluster_size = tiles.shape[1]
    columns = sources.shape[1]
    own_count = sources.shape[0] // cluster_size
    myself = lax.axis_index(("rows", "cols"))
    group = lax.all_gather(sources, "cols", axis=0, tiled=True)
    group_count = group.shape[0] // cluster_size
    reach = group_count // 2
    band = extended(group, (("rows", 0),), reach * cluster_size)
    band_blocks = band.reshape(-1, cluster_size, columns)
    base = lax.axis_index("rows") * group_count
    local_rows = block_list[:, 0] - base
    local_cols = block_list[:, 1] - base + reach
    totals = accumulate(tiles, local_rows, local_cols, band_blocks, group_count)
    summed = lax.psum_scatter(
        totals.reshape(group_count * cluster_size, columns), "cols", scatter_dimension=0, tiled=True
    )
    near = summed.astype(jnp.bfloat16)
    near_blocks = near.reshape(own_count, cluster_size, columns)
    devices = lax.axis_size(("rows", "cols"))
    capacity = -(-own_count // devices)
    total = slot_cluster.shape[0]
    where_slot = (
        jnp.zeros((total,), jnp.int32).at[slot_cluster].set(jnp.arange(total, dtype=jnp.int32))
    )
    local_index = jnp.arange(own_count, dtype=jnp.int32)
    my_clusters = myself * own_count + local_index
    target = where_slot[my_clusters] // own_count
    send_pos = target * capacity + ranks_within(target, local_index)
    held_clusters = lax.dynamic_slice_in_dim(slot_cluster, myself * own_count, own_count, 0)
    anchor = held_clusters // own_count
    anchor_local = held_clusters % own_count
    recv_pos = anchor * capacity + ranks_within(anchor, anchor_local)
    outbox = (
        jnp.zeros((devices * capacity, cluster_size, cluster_size), jnp.bfloat16)
        .at[recv_pos]
        .set(inverses)
    )
    inbox = lax.all_to_all(outbox, ("rows", "cols"), split_axis=0, concat_axis=0, tiled=True)
    mine = inbox[send_pos]
    result = jnp.einsum(
        "sij,sjr->sir", mine, near_blocks, preferred_element_type=jnp.float32
    ).astype(jnp.bfloat16)
    return (near, result.reshape(own_count * cluster_size, columns))


def solution(mesh):
    in_specs = (
        P(("rows", "cols"), None),
        P(("rows", "cols"), None, None),
        P(("rows", "cols"), None),
        P(("rows", "cols"), None, None),
        P(),
    )
    out_specs = (P(("rows", "cols"), None), P(("rows", "cols"), None))
    return jax.shard_map(
        per_device, mesh=mesh, in_specs=in_specs, out_specs=out_specs, check_vma=False
    )
```

profile of v0, /device:TPU:7, one launch (start us, length us, event | category | flops | bytes accessed | tf_op | source)
XLA Modules:
  0.0 632.2 jit_solution(4373505884216037214)
XLA Ops:
  7.2 0.0 all-gather.2.cloned.1.call-start
  7.2 0.7 all-gather.2.cloned.1.call-update
  7.9 0.0 copy-start.3
  7.9 0.0 reduce-scatter.2.cloned.1.call-start
  8.0 60.6 %all-gather.2.cloned.1.call-done = bf16[32768,128]{1,0:T(8,128)(2,1)} async-done(((bf16[8192,128]{1,0:T(8,128)(2,1)}), bf16[32768,128]{1,0:T(8,128)(2,1)}) %all-gather.2.cloned.1.call-update) | async-done | bytes 8388624 | tf_op jit(solution)/shard_map/all_gather | solution.py:54
  68.6 5.7 fusion.8
  74.3 1.9 collective-permute-start.1
  76.2 4.2 collective-permute-start
  80.5 0.0 copy-done.3
  80.5 88.8 %collective-permute-done.1 = bf16[16384,128]{1,0:T(8,128)(2,1)} collective-permute-done((bf16[16384,128]{1,0:T(8,128)(2,1)}, bf16[16384,128]{1,0:T(8,128)(2,1)}, u32[]{:S(2)}, u32[]{:S(2)}) %collective-permute-start.1) | collective-permute-done | bytes 4194336 | tf_op jit(solution)/shard_map/ppermute | solution.py:17
  169.4 90.4 %collective-permute-done = bf16[16384,128]{1,0:T(8,128)(2,1)} collective-permute-done((bf16[16384,128]{1,0:T(8,128)(2,1)}, bf16[16384,128]{1,0:T(8,128)(2,1)}, u32[]{:S(2)}, u32[]{:S(2)}) %collective-permute-start) | collective-permute-done | bytes 4194336 | tf_op jit(solution)/shard_map/ppermute | solution.py:16
  259.8 20.3 %pad_maximum_fusion = bf16[65536,128]{1,0:T(8,128)(2,1)} fusion(bf16[16384,128]{1,0:T(8,128)(2,1)} %collective-permute-done.1, bf16[32768,128]{1,0:T(8,128)(2,1)} %all-gather.2.cloned.1.call-done, bf16[16384,128]{1,0:T(8,128)(2,1)} %collective-permute-done), kind=kLoop, calls=%fused_computation.12 | loop fusion | flops 50331648 | bytes 33554432 | tf_op jit(solution)/shard_map/concatenate | solution.py:18
  280.1 7.8 %broadcast_in_dim.36 = f32[256,128,128]{2,1,0:T(8,128)} broadcast(f32[]{:T(128)} %constant.85.clone.1), dimensions={} | broadcast | bytes 16777220 | tf_op jit(solution)/shard_map/broadcast_in_dim | solution.py:45
  287.9 198.9 %while.13 = (s32[]{:T(128)}, f32[256,128,128]{2,1,0:T(8,128)}, s32[512]{0:T(512)S(1)}, bf16[512,128,128]{2,1,0:T(8,128)(2,1)}, s32[512]{0:T(512)S(1)}, /*index=5...) while((s32[]{:T(128)}, f32[256,128,128]{2,1,0:T(8,128)}, s32[512]{0:T(512)S(1)}, ...), condition=%wide.region_2.0_spmd, body=%wide.region_0.0_spmd.sunk | while | flops 269485440 | bytes 25171876 | solution.py:44
  287.9 0.1 compare_select_fusion.17
  288.0 6.7 %gather_fusion = bf16[64,128,128]{2,1,0:T(8,128)(2,1)S(1)} fusion(bf16[512,128,128]{2,1,0:T(8,128)(2,1)} %get-tuple-element.198, s32[1024]{0:T(1024)S(1)} %pad_clamp_fusion.4), kind=kCustom, calls=%fused_computation.clone.1 | custom fusion | bytes 4194560 | tf_op jit(solution)/shard_map/while/body/eval_jaxpr/gather | solution.py:38
  294.8 4.3 fusion.17
  299.1 13.8 %scatter_fusion = f32[256,128,128]{2,1,0:T(8,128)} fusion(f32[256,128,128]{2,1,0:T(8,128)} %get-tuple-element.184, s32[64]{0:T(128)S(1)} %get-tuple-element.171, f32[64,128,128]{2,1,0:T(8,128)} %fusion.17), kind=kCustom, calls=%fused_computation.3.clone.1 | custom fusion | flops 1048576 | bytes 12583168 | tf_op jit(solution)/shard_map/while/body/eval_jaxpr/scatter-add | solution.py:42
  312.9 0.1 compare_select_fusion.17
  313.0 6.7 %gather_fusion = bf16[64,128,128]{2,1,0:T(8,128)(2,1)S(1)} fusion(bf16[512,128,128]{2,1,0:T(8,128)(2,1)} %get-tuple-element.198, s32[1024]{0:T(1024)S(1)} %pad_clamp_fusion.4), kind=kCustom, calls=%fused_computation.clone.1 | custom fusion | bytes 4194560 | tf_op jit(solution)/shard_map/while/body/eval_jaxpr/gather | solution.py:38
  319.7 4.3 fusion.17
  324.0 13.7 %scatter_fusion = f32[256,128,128]{2,1,0:T(8,128)} fusion(f32[256,128,128]{2,1,0:T(8,128)} %get-tuple-element.184, s32[64]{0:T(128)S(1)} %get-tuple-element.171, f32[64,128,128]{2,1,0:T(8,128)} %fusion.17), kind=kCustom, calls=%fused_computation.3.clone.1 | custom fusion | flops 1048576 | bytes 12583168 | tf_op jit(solution)/shard_map/while/body/eval_jaxpr/scatter-add | solution.py:42
  337.7 0.1 compare_select_fusion.17
  337.8 6.7 %gather_fusion = bf16[64,128,128]{2,1,0:T(8,128)(2,1)S(1)} fusion(bf16[512,128,128]{2,1,0:T(8,128)(2,1)} %get-tuple-element.198, s32[1024]{0:T(1024)S(1)} %pad_clamp_fusion.4), kind=kCustom, calls=%fused_computation.clone.1 | custom fusion | bytes 4194560 | tf_op jit(solution)/shard_map/while/body/eval_jaxpr/gather | solution.py:38
  344.5 4.3 fusion.17
  348.8 13.7 %scatter_fusion = f32[256,128,128]{2,1,0:T(8,128)} fusion(f32[256,128,128]{2,1,0:T(8,128)} %get-tuple-element.184, s32[64]{0:T(128)S(1)} %get-tuple-element.171, f32[64,128,128]{2,1,0:T(8,128)} %fusion.17), kind=kCustom, calls=%fused_computation.3.clone.1 | custom fusion | flops 1048576 | bytes 12583168 | tf_op jit(solution)/shard_map/while/body/eval_jaxpr/scatter-add | solution.py:42
  362.6 0.1 compare_select_fusion.17
  362.7 6.7 %gather_fusion = bf16[64,128,128]{2,1,0:T(8,128)(2,1)S(1)} fusion(bf16[512,128,128]{2,1,0:T(8,128)(2,1)} %get-tuple-element.198, s32[1024]{0:T(1024)S(1)} %pad_clamp_fusion.4), kind=kCustom, calls=%fused_computation.clone.1 | custom fusion | bytes 4194560 | tf_op jit(solution)/shard_map/while/body/eval_jaxpr/gather | solution.py:38
  369.4 4.3 fusion.17
  373.7 13.7 %scatter_fusion = f32[256,128,128]{2,1,0:T(8,128)} fusion(f32[256,128,128]{2,1,0:T(8,128)} %get-tuple-element.184, s32[64]{0:T(128)S(1)} %get-tuple-element.171, f32[64,128,128]{2,1,0:T(8,128)} %fusion.17), kind=kCustom, calls=%fused_computation.3.clone.1 | custom fusion | flops 1048576 | bytes 12583168 | tf_op jit(solution)/shard_map/while/body/eval_jaxpr/scatter-add | solution.py:42
  387.4 0.1 compare_select_fusion.17
  387.5 6.7 %gather_fusion = bf16[64,128,128]{2,1,0:T(8,128)(2,1)S(1)} fusion(bf16[512,128,128]{2,1,0:T(8,128)(2,1)} %get-tuple-element.198, s32[1024]{0:T(1024)S(1)} %pad_clamp_fusion.4), kind=kCustom, calls=%fused_computation.clone.1 | custom fusion | bytes 4194560 | tf_op jit(solution)/shard_map/while/body/eval_jaxpr/gather | solution.py:38
  394.2 4.3 fusion.17
  398.6 13.6 %scatter_fusion = f32[256,128,128]{2,1,0:T(8,128)} fusion(f32[256,128,128]{2,1,0:T(8,128)} %get-tuple-element.184, s32[64]{0:T(128)S(1)} %get-tuple-element.171, f32[64,128,128]{2,1,0:T(8,128)} %fusion.17), kind=kCustom, calls=%fused_computation.3.clone.1 | custom fusion | flops 1048576 | bytes 12583168 | tf_op jit(solution)/shard_map/while/body/eval_jaxpr/scatter-add | solution.py:42
  412.2 0.1 compare_select_fusion.17
  412.3 6.7 %gather_fusion = bf16[64,128,128]{2,1,0:T(8,128)(2,1)S(1)} fusion(bf16[512,128,128]{2,1,0:T(8,128)(2,1)} %get-tuple-element.198, s32[1024]{0:T(1024)S(1)} %pad_clamp_fusion.4), kind=kCustom, calls=%fused_computation.clone.1 | custom fusion | bytes 4194560 | tf_op jit(solution)/shard_map/while/body/eval_jaxpr/gather | solution.py:38
  419.0 4.3 fusion.17
  423.3 13.7 %scatter_fusion = f32[256,128,128]{2,1,0:T(8,128)} fusion(f32[256,128,128]{2,1,0:T(8,128)} %get-tuple-element.184, s32[64]{0:T(128)S(1)} %get-tuple-element.171, f32[64,128,128]{2,1,0:T(8,128)} %fusion.17), kind=kCustom, calls=%fused_computation.3.clone.1 | custom fusion | flops 1048576 | bytes 12583168 | tf_op jit(solution)/shard_map/while/body/eval_jaxpr/scatter-add | solution.py:42
  437.1 0.1 compare_select_fusion.17
  437.1 6.7 %gather_fusion = bf16[64,128,128]{2,1,0:T(8,128)(2,1)S(1)} fusion(bf16[512,128,128]{2,1,0:T(8,128)(2,1)} %get-tuple-element.198, s32[1024]{0:T(1024)S(1)} %pad_clamp_fusion.4), kind=kCustom, calls=%fused_computation.clone.1 | custom fusion | bytes 4194560 | tf_op jit(solution)/shard_map/while/body/eval_jaxpr/gather | solution.py:38
  443.9 4.3 fusion.17
  448.2 13.7 %scatter_fusion = f32[256,128,128]{2,1,0:T(8,128)} fusion(f32[256,128,128]{2,1,0:T(8,128)} %get-tuple-element.184, s32[64]{0:T(128)S(1)} %get-tuple-element.171, f32[64,128,128]{2,1,0:T(8,128)} %fusion.17), kind=kCustom, calls=%fused_computation.3.clone.1 | custom fusion | flops 1048576 | bytes 12583168 | tf_op jit(solution)/shard_map/while/body/eval_jaxpr/scatter-add | solution.py:42
  461.9 0.1 compare_select_fusion.17
  462.0 6.7 %gather_fusion = bf16[64,128,128]{2,1,0:T(8,128)(2,1)S(1)} fusion(bf16[512,128,128]{2,1,0:T(8,128)(2,1)} %get-tuple-element.198, s32[1024]{0:T(1024)S(1)} %pad_clamp_fusion.4), kind=kCustom, calls=%fused_computation.clone.1 | custom fusion | bytes 4194560 | tf_op jit(solution)/shard_map/while/body/eval_jaxpr/gather | solution.py:38
  468.7 4.3 fusion.17
  473.0 13.8 %scatter_fusion = f32[256,128,128]{2,1,0:T(8,128)} fusion(f32[256,128,128]{2,1,0:T(8,128)} %get-tuple-element.184, s32[64]{0:T(128)S(1)} %get-tuple-element.171, f32[64,128,128]{2,1,0:T(8,128)} %fusion.17), kind=kCustom, calls=%fused_computation.3.clone.1 | custom fusion | flops 1048576 | bytes 12583168 | tf_op jit(solution)/shard_map/while/body/eval_jaxpr/scatter-add | solution.py:42
  486.8 0.0 reduce-scatter.2.cloned.1.call-update
  486.9 0.7 copy-done.2
  487.5 0.1 and_select_fusion.3
  487.6 0.2 convert_reduce_fusion.1
  487.8 1.8 broadcast_in_dim.37
  489.6 0.0 copy-done.1
  489.7 9.3 %scatter_fusion.1 = bf16[64,128,128]{2,1,0:T(8,128)(2,1)} fusion(bf16[64,128,128]{2,1,0:T(8,128)(2,1)} %broadcast_in_dim.37, s32[64]{0:T(128)S(1)} %compare_select_fusion.5, bf16[64,128,128]{2,1,0:T(8,128)(2,1)S(1)} %copy-done.1), kind=kCustom, calls=%fused_computation.4 | custom fusion | bytes 6291712 | tf_op jit(solution)/shard_map/scatter | solution.py:85
  498.9 4.7 all-to-all-start
  503.6 8.0 %scatter_custom_fusion.2 = s32[2048]{0:T(1024)S(1)} fusion(s32[2048]{0:T(1024)S(1)} %compare_select_fusion.2, s32[2048]{0:T(1024)S(1)} %iota.13, s32[]{:T(128)} %constant.84.clone.1), kind=kCustom, calls=%fused_computation.21 | custom fusion | bytes 8196 | tf_op jit(solution)/shard_map/scatter | solution.py:72
  511.7 0.8 gather_fusion.1
  512.5 0.2 convert_reduce_fusion
  512.7 39.0 %all-to-all-done = bf16[64,128,128]{2,1,0:T(8,128)(2,1)} async-done(((bf16[64,128,128]{2,1,0:T(8,128)(2,1)}), bf16[64,128,128]{2,1,0:T(8,128)(2,1)}, u32[]{:S(2)}, u32[]{:S(2)}) %all-to-all-start) | async-done | bytes 2097184 | tf_op jit(solution)/shard_map/all_to_all | solution.py:87
  551.7 2.5 gather_fusion.2
  554.2 66.7 %reduce-scatter.2.cloned.1.call-done = f32[8192,128]{1,0:T(8,128)} async-done(((f32[32768,128]{1,0:T(8,128)}), f32[8192,128]{1,0:T(8,128)}) %reduce-scatter.2.cloned.1.call-update) | async-done | bytes 4194320 | tf_op jit(solution)/shard_map/reduce_scatter | solution.py:63
  620.9 2.4 convert_element_type.12
  623.3 0.0 copy-start
  623.3 2.0 convolution_convert_fusion
  625.3 0.0 copy-done
  (20 shorter events, 0.1 us)
Async XLA Ops:
  7.2 61.4 %all-gather.2.cloned.1.call-start = ((), (), s32[]{:S(2)}) async-start(), calls=%async_computation.2 | async-start | bytes 10485760 | tf_op jit(solution)/shard_map/all_gather | solution.py:54
  7.9 72.6 %copy-start.3 = (s32[512,2]{0,1:T(2,128)S(1)}, s32[512,2]{0,1:T(2,128)}, u32[]{:S(2)}) copy-start(s32[512,2]{0,1:T(2,128)} %param.9) | copy-start | bytes 12292
  7.9 613.0 %reduce-scatter.2.cloned.1.call-start = ((), (), s32[]{:S(2)}) async-start(), calls=%async_computation.3 | async-start | bytes 20971520 | tf_op jit(solution)/shard_map/reduce_scatter | solution.py:63
  74.3 95.1 %collective-permute-start.1 = (bf16[16384,128]{1,0:T(8,128)(2,1)}, bf16[16384,128]{1,0:T(8,128)(2,1)}, u32[]{:S(2)}, u32[]{:S(2)}) collective-permute-start(bf16[16384,128]{1,0:T(8,128)(2,1)} %get-tuple-element.129), channel_id=1, source_target_pairs={{4,0},{8,4},{12,8},{16,12},{20,16},{24,20},{28,24},{5,1},{9,5},{13... | collective-permute-start | bytes 12582920 | tf_op jit(solution)/shard_map/ppermute | solution.py:17
  76.2 183.5 %collective-permute-start = (bf16[16384,128]{1,0:T(8,128)(2,1)}, bf16[16384,128]{1,0:T(8,128)(2,1)}, u32[]{:S(2)}, u32[]{:S(2)}) collective-permute-start(bf16[16384,128]{1,0:T(8,128)(2,1)} %get-tuple-element.128), channel_id=1, source_target_pairs={{0,4},{4,8},{8,12},{12,16},{16,20},{20,24},{24,28},{1,5},{5,9},{9,... | collective-permute-start | bytes 12582920 | tf_op jit(solution)/shard_map/ppermute | solution.py:16
  486.8 0.7 copy-start.2
  486.8 2.8 copy-start.1
  498.9 52.8 %all-to-all-start = ((bf16[64,128,128]{2,1,0:T(8,128)(2,1)}), bf16[64,128,128]{2,1,0:T(8,128)(2,1)}, u32[]{:S(2)}, u32[]{:S(2)}) async-start(bf16[64,128,128]{2,1,0:T(8,128)(2,1)} %scatter_fusion.1), calls=%async_computation.1 | async-start | bytes 4194304 | tf_op jit(solution)/shard_map/all_to_all | solution.py:87
  623.3 2.0 copy-start
Sparse Core Ops, SparseCore 0:
  9.6 58.9 all-gather.1
  487.0 133.8 reduce-scatter.1
where the time goes:
time: 638 us; the launch traced here: 632 us
  waiting for transfers between devices  346 us (54%)
  other arithmetic  134 us (21%)
  local copies, waits for them, and re-layouts  90.5 us (14%)
  matrix products  36.8 us (6%)
  between operations  14.2 us (2%)
  starting transfers between devices  10.9 us (2%)
    scatter-add x8, other arithmetic, add_block(): return totals.at[rows_here].add(product)  110 us
    ppermute x1, waiting for transfers between devices, extended(): before = lax.ppermute(last, axis, up)  90.4 us
    ppermute x1, waiting for transfers between devices, extended(): after = lax.ppermute(first, axis, down)  88.8 us
    reduce_scatter x1, waiting for transfers between devices, per_device(): lax.psum_scatter(totals.reshape(group_count * cluster_size, columns), 'co...  66.7 us
    all_gather x1, waiting for transfers between devices, per_device(): group = lax.all_gather(sources, 'cols', axis=0, tiled=True)  60.6 us
    gather x8, local copies, waits for them, and re-layouts, add_block(): picked = band_blocks[cols_here]  53.8 us
    all_to_all x1, waiting for transfers between devices, per_device(): lax.all_to_all(outbox, ('rows', 'cols'), split_axis=0, concat_axis=0, til...  39 us
    dot_general x8, matrix products, add_block(): jnp.einsum('tij,tjr->tir', block_tiles, picked, preferred_element_type=jn...  34.7 us
  transfers between devices with their start and end apart: 5, of which 5 were waited for; matrix products, arithmetic and copies ran while one was open for 4% of the time, Pallas kernels for 0%

commit v1 on v0

v1 whole, which is shorter than its diff:
```python
import functools

import jax
import jax.numpy as jnp
from jax import lax
from jax.experimental import pallas as pl
from jax.experimental.pallas import tpu as pltpu
from jax.sharding import PartitionSpec as P

AXES = ("rows", "cols")
MIB = 1024 * 1024
ANY = pl.BlockSpec(memory_space=pl.ANY)
SMEM = pl.BlockSpec(memory_space=pltpu.SMEM)


def pack_kernel(meta_ref, bucket_ref, tiles, keep, send, meta_keep, meta_send, counts, sem):
    total = tiles.shape[0]
    half = total // 2
    quarter = total // 4
    for first in (0, 3):
        counts[first] = 0
        counts[first + 1] = quarter
        counts[first + 2] = half - 1

    def deal(turn, carry):
        bucket = bucket_ref[turn]
        place = counts[bucket]
        late = jnp.logical_or(bucket == 2, bucket == 5)
        counts[bucket] = place + jnp.where(late, -1, 1)

        @pl.when(bucket < 3)
        def _():
            meta_keep[place] = meta_ref[turn]
            pltpu.make_async_copy(tiles.at[turn], keep.at[place], sem).start()

        @pl.when(bucket >= 3)
        def _():
            meta_send[place] = meta_ref[turn]
            pltpu.make_async_copy(tiles.at[turn], send.at[place], sem).start()

        return carry

    lax.fori_loop(0, total, deal, 0)
    pltpu.make_async_copy(tiles, tiles, sem).wait()


def pack(meta, bucket, tiles):
    half = tiles.shape[0] // 2
    block = jax.ShapeDtypeStruct((half,) + tiles.shape[1:], tiles.dtype)
    index = jax.ShapeDtypeStruct((half,), jnp.int32)
    return pl.pallas_call(
        pack_kernel,
        out_shape=(block, block, index, index),
        in_specs=[SMEM, SMEM, ANY],
        out_specs=(ANY, ANY, SMEM, SMEM),
        scratch_shapes=[pltpu.SMEM((8,), jnp.int32), pltpu.SemaphoreType.DMA],
        cost_estimate=pl.CostEstimate(flops=0, bytes_accessed=4 * tiles.size, transcendentals=0),
        name="pack",
    )(meta, bucket, tiles)


def load_band(pieces, band, sem):
    count = pieces[0].shape[0]
    return [
        pltpu.make_async_copy(piece, band.at[pl.ds(place * count, count)], sem.at[0])
        for place, piece in enumerate(pieces)
    ]


def add_tiles(meta_ref, first, count, tiles, band, acc, bits):
    mask = (1 << bits) - 1

    def add(turn, carry):
        meta = meta_ref[first + turn]
        row = lax.shift_right_logical(meta, bits)
        acc[row] += jnp.dot(
            tiles[turn], band[meta & mask], preferred_element_type=jnp.float32
        )
        return carry

    lax.fori_loop(0, count, add, 0, unroll=8)


def partial_kernel(bits, first, meta_keep, meta_recv, keep, recv, *rest):
    pieces, (out, band, mine, theirs, acc, sem) = rest[:6], rest[6:]
    count = mine.shape[0]
    copies = load_band(pieces, band, sem)
    copies.append(pltpu.make_async_copy(keep.at[pl.ds(first, count)], mine, sem.at[1]))
    copies.append(pltpu.make_async_copy(recv.at[pl.ds(first, count)], theirs, sem.at[2]))
    for copy in copies:
        copy.start()
    acc[...] = jnp.zeros_like(acc)
    pltpu.make_async_copy(band, band, sem.at[0]).wait()
    copies[6].wait()
    add_tiles(meta_keep, first, count, mine, band, acc, bits)
    copies[7].wait()
    add_tiles(meta_recv, first, count, theirs, band, acc, bits)
    out[...] = acc[...].astype(out.dtype)


def partial_sums(bits, meta_keep, meta_recv, keep, recv, pieces):
    count = keep.shape[0] // 2
    block = pieces[0].shape
    return pl.pallas_call(
        functools.partial(partial_kernel, bits, 0),
        out_shape=jax.ShapeDtypeStruct(block, jnp.bfloat16),
        in_specs=[SMEM, SMEM] + [ANY] * 8,
        out_specs=pl.BlockSpec(memory_space=pltpu.VMEM),
        scratch_shapes=[
            pltpu.VMEM((6 * block[0],) + block[1:], jnp.bfloat16),
            pltpu.VMEM((count,) + block[1:], jnp.bfloat16),
            pltpu.VMEM((count,) + block[1:], jnp.bfloat16),
            pltpu.VMEM(block, jnp.float32),
            pltpu.SemaphoreType.DMA((3,)),
        ],
        compiler_params=pltpu.CompilerParams(vmem_limit_bytes=48 * MIB),
        cost_estimate=pl.CostEstimate(
            flops=4 * count * block[1] * block[1] * block[2],
            bytes_accessed=22 * MIB,
            transcendentals=0,
        ),
        name="partial",
    )(meta_keep, meta_recv, keep, recv, *pieces)


def final_kernel(bits, first, meta_keep, meta_recv, places, keep, recv, inbox, other, *rest):
    pieces, (near, out, band, mine, theirs, inverse, acc, sem) = rest[:6], rest[6:]
    count = mine.shape[0]
    copies = load_band(pieces, band, sem)
    copies.append(pltpu.make_async_copy(keep.at[pl.ds(first, count)], mine, sem.at[1]))
    copies.append(pltpu.make_async_copy(recv.at[pl.ds(first, count)], theirs, sem.at[2]))
    copies.append(pltpu.make_async_copy(inbox, inverse, sem.at[3]))
    for copy in copies:
        copy.start()
    acc[...] = other[...].astype(jnp.float32)
    pltpu.make_async_copy(band, band, sem.at[0]).wait()
    copies[6].wait()
    add_tiles(meta_keep, first, count, mine, band, acc, bits)
    copies[7].wait()
    add_tiles(meta_recv, first, count, theirs, band, acc, bits)
    copies[8].wait()

    def apply(turn, carry):
        block = acc[turn].astype(jnp.bfloat16)
        near[turn] = block
        out[turn] = jnp.dot(
            inverse[places[turn]], block, preferred_element_type=jnp.float32
        ).astype(jnp.bfloat16)
        return carry

    lax.fori_loop(0, acc.shape[0], apply, 0, unroll=4)


def final(bits, meta_keep, meta_recv, places, keep, recv, inbox, other, pieces):
    count = keep.shape[0] // 2
    block = pieces[0].shape
    vmem = pl.BlockSpec(memory_space=pltpu.VMEM)
    result = jax.ShapeDtypeStruct(block, jnp.bfloat16)
    return pl.pallas_call(
        functools.partial(final_kernel, bits, count),
        out_shape=(result, result),
        in_specs=[SMEM] * 3 + [ANY] * 3 + [vmem] + [ANY] * 6,
        out_specs=(vmem, vmem),
        scratch_shapes=[
            pltpu.VMEM((6 * block[0],) + block[1:], jnp.bfloat16),
            pltpu.VMEM((count,) + block[1:], jnp.bfloat16),
            pltpu.VMEM((count,) + block[1:], jnp.bfloat16),
            pltpu.VMEM(inbox.shape, jnp.bfloat16),
            pltpu.VMEM(block, jnp.float32),
            pltpu.SemaphoreType.DMA((4,)),
        ],
        compiler_params=pltpu.CompilerParams(vmem_limit_bytes=48 * MIB),
        cost_estimate=pl.CostEstimate(
            flops=5 * count * block[1] * block[1] * block[2],
            bytes_accessed=28 * MIB,
            transcendentals=0,
        ),
        name="final",
    )(meta_keep, meta_recv, places, keep, recv, inbox, other, *pieces)


def ranks_within(labels):
    index = jnp.arange(labels.shape[0])
    same = labels[:, None] == labels[None, :]
    return jnp.sum((same & (index[:, None] > index[None, :])).astype(jnp.int32), axis=1)


def ranks_by(labels, key):
    same = labels[:, None] == labels[None, :]
    return jnp.sum((same & (key[:, None] > key[None, :])).astype(jnp.int32), axis=1)


def pick(values, wanted):
    position = jnp.arange(values.shape[0], dtype=jnp.int32)
    hit = wanted[:, None] == values[None, :]
    return jnp.sum(jnp.where(hit, position[None, :], 0), axis=1)


def per_device(rows, cols, sources, tiles, block_list, inverses, slot_cluster):
    size = tiles.shape[1]
    columns = sources.shape[1]
    own = sources.shape[0] // size
    devices = rows * cols
    half = cols // 2
    row = lax.axis_index("rows")
    col = lax.axis_index("cols")
    chip, core = col // 2, col % 2
    myself = row * cols + col
    blocks = sources.reshape(own, size, columns)

    def number(r, x, c):
        return r * cols + x * 2 + c

    def permute(value, pairs):
        return lax.ppermute(value, AXES, pairs)

    lines = [(x, c) for x in range(half) for c in range(2)]
    across = [
        (number(r, x, c), number(r, 1 - x, c)) for r in range(rows) for x, c in lines
    ]
    beside = [
        (number(r, x, c), number(r, x, 1 - c)) for r in range(rows) for x, c in lines
    ]
    up = [(r, r + 1) for r in range(rows - 1)]
    down = [(b, a) for a, b in up]
    early = [
        (number(a, x, c), number(b, x, c))
        for x, c in lines
        for a, b in (down if x == 0 else up)
    ]
    late = [
        (number(a, x, c), number(b, x, c))
        for x, c in lines
        for a, b in (up if x == 0 else down)
    ]

    other_chip = permute(blocks, across)
    halo_early = permute(blocks, early)
    own_beside = permute(blocks, beside)

    group = own * cols
    base = row * group
    bits = (8 * own - 1).bit_length()
    row_in = block_list[:, 0] - base
    owner = row_in // own
    column = block_list[:, 1] - base + group // 2
    quarter = column // own
    side = jnp.where(chip == 0, quarter // 2, 3 - quarter // 2)
    kind = (side + 3) % 4
    stays = owner % 2 == core
    reader = jnp.where(stays, core, 1 - core)
    slot = (jnp.minimum(kind, 2) * 2 + (quarter % 2 != reader)) * own + column % own
    meta = (row_in % own) * (1 << bits) + slot
    bucket = jnp.where(owner // 2 != chip, 0, jnp.where(kind == 3, 2, 1)) + jnp.where(stays, 0, 3)
    keep, send, meta_keep, meta_send = pack(meta, bucket, tiles)
    recv = permute(send, beside)
    meta_recv = permute(meta_send, beside)

    capacity = -(-own // devices)
    local = jnp.arange(own, dtype=jnp.int32)
    source = pick(slot_cluster, myself * own + local) // own
    places = source * capacity + ranks_by(source, local)
    held = lax.dynamic_slice_in_dim(slot_cluster, myself * own, own, 0)
    place_held = held // own * capacity + ranks_by(held // own, held % own)
    outbox = inverses[pick(place_held, jnp.arange(devices * capacity, dtype=jnp.int32))]
    inbox = lax.all_to_all(outbox, AXES, split_axis=0, concat_axis=0, tiled=True)

    other_beside = permute(other_chip, beside)
    halo_late = permute(other_chip, late)
    early_beside = permute(halo_early, beside)
    sums = partial_sums(
        bits,
        meta_keep,
        meta_recv,
        keep,
        recv,
        (blocks, own_beside, other_chip, other_beside, halo_early, early_beside),
    )
    other_sums = permute(sums, across)
    late_beside = permute(halo_late, beside)
    near, result = final(
        bits,
        meta_keep,
        meta_recv,
        places,
        keep,
        recv,
        inbox,
        other_sums,
        (blocks, own_beside, other_chip, other_beside, halo_late, late_beside),
    )
    return near.reshape(own * size, columns), result.reshape(own * size, columns)


def solution(mesh):
    spec = P(AXES, None)
    spec3 = P(AXES, None, None)
    return jax.shard_map(
        functools.partial(per_device, mesh.shape["rows"], mesh.shape["cols"]),
        mesh=mesh,
        in_specs=(spec, spec3, spec, spec3, P()),
        out_specs=(spec, spec),
        check_vma=False,
    )
```

time: 638 us -> 725 us (1.14)
  Pallas kernels: 0 us -> 545 us
  waiting for transfers between devices: 346 us -> 145 us
  other arithmetic: 134 us -> 2.88 us
  local copies, waits for them, and re-layouts: 90.5 us -> 6.65 us
  matrix products: 36.8 us -> 0 us
  between operations: 14.2 us -> 0.81 us
    pallas_call x0 -> x3, Pallas kernels: none -> 545 us  [the longest x1 511 us: pack(): pl.pallas_call(pack_kernel, out_shape=(block, block, index, index), in_sp...]
    scatter-add x8 -> x0, other arithmetic: 110 us -> none  [add_block(): return totals.at[rows_here].add(product)]
    reduce_scatter x1 -> x0, waiting for transfers between devices: 66.7 us -> none  [per_device(): lax.psum_scatter(totals.reshape(group_count * cluster_size, columns), 'co...]
    all_gather x1 -> x0, waiting for transfers between devices: 60.6 us -> none  [per_device(): group = lax.all_gather(sources, 'cols', axis=0, tiled=True)]
    ppermute x2 -> x10, waiting for transfers between devices: 179 us -> 121 us  [permute(): return lax.ppermute(value, AXES, pairs)]
    gather x10 -> x1, local copies, waits for them, and re-layouts: 57.1 us -> 2.13 us  [per_device(): inverses[pick(place_held, jnp.arange(devices * capacity, dtype=jnp.int32))]]
    dot_general x9 -> x0, matrix products: 36.8 us -> none  [the longest x8 34.7 us: add_block(): jnp.einsum('tij,tjr->tir', block_tiles, picked, preferred_element_type=jn...]
    concatenate x1 -> x0, other arithmetic: 20.3 us -> none  [extended(): value = jnp.concatenate([before, value, after], axis=dim)]
  transfers between devices with their start and end apart: 5 -> 11, of which waited for: 5 -> 4; matrix products, arithmetic and copies ran while one was open for 4% -> 0% of each run, Pallas kernels for 0% -> 2%
where the time goes in v1:
time: 725 us; the launch traced here: 717 us
  Pallas kernels  545 us (75%)
  waiting for transfers between devices  145 us (20%)
  starting transfers between devices  16.7 us (2%)
    pallas_call x1, Pallas kernels, pack(): pl.pallas_call(pack_kernel, out_shape=(block, block, index, index), in_sp...  511 us
    ppermute x10, waiting for transfers between devices, permute(): return lax.ppermute(value, AXES, pairs)  121 us
    all_to_all x1, waiting for transfers between devices, per_device(): lax.all_to_all(outbox, AXES, split_axis=0, concat_axis=0, tiled=True)  24 us
    pallas_call x1, Pallas kernels, final(): pl.pallas_call(functools.partial(final_kernel, bits, count), out_shape=(r...  18.7 us
    pallas_call x1, Pallas kernels, partial_sums(): pl.pallas_call(functools.partial(partial_kernel, bits, 0), out_shape=jax....  15 us
  transfers between devices with their start and end apart: 11, of which 4 were waited for; matrix products, arithmetic and copies ran while one was open for 0% of the time, Pallas kernels for 2%

profile of v1, /device:TPU:7, one launch (start us, length us, event | category | flops | bytes accessed | tf_op | source)
XLA Modules:
  0.0 716.8 jit_solution(13386365303210432973)
XLA Ops:
  0.6 0.0 copy-start
  0.7 0.9 subtract_add_fusion
  1.5 0.6 select_add_fusion
  2.1 0.6 fusion.2.meta_ref
  2.7 0.0 copy-start.6
  2.7 510.8 %pack.1 = (bf16[256,128,128]{2,1,0:T(8,128)(2,1)}, bf16[256,128,128]{2,1,0:T(8,128)(2,1)}, s32[256]{0:T(256)}, s32[256]{0:T(256)}) custom-call(s32[512]{0:T(512)} %fusion.2.meta_ref, s32[512]{0:T(512)} %get-tuple-element.16.bucket_ref, bf16[512,128,128]{2,1,0:T(8,128)(2,1)} %tiles.1), custom_call_target="tpu_custom_call" | custom-call | bytes 33554432 | tf_op jit(solution)/shard_map/pack/pallas_call | solution.py:51
  513.5 0.7 collective-permute-start.1
  514.3 0.3 collective-permute-start.3
  514.5 3.1 collective-permute-start.5
  517.7 0.7 collective-permute-start.2
  518.4 0.1 collective-permute-start
  518.5 0.0 copy-done.6
  518.5 0.1 and_select_fusion.1
  518.6 0.2 convert_reduce_fusion
  518.7 0.1 select_reduce_fusion.1
  518.9 42.9 %collective-permute-done.3.rest_2_ = bf16[64,128,128]{2,1,0:T(8,128)(2,1)} collective-permute-done((bf16[64,128,128]{2,1,0:T(8,128)(2,1)}, bf16[64,128,128]{2,1,0:T(8,128)(2,1)}, u32[]{:S(2)}, u32[]{:S(2)}) %collective-permute-start.3) | collective-permute-done | bytes 2097184 | tf_op jit(solution)/shard_map/ppermute | solution.py:215
  561.8 0.8 collective-permute-start.4
  562.7 0.0 collective-permute-done.meta_recv
  562.7 2.1 collective-permute-start.8
  564.8 0.0 collective-permute-done.5.rest_4_
  564.8 0.3 collective-permute-start.6
  565.2 0.0 copy-done
  565.2 2.1 gather_fusion
  567.3 0.0 copy-start.5
  567.3 7.2 %all-to-all-start = ((bf16[64,128,128]{2,1,0:T(8,128)(2,1)}), bf16[64,128,128]{2,1,0:T(8,128)(2,1)}, u32[]{:S(2)}, u32[]{:S(2)}) async-start(bf16[64,128,128]{2,1,0:T(8,128)(2,1)} %gather_fusion), calls=%async_computation | async-start | bytes 4194304 | tf_op jit(solution)/shard_map/all_to_all | solution.py:266
  574.5 55.3 %collective-permute-done.8.rest_4_ = bf16[64,128,128]{2,1,0:T(8,128)(2,1)} collective-permute-done((bf16[64,128,128]{2,1,0:T(8,128)(2,1)}, bf16[64,128,128]{2,1,0:T(8,128)(2,1)}, u32[]{:S(2)}, u32[]{:S(2)}) %collective-permute-start.8) | collective-permute-done | bytes 2097184 | tf_op jit(solution)/shard_map/ppermute | solution.py:215
  629.8 1.2 collective-permute-start.9
  631.0 0.0 collective-permute-done.2.rest_1_
  631.0 0.0 collective-permute-done.4.rest_3_
  631.0 0.0 collective-permute-done.6.rest_5_
  631.0 0.0 collective-permute-done.1.recv
  631.0 0.0 copy-done.5
  631.0 0.0 copy-start.2
  631.0 1.6 copy-done.2
  632.6 15.0 %partial.1 = bf16[64,128,128]{2,1,0:T(8,128)(2,1)} custom-call(s32[256]{0:T(256)S(1)} %copy-done.5, s32[256]{0:T(256)S(1)} %collective-permute-done.meta_recv, bf16[256,128,128]{2,1,0:T(8,128)(2,1)} %get-tuple-element.10.keep, bf16[256,128,128]{2,1,0:T(8,128)(2,1)} %collective-permute-done.1.recv, bf16[64,128,128]{2,1,0:T(8,128)(2,1)S(1)} %bitcast.13, ...), custom_call_target="tpu_custom_call" | custom-call | flops 1073741824 | bytes 23068672 | tf_op jit(solution)/shard_map/partial/pallas_call | solution.py:104
  647.7 0.1 collective-permute-start.7
  647.7 0.2 select_reduce_fusion
  648.0 0.2 convert_reduce_fusion.1
  648.2 24.0 %all-to-all-done.inbox = bf16[64,128,128]{2,1,0:T(8,128)(2,1)} async-done(((bf16[64,128,128]{2,1,0:T(8,128)(2,1)}), bf16[64,128,128]{2,1,0:T(8,128)(2,1)}, u32[]{:S(2)}, u32[]{:S(2)}) %all-to-all-start) | async-done | bytes 2097184 | tf_op jit(solution)/shard_map/all_to_all | solution.py:266
  672.2 0.0 collective-permute-done.9.rest_5_
  672.2 23.0 %collective-permute-done.7.other = bf16[64,128,128]{2,1,0:T(8,128)(2,1)S(1)} collective-permute-done((bf16[64,128,128]{2,1,0:T(8,128)(2,1)}, bf16[64,128,128]{2,1,0:T(8,128)(2,1)S(1)}, u32[]{:S(2)}, u32[]{:S(2)}) %collective-permute-start.7) | collective-permute-done | bytes 2097184 | tf_op jit(solution)/shard_map/ppermute | solution.py:215
  695.2 0.0 copy-start.3
  695.2 1.3 copy-done.3
  696.5 0.0 copy-start.4
  696.5 1.6 copy-done.4
  698.1 0.0 copy-start.1
  698.1 18.7 %final.1 = (bf16[64,128,128]{2,1,0:T(8,128)(2,1)}, bf16[64,128,128]{2,1,0:T(8,128)(2,1)}) custom-call(s32[256]{0:T(256)S(1)} %copy-done.5, s32[256]{0:T(256)S(1)} %collective-permute-done.meta_recv, s32[64]{0:T(128)S(1)} %multiply_add_fusion.1.places, bf16[256,128,128]{2,1,0:T(8,128)(2,1)} %get-tuple-element.10.keep, ...), custom_call_target="tpu_custom_call" | custom-call | flops 1342177280 | bytes 29360128 | tf_op jit(solution)/shard_map/final/pallas_call | solution.py:159
  716.8 0.0 copy-done.1
  (7 shorter events, 0.1 us)
Async XLA Ops:
  0.6 564.5 %copy-start = (bf16[64,128,128]{2,1,0:T(8,128)(2,1)S(1)}, bf16[64,128,128]{2,1,0:T(8,128)(2,1)}, u32[]{:S(2)}) copy-start(bf16[64,128,128]{2,1,0:T(8,128)(2,1)} %param.8) | copy-start | bytes 6291460
  2.7 515.7 %copy-start.6 = (s32[2048]{0:T(1024)S(1)}, s32[2048]{0:T(1024)}, u32[]{:S(2)}) copy-start(s32[2048]{0:T(1024)} %param.9) | copy-start | bytes 24580
  513.5 117.5 %collective-permute-start.1 = (bf16[256,128,128]{2,1,0:T(8,128)(2,1)}, bf16[256,128,128]{2,1,0:T(8,128)(2,1)}, u32[]{:S(2)}, u32[]{:S(2)}) collective-permute-start(bf16[256,128,128]{2,1,0:T(8,128)(2,1)} %get-tuple-element.11), channel_id=1, source_target_pairs={{0,1},{1,0},{2,3},{3,2},{4,5},{5,4},{6,7},{7,6},{8,9},{9,8},{10,11... | collective-permute-start | bytes 25165832 | tf_op jit(solution)/shard_map/ppermute | solution.py:215
  514.3 47.5 %collective-permute-start.3 = (bf16[64,128,128]{2,1,0:T(8,128)(2,1)}, bf16[64,128,128]{2,1,0:T(8,128)(2,1)}, u32[]{:S(2)}, u32[]{:S(2)}) collective-permute-start(bf16[64,128,128]{2,1,0:T(8,128)(2,1)} %bitcast.9), channel_id=1, source_target_pairs={{0,2},{1,3},{2,0},{3,1},{4,6},{5,7},{6,4},{7,5},{8,10},{9,11},{10,... | collective-permute-start | bytes 6291464 | tf_op jit(solution)/shard_map/ppermute | solution.py:215
  514.5 50.2 %collective-permute-start.5 = (bf16[64,128,128]{2,1,0:T(8,128)(2,1)}, bf16[64,128,128]{2,1,0:T(8,128)(2,1)}, u32[]{:S(2)}, u32[]{:S(2)}) collective-permute-start(bf16[64,128,128]{2,1,0:T(8,128)(2,1)} %bitcast.10), channel_id=1, source_target_pairs={{4,0},{8,4},{12,8},{16,12},{20,16},{24,20},{28,24},{5,1},{9,5},{13... | collective-permute-start | bytes 6291464 | tf_op jit(solution)/shard_map/ppermute | solution.py:215
  517.7 113.3 %collective-permute-start.2 = (bf16[64,128,128]{2,1,0:T(8,128)(2,1)}, bf16[64,128,128]{2,1,0:T(8,128)(2,1)}, u32[]{:S(2)}, u32[]{:S(2)}) collective-permute-start(bf16[64,128,128]{2,1,0:T(8,128)(2,1)} %bitcast.11), channel_id=1, source_target_pairs={{0,1},{1,0},{2,3},{3,2},{4,5},{5,4},{6,7},{7,6},{8,9},{9,8},{10,11... | collective-permute-start | bytes 6291464 | tf_op jit(solution)/shard_map/ppermute | solution.py:215
  518.4 44.3 %collective-permute-start = (s32[256]{0:T(256)}, s32[256]{0:T(256)S(1)}, u32[]{:S(2)}, u32[]{:S(2)}) collective-permute-start(s32[256]{0:T(256)} %get-tuple-element.9), channel_id=1, source_target_pairs={{0,1},{1,0},{2,3},{3,2},{4,5},{5,4},{6,7},{7,6},{8,9},{9,8},{10,11... | collective-permute-start | bytes 3080 | tf_op jit(solution)/shard_map/ppermute | solution.py:215
  561.8 69.2 %collective-permute-start.4 = (bf16[64,128,128]{2,1,0:T(8,128)(2,1)}, bf16[64,128,128]{2,1,0:T(8,128)(2,1)}, u32[]{:S(2)}, u32[]{:S(2)}) collective-permute-start(bf16[64,128,128]{2,1,0:T(8,128)(2,1)} %collective-permute-done.3.rest_2_), channel_id=1, source_target_pairs={{0,1},{1,0},{2,3},{3,2},{4,5},{5,4},{6,7},{7,6},{8,9},{9,8},{10,11... | collective-permute-start | bytes 6291464 | tf_op jit(solution)/shard_map/ppermute | solution.py:215
  562.7 67.2 %collective-permute-start.8 = (bf16[64,128,128]{2,1,0:T(8,128)(2,1)}, bf16[64,128,128]{2,1,0:T(8,128)(2,1)}, u32[]{:S(2)}, u32[]{:S(2)}) collective-permute-start(bf16[64,128,128]{2,1,0:T(8,128)(2,1)} %collective-permute-done.3.rest_2_), channel_id=1, source_target_pairs={{0,4},{4,8},{8,12},{12,16},{16,20},{20,24},{24,28},{1,5},{5,9},{9,... | collective-permute-start | bytes 6291464 | tf_op jit(solution)/shard_map/ppermute | solution.py:215
  564.8 66.2 %collective-permute-start.6 = (bf16[64,128,128]{2,1,0:T(8,128)(2,1)}, bf16[64,128,128]{2,1,0:T(8,128)(2,1)}, u32[]{:S(2)}, u32[]{:S(2)}) collective-permute-start(bf16[64,128,128]{2,1,0:T(8,128)(2,1)} %collective-permute-done.5.rest_4_), channel_id=1, source_target_pairs={{0,1},{1,0},{2,3},{3,2},{4,5},{5,4},{6,7},{7,6},{8,9},{9,8},{10,11... | collective-permute-start | bytes 6291464 | tf_op jit(solution)/shard_map/ppermute | solution.py:215
  567.3 63.7 %copy-start.5 = (s32[256]{0:T(256)S(1)}, s32[256]{0:T(256)}, u32[]{:S(2)}) copy-start(s32[256]{0:T(256)} %get-tuple-element.8.meta_keep) | copy-start | bytes 3076
  567.3 104.9 %all-to-all-start = ((bf16[64,128,128]{2,1,0:T(8,128)(2,1)}), bf16[64,128,128]{2,1,0:T(8,128)(2,1)}, u32[]{:S(2)}, u32[]{:S(2)}) async-start(bf16[64,128,128]{2,1,0:T(8,128)(2,1)} %gather_fusion), calls=%async_computation | async-start | bytes 4194304 | tf_op jit(solution)/shard_map/all_to_all | solution.py:266
  629.8 42.4 %collective-permute-start.9 = (bf16[64,128,128]{2,1,0:T(8,128)(2,1)}, bf16[64,128,128]{2,1,0:T(8,128)(2,1)}, u32[]{:S(2)}, u32[]{:S(2)}) collective-permute-start(bf16[64,128,128]{2,1,0:T(8,128)(2,1)} %collective-permute-done.8.rest_4_), channel_id=1, source_target_pairs={{0,1},{1,0},{2,3},{3,2},{4,5},{5,4},{6,7},{7,6},{8,9},{9,8},{10,11... | collective-permute-start | bytes 6291464 | tf_op jit(solution)/shard_map/ppermute | solution.py:215
  631.0 1.6 copy-start.2
  647.7 47.5 %collective-permute-start.7 = (bf16[64,128,128]{2,1,0:T(8,128)(2,1)}, bf16[64,128,128]{2,1,0:T(8,128)(2,1)S(1)}, u32[]{:S(2)}, u32[]{:S(2)}) collective-permute-start(bf16[64,128,128]{2,1,0:T(8,128)(2,1)} %partial.1), channel_id=1, source_target_pairs={{0,2},{1,3},{2,0},{3,1},{4,6},{5,7},{6,4},{7,5},{8,10},{9,11},{10,... | collective-permute-start | bytes 6291464 | tf_op jit(solution)/shard_map/ppermute | solution.py:215
  695.2 1.3 copy-start.3
  696.5 1.6 copy-start.4
  698.1 18.7 %copy-start.1 = (bf16[64,128,128]{2,1,0:T(8,128)(2,1)S(1)}, bf16[64,128,128]{2,1,0:T(8,128)(2,1)}, u32[]{:S(2)}) copy-start(bf16[64,128,128]{2,1,0:T(8,128)(2,1)} %param.8) | copy-start | bytes 6291460

commit v2 on v1

v2 whole, which is shorter than its diff:
```python
import functools

import jax
import jax.numpy as jnp
from jax import lax
from jax.experimental import pallas as pl
from jax.experimental.pallas import tpu as pltpu
from jax.sharding import PartitionSpec as P

AXES = ("rows", "cols")
MIB = 1024 * 1024
HBM = pl.BlockSpec(memory_space=pltpu.HBM)
SMEM = pl.BlockSpec(memory_space=pltpu.SMEM)
VMEM = pl.BlockSpec(memory_space=pltpu.VMEM)
CHUNK = 16


def params(mib):
    return pltpu.CompilerParams(vmem_limit_bytes=mib * MIB)


def cost(flops, mib):
    return pl.CostEstimate(flops=flops, bytes_accessed=mib * MIB, transcendentals=0)


def gather_kernel(first, order_ref, tiles, *rest):
    outs, (held, sem) = rest[:-2], rest[-2:]
    count = outs[0].shape[0]
    for part in range(len(outs)):

        def fetch(turn, carry):
            place = part * count + turn
            pltpu.make_async_copy(
                tiles.at[order_ref[first + place]], held.at[place], sem.at[part]
            ).start()
            return carry

        lax.fori_loop(0, count, fetch, 0, unroll=4)
    copies = []
    for part, out in enumerate(outs):
        block = held.at[pl.ds(part * count, count)]
        pltpu.make_async_copy(block, block, sem.at[part]).wait()
        copies.append(pltpu.make_async_copy(block, out, sem.at[len(outs) + part]))
        copies[-1].start()
    for copy in copies:
        copy.wait()


def gather_tiles(order, tiles, first, parts, name):
    count = tiles.shape[0] // 4
    block = (count,) + tiles.shape[1:]
    return pl.pallas_call(
        functools.partial(gather_kernel, first),
        out_shape=(jax.ShapeDtypeStruct(block, tiles.dtype),) * parts,
        in_specs=[SMEM, HBM],
        out_specs=(HBM,) * parts,
        scratch_shapes=[
            pltpu.VMEM((parts * count,) + tiles.shape[1:], tiles.dtype),
            pltpu.SemaphoreType.DMA((2 * parts,)),
        ],
        compiler_params=params(60),
        cost_estimate=cost(0, 8 * parts),
        name=name,
    )(order, tiles)


def add_tiles(meta_ref, place, count, tiles, start, band, acc, bits):
    mask = (1 << bits) - 1
    for turn in range(count):
        meta = meta_ref[place + turn]
        row = lax.shift_right_logical(meta, bits)
        acc[row] += jnp.dot(
            tiles[start + turn], band[meta & mask], preferred_element_type=jnp.float32
        )


def sums_kernel(bits, whole, meta_keep, meta_recv, bounds, keep, recv, *rest):
    count = keep.shape[0]
    pieces, (out, band, mine, theirs, acc, sem) = rest[:-6], rest[-6:]
    size = pieces[0].shape[0]
    loads = [
        pltpu.make_async_copy(piece, band.at[pl.ds(place * size, size)], sem.at[0])
        for place, piece in enumerate(pieces)
    ]
    loads.append(pltpu.make_async_copy(keep, mine, sem.at[1]))
    loads.append(pltpu.make_async_copy(recv, theirs, sem.at[2]))
    for load in loads:
        load.start()
    acc[...] = jnp.zeros_like(acc)
    pltpu.make_async_copy(band, band, sem.at[0]).wait()
    for side, (meta, held) in enumerate(((meta_keep, mine), (meta_recv, theirs))):
        loads[len(pieces) + side].wait()
        if whole:

            def add(turn, carry):
                add_tiles(meta, turn * CHUNK, CHUNK, held, turn * CHUNK, band, acc, bits)
                return carry

            lax.fori_loop(0, count // CHUNK, add, 0)
        else:

            def add_one(turn, carry):
                add_tiles(meta, turn, 1, held, turn, band, acc, bits)
                return carry

            end = bounds[side]
            even = end // 8 * 8

            def add_eight(turn, carry):
                add_tiles(meta, turn * 8, 8, held, turn * 8, band, acc, bits)
                return carry

            lax.fori_loop(0, end // 8, add_eight, 0)
            lax.fori_loop(even, end, add_one, 0)
    out[...] = acc[...].astype(out.dtype)


def sums(bits, whole, dtype, meta_keep, meta_recv, bounds, keep, recv, pieces, name):
    block = pieces[0].shape
    held = pltpu.VMEM(keep.shape, keep.dtype)
    return pl.pallas_call(
        functools.partial(sums_kernel, bits, whole),
        out_shape=jax.ShapeDtypeStruct(block, dtype),
        in_specs=[SMEM] * 3 + [HBM] * (2 + len(pieces)),
        out_specs=VMEM,
        scratch_shapes=[
            pltpu.VMEM((len(pieces) * block[0],) + block[1:], jnp.bfloat16),
            held,
            held,
            pltpu.VMEM(block, jnp.float32),
            pltpu.SemaphoreType.DMA((3,)),
        ],
        compiler_params=params(60),
        cost_estimate=cost(4 * keep.size * block[2], 24),
        name=name,
    )(meta_keep, meta_recv, bounds, keep, recv, *pieces)


def final_kernel(
    bits, meta_keep, meta_recv, bounds, places, early, other, keep, recv, late, beside, inbox, *rest
):
    near, out, acc, sent, band, mine, theirs, inverse, sem = rest
    count = keep.shape[0]
    size = late.shape[0]
    loads = [
        pltpu.make_async_copy(early, acc, sem.at[0]),
        pltpu.make_async_copy(other, sent, sem.at[1]),
        pltpu.make_async_copy(late, band.at[pl.ds(0, size)], sem.at[2]),
        pltpu.make_async_copy(beside, band.at[pl.ds(size, size)], sem.at[3]),
        pltpu.make_async_copy(inbox, inverse, sem.at[4]),
    ]
    for load in loads:
        load.start()
    sides = ((meta_keep, keep, mine), (meta_recv, recv, theirs))

    def chunk_copy(side, chunk):
        piece = pl.ds(pl.multiple_of(chunk * CHUNK, CHUNK), CHUNK)
        return pltpu.make_async_copy(sides[side][1].at[piece], sides[side][2].at[piece], sem.at[5 + side])

    for side in (0, 1):

        def fetch(chunk, carry):
            chunk_copy(side, chunk).start()
            return carry

        lax.fori_loop(bounds[side] // CHUNK, count // CHUNK, fetch, 0)
    for load in loads[:4]:
        load.wait()
    for side in (0, 1):

        def settle(chunk, carry):
            chunk_copy(side, chunk).wait()
            return carry

        lax.fori_loop(bounds[side] // CHUNK, count // CHUNK, settle, 0)
    for side, (meta_ref, keep_ref, held) in enumerate(sides):

        def add(turn, carry):
            meta = meta_ref[turn]
            row = lax.shift_right_logical(meta, bits)
            slot = (meta & ((1 << bits) - 1)) - 4 * size
            acc[row] += jnp.dot(held[turn], band[slot], preferred_element_type=jnp.float32)
            return carry

        def add_eight(turn, carry):
            for step in range(8):
                add(turn * 8 + step, carry)
            return carry

        first = bounds[side]
        even = (first + 7) // 8
        lax.fori_loop(first, even * 8, add, 0)
        lax.fori_loop(even, count // 8, add_eight, 0)
    loads[4].wait()

    def apply(turn, carry):
        block = (acc[turn] + sent[turn].astype(jnp.float32)).astype(jnp.bfloat16)
        near[turn] = block
        out[turn] = jnp.dot(
            inverse[places[turn]], block, preferred_element_type=jnp.float32
        ).astype(jnp.bfloat16)
        return carry

    lax.fori_loop(0, size, apply, 0, unroll=8)


def final(bits, meta_keep, meta_recv, bounds, places, early, other, keep, recv, late, beside, inbox):
    block = late.shape
    held = pltpu.VMEM(keep.shape, keep.dtype)
    result = jax.ShapeDtypeStruct(block, jnp.bfloat16)
    return pl.pallas_call(
        functools.partial(final_kernel, bits),
        out_shape=(result, result),
        in_specs=[SMEM] * 4 + [HBM] * 7,
        out_specs=(VMEM, VMEM),
        scratch_shapes=[
            pltpu.VMEM(block, jnp.float32),
            pltpu.VMEM(block, jnp.bfloat16),
            pltpu.VMEM((2 * block[0],) + block[1:], jnp.bfloat16),
            held,
            held,
            pltpu.VMEM(inbox.shape, jnp.bfloat16),
            pltpu.SemaphoreType.DMA((7,)),
        ],
        compiler_params=params(60),
        cost_estimate=cost(3 * keep.size * block[2], 20),
        name="final",
    )(meta_keep, meta_recv, bounds, places, early, other, keep, recv, late, beside, inbox)


def ranks_by(labels, key):
    same = labels[:, None] == labels[None, :]
    return jnp.sum((same & (key[:, None] > key[None, :])).astype(jnp.int32), axis=1)


def pick(values, wanted):
    position = jnp.arange(values.shape[0], dtype=jnp.int32)
    hit = wanted[:, None] == values[None, :]
    return jnp.sum(jnp.where(hit, position[None, :], 0), axis=1)


def per_device(rows, cols, sources, tiles, block_list, inverses, slot_cluster):
    size = tiles.shape[1]
    columns = sources.shape[1]
    own = sources.shape[0] // size
    devices = rows * cols
    half = cols // 2
    row = lax.axis_index("rows")
    col = lax.axis_index("cols")
    chip, core = col // 2, col % 2
    myself = row * cols + col
    blocks = sources.reshape(own, size, columns)

    def number(r, x, c):
        return r * cols + x * 2 + c

    def permute(value, pairs):
        return lax.ppermute(value, AXES, pairs)

    lines = [(x, c) for x in range(half) for c in range(2)]
    across = [
        (number(r, x, c), number(r, 1 - x, c)) for r in range(rows) for x, c in lines
    ]
    beside = [
        (number(r, x, c), number(r, x, 1 - c)) for r in range(rows) for x, c in lines
    ]
    up = [(r, r + 1) for r in range(rows - 1)]
    down = [(b, a) for a, b in up]
    early = [
        (number(a, x, c), number(b, x, c))
        for x, c in lines
        for a, b in (down if x == 0 else up)
    ]
    late = [
        (number(a, x, c), number(b, x, c))
        for x, c in lines
        for a, b in (up if x == 0 else down)
    ]

    other_chip = permute(blocks, across)
    halo_early = permute(blocks, early)
    own_beside = permute(blocks, beside)

    group = own * cols
    base = row * group
    bits = (8 * own - 1).bit_length()
    row_in = block_list[:, 0] - base
    owner = row_in // own
    column = block_list[:, 1] - base + group // 2
    quarter = column // own
    side = jnp.where(chip == 0, quarter // 2, 3 - quarter // 2)
    kind = (side + 3) % 4
    stays = owner % 2 == core
    reader = jnp.where(stays, core, 1 - core)
    slot = (jnp.minimum(kind, 2) * 2 + (quarter % 2 != reader)) * own + column % own
    meta = (row_in % own) * (1 << bits) + slot
    bucket = jnp.where(owner // 2 != chip, 0, jnp.where(kind == 3, 2, 1)) + jnp.where(stays, 0, 3)
    total = tiles.shape[0]
    quarter_count = total // 4
    index = jnp.arange(total, dtype=jnp.int32)
    key = bucket * total + index
    rank = jnp.sum((key[:, None] > key[None, :]).astype(jnp.int32), axis=1)
    placed = rank[None, :] == index[:, None]
    order = jnp.sum(jnp.where(placed, index[None, :], 0), axis=1)
    meta = jnp.sum(jnp.where(placed, meta[None, :], 0), axis=1)
    bound_keep = jnp.sum((bucket == 1).astype(jnp.int32), keepdims=True)
    bound_send = jnp.sum((bucket == 4).astype(jnp.int32), keepdims=True)
    padding = jnp.zeros((127,), jnp.int32)
    send_cross, send_own = gather_tiles(order, tiles, 2 * quarter_count, 2, "pack_send")
    recv_cross = permute(send_cross, beside)
    recv_own = permute(send_own, beside)
    meta_recv = permute(
        jnp.concatenate([meta[2 * quarter_count :], bound_send, padding]), beside
    )
    keep_cross, keep_own = gather_tiles(order, tiles, 0, 2, "pack_keep")
    bounds = jnp.concatenate([bound_keep, meta_recv[2 * quarter_count : 2 * quarter_count + 1]])

    capacity = -(-own // devices)
    local = jnp.arange(own, dtype=jnp.int32)
    source = pick(slot_cluster, myself * own + local) // own
    places = source * capacity + ranks_by(source, local)
    held = lax.dynamic_slice_in_dim(slot_cluster, myself * own, own, 0)
    place_held = held // own * capacity + ranks_by(held // own, held % own)
    outbox = inverses[pick(place_held, jnp.arange(devices * capacity, dtype=jnp.int32))]
    inbox = lax.all_to_all(outbox, AXES, split_axis=0, concat_axis=0, tiled=True)

    other_beside = permute(other_chip, beside)
    halo_late = permute(other_chip, late)
    early_beside = permute(halo_early, beside)
    group_pieces = (blocks, own_beside, other_chip, other_beside)
    cross = sums(
        bits,
        True,
        jnp.bfloat16,
        meta[:quarter_count],
        meta_recv[:quarter_count],
        bounds,
        keep_cross,
        recv_cross,
        group_pieces + (halo_early, early_beside),
        "cross",
    )
    other_sums = permute(cross, across)
    own_keep = meta[quarter_count : 2 * quarter_count]
    own_recv = meta_recv[quarter_count : 2 * quarter_count]
    early_sums = sums(
        bits,
        False,
        jnp.float32,
        own_keep,
        own_recv,
        bounds,
        keep_own,
        recv_own,
        group_pieces,
        "own",
    )
    halo_late, early_sums = lax.optimization_barrier((halo_late, early_sums))
    late_beside = permute(halo_late, beside)
    near, result = final(
        bits,
        own_keep,
        own_recv,
        bounds,
        places,
        early_sums,
        other_sums,
        keep_own,
        recv_own,
        halo_late,
        late_beside,
        inbox,
    )
    return near.reshape(own * size, columns), result.reshape(own * size, columns)


def solution(mesh):
    spec = P(AXES, None)
    spec3 = P(AXES, None, None)
    return jax.shard_map(
        functools.partial(per_device, mesh.shape["rows"], mesh.shape["cols"]),
        mesh=mesh,
        in_specs=(spec, spec3, spec, spec3, P()),
        out_specs=(spec, spec),
        check_vma=False,
    )
```

time: 725 us -> 173 us (0.24); the launches traced: 717 us -> 173 us
  Pallas kernels: 545 us -> 54.1 us
  waiting for transfers between devices: 145 us -> 83.9 us
    pallas_call x3 -> x5, Pallas kernels: 545 us -> 54.1 us  [the longest x2 26.5 us: sums(): pl.pallas_call(functools.partial(sums_kernel, bits, whole), out_shape=jax...]
    ppermute x10 -> x11, waiting for transfers between devices: 121 us -> 44.2 us  [permute(): return lax.ppermute(value, AXES, pairs)]
    all_to_all x1, waiting for transfers between devices: 24 us -> 39.7 us  [per_device(): lax.all_to_all(outbox, AXES, split_axis=0, concat_axis=0, tiled=True)]
    ppermute x10 -> x11, starting transfers between devices: 9.48 us -> 15.2 us  [permute(): return lax.ppermute(value, AXES, pairs)]
  transfers between devices with their start and end apart: 11 -> 12, of which waited for: 4 -> 5; matrix products, arithmetic and copies ran while one was open for 0% -> 6% of each run, Pallas kernels for 2% -> 23%
where the time goes in v2:
time: 173 us
  waiting for transfers between devices  83.9 us (48%)
  Pallas kernels  54.1 us (31%)
  starting transfers between devices  23.7 us (14%)
  other arithmetic  6.73 us (4%)
  local copies, waits for them, and re-layouts  3.78 us (2%)
    ppermute x11, waiting for transfers between devices, permute(): return lax.ppermute(value, AXES, pairs)  44.2 us
    all_to_all x1, waiting for transfers between devices, per_device(): lax.all_to_all(outbox, AXES, split_axis=0, concat_axis=0, tiled=True)  39.7 us
    pallas_call x2, Pallas kernels, sums(): pl.pallas_call(functools.partial(sums_kernel, bits, whole), out_shape=jax...  26.5 us
    ppermute x11, starting transfers between devices, permute(): return lax.ppermute(value, AXES, pairs)  15.2 us
    pallas_call x2, Pallas kernels, gather_tiles(): pl.pallas_call(functools.partial(gather_kernel, first), out_shape=(jax.Sh...  13.9 us
    pallas_call x1, Pallas kernels, final(): pl.pallas_call(functools.partial(final_kernel, bits), out_shape=(result,...  13.6 us
    all_to_all x1, starting transfers between devices, per_device(): lax.all_to_all(outbox, AXES, split_axis=0, concat_axis=0, tiled=True)  8.55 us
  transfers between devices with their start and end apart: 12, of which 5 were waited for; matrix products, arithmetic and copies ran while one was open for 6% of the time, Pallas kernels for 23%

profile of v2, /device:TPU:7, one launch (start us, length us, event | category | flops | bytes accessed | tf_op | source)
XLA Modules:
  0.0 172.9 jit_solution(9191660753998916378)
XLA Ops:
  0.6 0.0 copy-start
  0.6 0.3 collective-permute-start.1
  1.0 3.3 %collective-permute-start.7 = (bf16[64,128,128]{2,1,0:T(8,128)(2,1)}, bf16[64,128,128]{2,1,0:T(8,128)(2,1)}, u32[]{:S(2)}, u32[]{:S(2)}) collective-permute-start(bf16[64,128,128]{2,1,0:T(8,128)(2,1)} %bitcast.13), channel_id=1, source_target_pairs={{4,0},{8,4},{12,8},{16,12},{20,16},{24,20},{28,24},{5,1},{9,5},{13... | collective-permute-start | bytes 6291464 | tf_op jit(solution)/shard_map/ppermute | solution.py:258
  4.2 1.3 collective-permute-start.4
  5.5 0.8 iota_add_fusion.1
  6.4 0.7 convert_reduce_fusion.3
  7.1 0.2 convert_reduce_fusion
  7.4 0.9 select_reduce_fusion
  8.3 0.0 copy-start.2
  8.3 7.0 %pack_send.1 = (bf16[128,128,128]{2,1,0:T(8,128)(2,1)}, bf16[128,128,128]{2,1,0:T(8,128)(2,1)}) custom-call(s32[512]{0:T(512)} %get-tuple-element.18.order_ref, bf16[512,128,128]{2,1,0:T(8,128)(2,1)} %tiles.3), custom_call_target="tpu_custom_call" | custom-call | bytes 16777216 | tf_op jit(solution)/shard_map/pack_send/pallas_call | solution.py:52
  15.3 0.1 collective-permute-start.6
  15.4 0.7 pad_add_fusion
  16.1 0.5 collective-permute-start
  16.6 5.9 %collective-permute-done = s32[384]{0:T(512)S(1)} collective-permute-done((s32[384]{0:T(512)S(1)}, s32[384]{0:T(512)S(1)}, u32[]{:S(2)}, u32[]{:S(2)}) %collective-permute-start) | collective-permute-done | bytes 1568 | tf_op jit(solution)/shard_map/ppermute | solution.py:258
  22.5 0.1 collective-permute-start.3
  22.7 0.0 copy-done.2
  22.7 0.1 and_select_fusion.7
  22.7 0.2 convert_reduce_fusion.1
  22.9 0.1 select_reduce_fusion.3
  23.1 24.5 %collective-permute-done.1.rest_2_ = bf16[64,128,128]{2,1,0:T(8,128)(2,1)} collective-permute-done((bf16[64,128,128]{2,1,0:T(8,128)(2,1)}, bf16[64,128,128]{2,1,0:T(8,128)(2,1)}, u32[]{:S(2)}, u32[]{:S(2)}) %collective-permute-start.1) | collective-permute-done | bytes 2097184 | tf_op jit(solution)/shard_map/ppermute | solution.py:258
  47.5 1.5 collective-permute-start.5
  49.1 0.4 collective-permute-done.7.rest_4_
  49.5 1.9 %collective-permute-start.2 = (bf16[64,128,128]{2,1,0:T(8,128)(2,1)}, bf16[64,128,128]{2,1,0:T(8,128)(2,1)}, u32[]{:S(2)}, u32[]{:S(2)}) collective-permute-start(bf16[64,128,128]{2,1,0:T(8,128)(2,1)} %collective-permute-done.1.rest_2_), channel_id=1, source_target_pairs={{0,4},{4,8},{8,12},{12,16},{16,20},{20,24},{24,28},{1,5},{5,9},{9,... | collective-permute-start | bytes 6291464 | tf_op jit(solution)/shard_map/ppermute | solution.py:258
  51.4 0.0 collective-permute-done.4.rest_1_
  51.4 1.9 %collective-permute-start.8 = (bf16[64,128,128]{2,1,0:T(8,128)(2,1)}, bf16[64,128,128]{2,1,0:T(8,128)(2,1)}, u32[]{:S(2)}, u32[]{:S(2)}) collective-permute-start(bf16[64,128,128]{2,1,0:T(8,128)(2,1)} %collective-permute-done.7.rest_4_), channel_id=1, source_target_pairs={{0,1},{1,0},{2,3},{3,2},{4,5},{5,4},{6,7},{7,6},{8,9},{9,8},{10,11... | collective-permute-start | bytes 6291464 | tf_op jit(solution)/shard_map/ppermute | solution.py:258
  53.4 0.0 copy-done
  53.4 2.1 %gather_fusion = bf16[64,128,128]{2,1,0:T(8,128)(2,1)} fusion(bf16[64,128,128]{2,1,0:T(8,128)(2,1)S(1)} %copy-done, s32[1024]{0:T(1024)S(1)} %pad_clamp_fusion), kind=kCustom, calls=%fused_computation | custom fusion | bytes 4194560 | tf_op jit(solution)/shard_map/gather | solution.py:324
  55.5 8.6 %all-to-all-start = ((bf16[64,128,128]{2,1,0:T(8,128)(2,1)}), bf16[64,128,128]{2,1,0:T(8,128)(2,1)}, u32[]{:S(2)}, u32[]{:S(2)}) async-start(bf16[64,128,128]{2,1,0:T(8,128)(2,1)} %gather_fusion), calls=%async_computation | async-start | bytes 4194304 | tf_op jit(solution)/shard_map/all_to_all | solution.py:325
  64.1 6.9 %pack_keep.1 = (bf16[128,128,128]{2,1,0:T(8,128)(2,1)}, bf16[128,128,128]{2,1,0:T(8,128)(2,1)}) custom-call(s32[512]{0:T(512)} %get-tuple-element.18.order_ref, bf16[512,128,128]{2,1,0:T(8,128)(2,1)} %tiles.3), custom_call_target="tpu_custom_call" | custom-call | bytes 16777216 | tf_op jit(solution)/shard_map/pack_keep/pallas_call | solution.py:52
  71.0 0.5 fusion.18
  71.5 0.5 slice.29
  72.0 1.9 %pad_add_fusion.1.bounds = s32[2]{0:T(128)} fusion(s32[1]{0:T(128)} %slice.29, s32[1]{0:T(128)} %bitcast.4), kind=kLoop, calls=%fused_computation.103 | loop fusion | flops 2 | bytes 16 | tf_op jit(solution)/shard_map/concatenate | solution.py:316
  73.9 0.6 fusion.17
  74.5 0.0 collective-permute-done.6.recv
  74.5 0.0 collective-permute-done.5.rest_3_
  74.5 0.0 collective-permute-done.8.rest_5_
  74.5 13.1 %cross.1 = bf16[64,128,128]{2,1,0:T(8,128)(2,1)} custom-call(s32[128]{0:T(128)} %get-tuple-element.31.meta_keep, s32[128]{0:T(128)} %get-tuple-element.29.meta_recv, s32[2]{0:T(128)} %pad_add_fusion.1.bounds, bf16[128,128,128]{2,1,0:T(8,128)(2,1)} %get-tuple-element.13.keep, bf16[128,128,128]{2,1,0:T(8,128)(2,1)} %collective-permute-done.6.recv, ...), custom_call_target="tpu_custom_call" | custom-call | flops 1073741824 | bytes 25165824 | tf_op jit(solution)/shard_map/cross/pallas_call | solution.py:121
  87.6 0.3 collective-permute-start.9
  87.8 0.0 collective-permute-done.3.recv
  87.8 13.4 %own.1.early = f32[64,128,128]{2,1,0:T(8,128)} custom-call(s32[128]{0:T(128)} %get-tuple-element.32.meta_keep, s32[128]{0:T(128)} %get-tuple-element.30.meta_recv, s32[2]{0:T(128)} %pad_add_fusion.1.bounds, bf16[128,128,128]{2,1,0:T(8,128)(2,1)} %get-tuple-element.10.keep, bf16[128,128,128]{2,1,0:T(8,128)(2,1)} %collective-permute-done.3.recv, ...), custom_call_target="tpu_custom_call" | custom-call | flops 1073741824 | bytes 25165824 | tf_op jit(solution)/shard_map/own/pallas_call | solution.py:121
  101.3 13.4 %collective-permute-done.2.late = bf16[64,128,128]{2,1,0:T(8,128)(2,1)} collective-permute-done((bf16[64,128,128]{2,1,0:T(8,128)(2,1)}, bf16[64,128,128]{2,1,0:T(8,128)(2,1)}, u32[]{:S(2)}, u32[]{:S(2)}) %collective-permute-start.2) | collective-permute-done | bytes 2097184 | tf_op jit(solution)/shard_map/ppermute | solution.py:258
  114.7 3.9 %collective-permute-start.10 = (bf16[64,128,128]{2,1,0:T(8,128)(2,1)}, bf16[64,128,128]{2,1,0:T(8,128)(2,1)}, u32[]{:S(2)}, u32[]{:S(2)}) collective-permute-start(bf16[64,128,128]{2,1,0:T(8,128)(2,1)} %collective-permute-done.2.late), channel_id=1, source_target_pairs={{0,1},{1,0},{2,3},{3,2},{4,5},{5,4},{6,7},{7,6},{8,9},{9,8},{10,11... | collective-permute-start | bytes 6291464 | tf_op jit(solution)/shard_map/ppermute | solution.py:258
  118.6 0.2 select_reduce_fusion.2
  118.8 0.2 convert_reduce_fusion.2
  119.0 0.6 multiply_add_fusion.1.places
  119.6 39.7 %all-to-all-done.inbox = bf16[64,128,128]{2,1,0:T(8,128)(2,1)} async-done(((bf16[64,128,128]{2,1,0:T(8,128)(2,1)}), bf16[64,128,128]{2,1,0:T(8,128)(2,1)}, u32[]{:S(2)}, u32[]{:S(2)}) %all-to-all-start) | async-done | bytes 2097184 | tf_op jit(solution)/shard_map/all_to_all | solution.py:325
  159.3 0.0 collective-permute-done.9.other
  159.3 0.0 collective-permute-done.10.beside
  159.3 0.0 copy-start.1
  159.3 13.6 %final.1 = (bf16[64,128,128]{2,1,0:T(8,128)(2,1)}, bf16[64,128,128]{2,1,0:T(8,128)(2,1)}) custom-call(s32[128]{0:T(128)} %get-tuple-element.32.meta_keep, s32[128]{0:T(128)} %get-tuple-element.30.meta_recv, s32[2]{0:T(128)} %pad_add_fusion.1.bounds, s32[64]{0:T(128)} %multiply_add_fusion.1.places, f32[64,128,128]{2,1,0:T(8,128)} %own.1.early, ...), custom_call_target="tpu_custom_call" | custom-call | flops 805306368 | bytes 20971520 | tf_op jit(solution)/shard_map/final/pallas_call | solution.py:211
  172.9 0.0 copy-done.1
  (9 shorter events, 0.1 us)
Async XLA Ops:
  0.6 52.7 %copy-start = (bf16[64,128,128]{2,1,0:T(8,128)(2,1)S(1)}, bf16[64,128,128]{2,1,0:T(8,128)(2,1)}, u32[]{:S(2)}) copy-start(bf16[64,128,128]{2,1,0:T(8,128)(2,1)} %param.8) | copy-start | bytes 6291460
  0.6 46.9 %collective-permute-start.1 = (bf16[64,128,128]{2,1,0:T(8,128)(2,1)}, bf16[64,128,128]{2,1,0:T(8,128)(2,1)}, u32[]{:S(2)}, u32[]{:S(2)}) collective-permute-start(bf16[64,128,128]{2,1,0:T(8,128)(2,1)} %bitcast.12), channel_id=1, source_target_pairs={{0,2},{1,3},{2,0},{3,1},{4,6},{5,7},{6,4},{7,5},{8,10},{9,11},{10,... | collective-permute-start | bytes 6291464 | tf_op jit(solution)/shard_map/ppermute | solution.py:258
  1.0 48.5 %collective-permute-start.7 = (bf16[64,128,128]{2,1,0:T(8,128)(2,1)}, bf16[64,128,128]{2,1,0:T(8,128)(2,1)}, u32[]{:S(2)}, u32[]{:S(2)}) collective-permute-start(bf16[64,128,128]{2,1,0:T(8,128)(2,1)} %bitcast.13), channel_id=1, source_target_pairs={{4,0},{8,4},{12,8},{16,12},{20,16},{24,20},{28,24},{5,1},{9,5},{13... | collective-permute-start | bytes 6291464 | tf_op jit(solution)/shard_map/ppermute | solution.py:258
  4.2 47.2 %collective-permute-start.4 = (bf16[64,128,128]{2,1,0:T(8,128)(2,1)}, bf16[64,128,128]{2,1,0:T(8,128)(2,1)}, u32[]{:S(2)}, u32[]{:S(2)}) collective-permute-start(bf16[64,128,128]{2,1,0:T(8,128)(2,1)} %bitcast.14), channel_id=1, source_target_pairs={{0,1},{1,0},{2,3},{3,2},{4,5},{5,4},{6,7},{7,6},{8,9},{9,8},{10,11... | collective-permute-start | bytes 6291464 | tf_op jit(solution)/shard_map/ppermute | solution.py:258
  8.3 14.4 %copy-start.2 = (s32[2048]{0:T(1024)S(1)}, s32[2048]{0:T(1024)}, u32[]{:S(2)}) copy-start(s32[2048]{0:T(1024)} %param.9) | copy-start | bytes 24580
  15.3 59.2 %collective-permute-start.6 = (bf16[128,128,128]{2,1,0:T(8,128)(2,1)}, bf16[128,128,128]{2,1,0:T(8,128)(2,1)}, u32[]{:S(2)}, u32[]{:S(2)}) collective-permute-start(bf16[128,128,128]{2,1,0:T(8,128)(2,1)} %get-tuple-element.14), channel_id=1, source_target_pairs={{0,1},{1,0},{2,3},{3,2},{4,5},{5,4},{6,7},{7,6},{8,9},{9,8},{10,11... | collective-permute-start | bytes 12582920 | tf_op jit(solution)/shard_map/ppermute | solution.py:258
  16.1 6.4 %collective-permute-start = (s32[384]{0:T(512)S(1)}, s32[384]{0:T(512)S(1)}, u32[]{:S(2)}, u32[]{:S(2)}) collective-permute-start(s32[384]{0:T(512)S(1)} %pad_add_fusion), channel_id=1, source_target_pairs={{0,1},{1,0},{2,3},{3,2},{4,5},{5,4},{6,7},{7,6},{8,9},{9,8},{10,11... | collective-permute-start | bytes 4616 | tf_op jit(solution)/shard_map/ppermute | solution.py:258
  22.5 65.3 %collective-permute-start.3 = (bf16[128,128,128]{2,1,0:T(8,128)(2,1)}, bf16[128,128,128]{2,1,0:T(8,128)(2,1)}, u32[]{:S(2)}, u32[]{:S(2)}) collective-permute-start(bf16[128,128,128]{2,1,0:T(8,128)(2,1)} %get-tuple-element.11), channel_id=1, source_target_pairs={{0,1},{1,0},{2,3},{3,2},{4,5},{5,4},{6,7},{7,6},{8,9},{9,8},{10,11... | collective-permute-start | bytes 12582920 | tf_op jit(solution)/shard_map/ppermute | solution.py:258
  47.5 26.9 %collective-permute-start.5 = (bf16[64,128,128]{2,1,0:T(8,128)(2,1)}, bf16[64,128,128]{2,1,0:T(8,128)(2,1)}, u32[]{:S(2)}, u32[]{:S(2)}) collective-permute-start(bf16[64,128,128]{2,1,0:T(8,128)(2,1)} %collective-permute-done.1.rest_2_), channel_id=1, source_target_pairs={{0,1},{1,0},{2,3},{3,2},{4,5},{5,4},{6,7},{7,6},{8,9},{9,8},{10,11... | collective-permute-start | bytes 6291464 | tf_op jit(solution)/shard_map/ppermute | solution.py:258
  49.5 65.2 %collective-permute-start.2 = (bf16[64,128,128]{2,1,0:T(8,128)(2,1)}, bf16[64,128,128]{2,1,0:T(8,128)(2,1)}, u32[]{:S(2)}, u32[]{:S(2)}) collective-permute-start(bf16[64,128,128]{2,1,0:T(8,128)(2,1)} %collective-permute-done.1.rest_2_), channel_id=1, source_target_pairs={{0,4},{4,8},{8,12},{12,16},{16,20},{20,24},{24,28},{1,5},{5,9},{9,... | collective-permute-start | bytes 6291464 | tf_op jit(solution)/shard_map/ppermute | solution.py:258
  51.4 23.1 %collective-permute-start.8 = (bf16[64,128,128]{2,1,0:T(8,128)(2,1)}, bf16[64,128,128]{2,1,0:T(8,128)(2,1)}, u32[]{:S(2)}, u32[]{:S(2)}) collective-permute-start(bf16[64,128,128]{2,1,0:T(8,128)(2,1)} %collective-permute-done.7.rest_4_), channel_id=1, source_target_pairs={{0,1},{1,0},{2,3},{3,2},{4,5},{5,4},{6,7},{7,6},{8,9},{9,8},{10,11... | collective-permute-start | bytes 6291464 | tf_op jit(solution)/shard_map/ppermute | solution.py:258
  55.5 103.8 %all-to-all-start = ((bf16[64,128,128]{2,1,0:T(8,128)(2,1)}), bf16[64,128,128]{2,1,0:T(8,128)(2,1)}, u32[]{:S(2)}, u32[]{:S(2)}) async-start(bf16[64,128,128]{2,1,0:T(8,128)(2,1)} %gather_fusion), calls=%async_computation | async-start | bytes 4194304 | tf_op jit(solution)/shard_map/all_to_all | solution.py:325
  87.6 71.7 %collective-permute-start.9 = (bf16[64,128,128]{2,1,0:T(8,128)(2,1)}, bf16[64,128,128]{2,1,0:T(8,128)(2,1)}, u32[]{:S(2)}, u32[]{:S(2)}) collective-permute-start(bf16[64,128,128]{2,1,0:T(8,128)(2,1)} %cross.1), channel_id=1, source_target_pairs={{0,2},{1,3},{2,0},{3,1},{4,6},{5,7},{6,4},{7,5},{8,10},{9,11},{10,... | collective-permute-start | bytes 6291464 | tf_op jit(solution)/shard_map/ppermute | solution.py:258
  114.7 44.6 %collective-permute-start.10 = (bf16[64,128,128]{2,1,0:T(8,128)(2,1)}, bf16[64,128,128]{2,1,0:T(8,128)(2,1)}, u32[]{:S(2)}, u32[]{:S(2)}) collective-permute-start(bf16[64,128,128]{2,1,0:T(8,128)(2,1)} %collective-permute-done.2.late), channel_id=1, source_target_pairs={{0,1},{1,0},{2,3},{3,2},{4,5},{5,4},{6,7},{7,6},{8,9},{9,8},{10,11... | collective-permute-start | bytes 6291464 | tf_op jit(solution)/shard_map/ppermute | solution.py:258
  159.3 13.6 %copy-start.1 = (bf16[64,128,128]{2,1,0:T(8,128)(2,1)S(1)}, bf16[64,128,128]{2,1,0:T(8,128)(2,1)}, u32[]{:S(2)}) copy-start(bf16[64,128,128]{2,1,0:T(8,128)(2,1)} %param.8) | copy-start | bytes 6291460

commit v3 on v2

--- a/solution.py
+++ b/solution.py
@@ -322,6 +322,38 @@
     held = lax.dynamic_slice_in_dim(slot_cluster, myself * own, own, 0)
     place_held = held // own * capacity + ranks_by(held // own, held % own)
     outbox = inverses[pick(place_held, jnp.arange(devices * capacity, dtype=jnp.int32))]
+
+    own_keep = meta[quarter_count : 2 * quarter_count]
+    own_recv = meta_recv[quarter_count : 2 * quarter_count]
+    cross_keep = meta[:quarter_count]
+    cross_recv = meta_recv[:quarter_count]
+    (
+        other_chip,
+        halo_early,
+        keep_cross,
+        keep_own,
+        outbox,
+        bounds,
+        own_keep,
+        own_recv,
+        cross_keep,
+        cross_recv,
+        places,
+    ) = lax.optimization_barrier(
+        (
+            other_chip,
+            halo_early,
+            keep_cross,
+            keep_own,
+            outbox,
+            bounds,
+            own_keep,
+            own_recv,
+            cross_keep,
+            cross_recv,
+            places,
+        )
+    )
     inbox = lax.all_to_all(outbox, AXES, split_axis=0, concat_axis=0, tiled=True)
 
     other_beside = permute(other_chip, beside)
@@ -332,8 +364,8 @@
         bits,
         True,
         jnp.bfloat16,
-        meta[:quarter_count],
-        meta_recv[:quarter_count],
+        cross_keep,
+        cross_recv,
         bounds,
         keep_cross,
         recv_cross,
@@ -341,8 +373,6 @@
         "cross",
     )
     other_sums = permute(cross, across)
-    own_keep = meta[quarter_count : 2 * quarter_count]
-    own_recv = meta_recv[quarter_count : 2 * quarter_count]
     early_sums = sums(
         bits,
         False,

time: 173 us -> 177 us (1.023)
  waiting for transfers between devices: 83.9 us -> 90.8 us
  starting transfers between devices: 23.7 us -> 19 us
    ppermute x11, waiting for transfers between devices: 44.2 us -> 51.2 us  [permute(): return lax.ppermute(value, AXES, pairs)]
    ppermute x11, starting transfers between devices: 15.2 us -> 12.4 us  [permute(): return lax.ppermute(value, AXES, pairs)]
    all_to_all x1, starting transfers between devices: 8.55 us -> 6.57 us  [per_device(): lax.all_to_all(outbox, AXES, split_axis=0, concat_axis=0, tiled=True)]
  transfers between devices with their start and end apart: 12 -> 12, of which waited for: 5 -> 4; matrix products, arithmetic and copies ran while one was open for 6% -> 6% of each run, Pallas kernels for 23% -> 23%
where the time goes in v3:
time: 177 us; the launch traced here: 176 us
  waiting for transfers between devices  90.8 us (51%)
  Pallas kernels  53.9 us (30%)
  starting transfers between devices  19 us (11%)
  other arithmetic  6.58 us (4%)
  local copies, waits for them, and re-layouts  5.12 us (3%)
    ppermute x11, waiting for transfers between devices, permute(): return lax.ppermute(value, AXES, pairs)  51.2 us
    all_to_all x1, waiting for transfers between devices, per_device(): lax.all_to_all(outbox, AXES, split_axis=0, concat_axis=0, tiled=True)  39.6 us
    pallas_call x2, Pallas kernels, sums(): pl.pallas_call(functools.partial(sums_kernel, bits, whole), out_shape=jax...  26.6 us
    pallas_call x2, Pallas kernels, gather_tiles(): pl.pallas_call(functools.partial(gather_kernel, first), out_shape=(jax.Sh...  13.9 us
    pallas_call x1, Pallas kernels, final(): pl.pallas_call(functools.partial(final_kernel, bits), out_shape=(result,...  13.4 us
    ppermute x11, starting transfers between devices, permute(): return lax.ppermute(value, AXES, pairs)  12.4 us
    all_to_all x1, starting transfers between devices, per_device(): lax.all_to_all(outbox, AXES, split_axis=0, concat_axis=0, tiled=True)  6.57 us
  transfers between devices with their start and end apart: 12, of which 4 were waited for; matrix products, arithmetic and copies ran while one was open for 6% of the time, Pallas kernels for 23%

profile of v3, /device:TPU:7, one launch (start us, length us, event | category | flops | bytes accessed | tf_op | source)
XLA Modules:
  0.0 176.2 jit_solution(16063812507713353322)
XLA Ops:
  0.6 0.0 copy-start
  0.6 0.7 collective-permute-start.5
  1.4 3.1 %collective-permute-start.1 = (bf16[64,128,128]{2,1,0:T(8,128)(2,1)}, bf16[64,128,128]{2,1,0:T(8,128)(2,1)}, u32[]{:S(2)}, u32[]{:S(2)}) collective-permute-start(bf16[64,128,128]{2,1,0:T(8,128)(2,1)} %bitcast.13), channel_id=1, source_target_pairs={{4,0},{8,4},{12,8},{16,12},{20,16},{24,20},{28,24},{5,1},{9,5},{13... | collective-permute-start | bytes 6291464 | tf_op jit(solution)/shard_map/ppermute | solution.py:258
  4.5 0.1 collective-permute-start
  4.6 0.8 iota_add_fusion.1
  5.5 0.7 convert_reduce_fusion.4
  6.2 0.2 convert_reduce_fusion
  6.4 0.9 select_reduce_fusion
  7.4 0.7 pad_add_fusion
  8.1 0.4 collective-permute-start.2
  8.5 0.0 copy-start.3
  8.5 7.0 %pack_send.1 = (bf16[128,128,128]{2,1,0:T(8,128)(2,1)}, bf16[128,128,128]{2,1,0:T(8,128)(2,1)}) custom-call(s32[512]{0:T(512)} %get-tuple-element.43.order_ref, bf16[512,128,128]{2,1,0:T(8,128)(2,1)} %tiles.3), custom_call_target="tpu_custom_call" | custom-call | bytes 16777216 | tf_op jit(solution)/shard_map/pack_send/pallas_call | solution.py:52
  15.5 0.1 collective-permute-start.7
  15.7 0.0 copy-done.3
  15.7 0.1 and_select_fusion.8
  15.8 0.2 convert_reduce_fusion.2
  15.9 0.0 collective-permute-done.2
  15.9 0.5 collective-permute-start.4
  16.5 6.9 %pack_keep.1 = (bf16[128,128,128]{2,1,0:T(8,128)(2,1)}, bf16[128,128,128]{2,1,0:T(8,128)(2,1)}) custom-call(s32[512]{0:T(512)} %get-tuple-element.43.order_ref, bf16[512,128,128]{2,1,0:T(8,128)(2,1)} %tiles.3), custom_call_target="tpu_custom_call" | custom-call | bytes 16777216 | tf_op jit(solution)/shard_map/pack_keep/pallas_call | solution.py:52
  23.4 0.1 select_reduce_fusion.3
  23.5 0.0 copy-done
  23.5 2.2 %gather_fusion = bf16[64,128,128]{2,1,0:T(8,128)(2,1)} fusion(bf16[64,128,128]{2,1,0:T(8,128)(2,1)S(1)} %copy-done, s32[1024]{0:T(1024)S(1)} %pad_clamp_fusion), kind=kCustom, calls=%fused_computation | custom fusion | bytes 4194560 | tf_op jit(solution)/shard_map/gather | solution.py:324
  25.7 0.2 select_reduce_fusion.2
  25.9 0.2 convert_reduce_fusion.1
  26.1 0.5 multiply_add_fusion.places
  26.6 0.6 fusion.18
  27.2 0.5 slice.27
  27.7 1.8 %pad_add_fusion.1.bounds = s32[2]{0:T(128)} fusion(s32[1]{0:T(128)} %slice.27, s32[1]{0:T(128)} %bitcast.6), kind=kLoop, calls=%fused_computation.103 | loop fusion | flops 2 | bytes 16 | tf_op jit(solution)/shard_map/concatenate | solution.py:316
  29.5 0.5 fusion.17
  30.1 20.6 %collective-permute-done.1.rest_4_ = bf16[64,128,128]{2,1,0:T(8,128)(2,1)} collective-permute-done((bf16[64,128,128]{2,1,0:T(8,128)(2,1)}, bf16[64,128,128]{2,1,0:T(8,128)(2,1)}, u32[]{:S(2)}, u32[]{:S(2)}) %collective-permute-start.1) | collective-permute-done | bytes 2097184 | tf_op jit(solution)/shard_map/ppermute | solution.py:258
  50.7 1.0 collective-permute-done.rest_2_
  51.7 1.3 collective-permute-start.8
  53.0 0.0 collective-permute-start.6
  53.0 0.0 collective-permute-done.5.rest_1_
  53.0 3.4 %collective-permute-start.3 = (bf16[64,128,128]{2,1,0:T(8,128)(2,1)}, bf16[64,128,128]{2,1,0:T(8,128)(2,1)}, u32[]{:S(2)}, u32[]{:S(2)}) collective-permute-start(bf16[64,128,128]{2,1,0:T(8,128)(2,1)} %collective-permute-done.rest_2_), channel_id=1, source_target_pairs={{0,4},{4,8},{8,12},{12,16},{16,20},{20,24},{24,28},{1,5},{5,9},{9,... | collective-permute-start | bytes 6291464 | tf_op jit(solution)/shard_map/ppermute | solution.py:258
  56.4 6.6 %all-to-all-start = ((bf16[64,128,128]{2,1,0:T(8,128)(2,1)}), bf16[64,128,128]{2,1,0:T(8,128)(2,1)}, u32[]{:S(2)}, u32[]{:S(2)}) async-start(bf16[64,128,128]{2,1,0:T(8,128)(2,1)} %gather_fusion), calls=%async_computation | async-start | bytes 4194304 | tf_op jit(solution)/shard_map/all_to_all | solution.py:357
  63.0 0.0 collective-permute-done.7.recv
  63.0 0.0 collective-permute-done.8.rest_5_
  63.0 0.0 collective-permute-done.6.rest_3_
  63.0 0.0 copy-start.2
  63.0 1.3 copy-done.2
  64.3 13.1 %cross.1 = bf16[64,128,128]{2,1,0:T(8,128)(2,1)} custom-call(s32[128]{0:T(128)} %get-tuple-element.31.meta_keep, s32[128]{0:T(128)} %get-tuple-element.32.meta_recv, s32[2]{0:T(128)} %pad_add_fusion.1.bounds, bf16[128,128,128]{2,1,0:T(8,128)(2,1)} %get-tuple-element.33.keep, bf16[128,128,128]{2,1,0:T(8,128)(2,1)} %collective-permute-done.7.recv, ...), custom_call_target="tpu_custom_call" | custom-call | flops 1073741824 | bytes 25165824 | tf_op jit(solution)/shard_map/cross/pallas_call | solution.py:121
  77.4 0.3 collective-permute-start.9
  77.8 0.0 collective-permute-done.4.recv
  77.8 13.5 %own.1.early = f32[64,128,128]{2,1,0:T(8,128)} custom-call(s32[128]{0:T(128)} %get-tuple-element.23.meta_keep, s32[128]{0:T(128)} %get-tuple-element.24.meta_recv, s32[2]{0:T(128)} %pad_add_fusion.1.bounds, bf16[128,128,128]{2,1,0:T(8,128)(2,1)} %get-tuple-element.28.keep, bf16[128,128,128]{2,1,0:T(8,128)(2,1)} %collective-permute-done.4.recv, ...), custom_call_target="tpu_custom_call" | custom-call | flops 1073741824 | bytes 25165824 | tf_op jit(solution)/shard_map/own/pallas_call | solution.py:121
  91.3 29.5 %collective-permute-done.3.late = bf16[64,128,128]{2,1,0:T(8,128)(2,1)} collective-permute-done((bf16[64,128,128]{2,1,0:T(8,128)(2,1)}, bf16[64,128,128]{2,1,0:T(8,128)(2,1)}, u32[]{:S(2)}, u32[]{:S(2)}) %collective-permute-start.3) | collective-permute-done | bytes 2097184 | tf_op jit(solution)/shard_map/ppermute | solution.py:258
  120.8 2.3 %collective-permute-start.10 = (bf16[64,128,128]{2,1,0:T(8,128)(2,1)}, bf16[64,128,128]{2,1,0:T(8,128)(2,1)}, u32[]{:S(2)}, u32[]{:S(2)}) collective-permute-start(bf16[64,128,128]{2,1,0:T(8,128)(2,1)} %collective-permute-done.3.late), channel_id=1, source_target_pairs={{0,1},{1,0},{2,3},{3,2},{4,5},{5,4},{6,7},{7,6},{8,9},{9,8},{10,11... | collective-permute-start | bytes 6291464 | tf_op jit(solution)/shard_map/ppermute | solution.py:258
  123.2 39.6 %all-to-all-done.inbox = bf16[64,128,128]{2,1,0:T(8,128)(2,1)} async-done(((bf16[64,128,128]{2,1,0:T(8,128)(2,1)}), bf16[64,128,128]{2,1,0:T(8,128)(2,1)}, u32[]{:S(2)}, u32[]{:S(2)}) %all-to-all-start) | async-done | bytes 2097184 | tf_op jit(solution)/shard_map/all_to_all | solution.py:357
  162.8 0.0 collective-permute-done.9.other
  162.8 0.0 collective-permute-done.10.beside
  162.8 0.0 copy-start.1
  162.8 13.4 %final.1 = (bf16[64,128,128]{2,1,0:T(8,128)(2,1)}, bf16[64,128,128]{2,1,0:T(8,128)(2,1)}) custom-call(s32[128]{0:T(128)} %get-tuple-element.23.meta_keep, s32[128]{0:T(128)} %get-tuple-element.24.meta_recv, s32[2]{0:T(128)} %pad_add_fusion.1.bounds, s32[64]{0:T(128)} %multiply_add_fusion.places, f32[64,128,128]{2,1,0:T(8,128)} %own.1.early, ...), custom_call_target="tpu_custom_call" | custom-call | flops 805306368 | bytes 20971520 | tf_op jit(solution)/shard_map/final/pallas_call | solution.py:211
  176.2 0.0 copy-done.1
  (9 shorter events, 0.1 us)
Async XLA Ops:
  0.6 22.9 %copy-start = (bf16[64,128,128]{2,1,0:T(8,128)(2,1)S(1)}, bf16[64,128,128]{2,1,0:T(8,128)(2,1)}, u32[]{:S(2)}) copy-start(bf16[64,128,128]{2,1,0:T(8,128)(2,1)} %param.8) | copy-start | bytes 6291460
  0.6 52.3 %collective-permute-start.5 = (bf16[64,128,128]{2,1,0:T(8,128)(2,1)}, bf16[64,128,128]{2,1,0:T(8,128)(2,1)}, u32[]{:S(2)}, u32[]{:S(2)}) collective-permute-start(bf16[64,128,128]{2,1,0:T(8,128)(2,1)} %bitcast.12), channel_id=1, source_target_pairs={{0,1},{1,0},{2,3},{3,2},{4,5},{5,4},{6,7},{7,6},{8,9},{9,8},{10,11... | collective-permute-start | bytes 6291464 | tf_op jit(solution)/shard_map/ppermute | solution.py:258
  1.4 49.3 %collective-permute-start.1 = (bf16[64,128,128]{2,1,0:T(8,128)(2,1)}, bf16[64,128,128]{2,1,0:T(8,128)(2,1)}, u32[]{:S(2)}, u32[]{:S(2)}) collective-permute-start(bf16[64,128,128]{2,1,0:T(8,128)(2,1)} %bitcast.13), channel_id=1, source_target_pairs={{4,0},{8,4},{12,8},{16,12},{20,16},{24,20},{28,24},{5,1},{9,5},{13... | collective-permute-start | bytes 6291464 | tf_op jit(solution)/shard_map/ppermute | solution.py:258
  4.5 47.1 %collective-permute-start = (bf16[64,128,128]{2,1,0:T(8,128)(2,1)}, bf16[64,128,128]{2,1,0:T(8,128)(2,1)}, u32[]{:S(2)}, u32[]{:S(2)}) collective-permute-start(bf16[64,128,128]{2,1,0:T(8,128)(2,1)} %bitcast.14), channel_id=1, source_target_pairs={{0,2},{1,3},{2,0},{3,1},{4,6},{5,7},{6,4},{7,5},{8,10},{9,11},{10,... | collective-permute-start | bytes 6291464 | tf_op jit(solution)/shard_map/ppermute | solution.py:258
  8.1 7.9 %collective-permute-start.2 = (s32[384]{0:T(512)S(1)}, s32[384]{0:T(512)S(1)}, u32[]{:S(2)}, u32[]{:S(2)}) collective-permute-start(s32[384]{0:T(512)S(1)} %pad_add_fusion), channel_id=1, source_target_pairs={{0,1},{1,0},{2,3},{3,2},{4,5},{5,4},{6,7},{7,6},{8,9},{9,8},{10,11... | collective-permute-start | bytes 4616 | tf_op jit(solution)/shard_map/ppermute | solution.py:258
  8.5 7.1 %copy-start.3 = (s32[2048]{0:T(1024)S(1)}, s32[2048]{0:T(1024)}, u32[]{:S(2)}) copy-start(s32[2048]{0:T(1024)} %param.9) | copy-start | bytes 24580
  15.5 47.4 %collective-permute-start.7 = (bf16[128,128,128]{2,1,0:T(8,128)(2,1)}, bf16[128,128,128]{2,1,0:T(8,128)(2,1)}, u32[]{:S(2)}, u32[]{:S(2)}) collective-permute-start(bf16[128,128,128]{2,1,0:T(8,128)(2,1)} %get-tuple-element.34), channel_id=1, source_target_pairs={{0,1},{1,0},{2,3},{3,2},{4,5},{5,4},{6,7},{7,6},{8,9},{9,8},{10,11... | collective-permute-start | bytes 12582920 | tf_op jit(solution)/shard_map/ppermute | solution.py:258
  15.9 61.8 %collective-permute-start.4 = (bf16[128,128,128]{2,1,0:T(8,128)(2,1)}, bf16[128,128,128]{2,1,0:T(8,128)(2,1)}, u32[]{:S(2)}, u32[]{:S(2)}) collective-permute-start(bf16[128,128,128]{2,1,0:T(8,128)(2,1)} %get-tuple-element.29), channel_id=1, source_target_pairs={{0,1},{1,0},{2,3},{3,2},{4,5},{5,4},{6,7},{7,6},{8,9},{9,8},{10,11... | collective-permute-start | bytes 12582920 | tf_op jit(solution)/shard_map/ppermute | solution.py:258
  51.7 11.3 %collective-permute-start.8 = (bf16[64,128,128]{2,1,0:T(8,128)(2,1)}, bf16[64,128,128]{2,1,0:T(8,128)(2,1)}, u32[]{:S(2)}, u32[]{:S(2)}) collective-permute-start(bf16[64,128,128]{2,1,0:T(8,128)(2,1)} %collective-permute-done.1.rest_4_), channel_id=1, source_target_pairs={{0,1},{1,0},{2,3},{3,2},{4,5},{5,4},{6,7},{7,6},{8,9},{9,8},{10,11... | collective-permute-start | bytes 6291464 | tf_op jit(solution)/shard_map/ppermute | solution.py:258
  53.0 10.0 %collective-permute-start.6 = (bf16[64,128,128]{2,1,0:T(8,128)(2,1)}, bf16[64,128,128]{2,1,0:T(8,128)(2,1)S(1)}, u32[]{:S(2)}, u32[]{:S(2)}) collective-permute-start(bf16[64,128,128]{2,1,0:T(8,128)(2,1)} %collective-permute-done.rest_2_), channel_id=1, source_target_pairs={{0,1},{1,0},{2,3},{3,2},{4,5},{5,4},{6,7},{7,6},{8,9},{9,8},{10,11... | collective-permute-start | bytes 6291464 | tf_op jit(solution)/shard_map/ppermute | solution.py:258
  53.0 67.9 %collective-permute-start.3 = (bf16[64,128,128]{2,1,0:T(8,128)(2,1)}, bf16[64,128,128]{2,1,0:T(8,128)(2,1)}, u32[]{:S(2)}, u32[]{:S(2)}) collective-permute-start(bf16[64,128,128]{2,1,0:T(8,128)(2,1)} %collective-permute-done.rest_2_), channel_id=1, source_target_pairs={{0,4},{4,8},{8,12},{12,16},{16,20},{20,24},{24,28},{1,5},{5,9},{9,... | collective-permute-start | bytes 6291464 | tf_op jit(solution)/shard_map/ppermute | solution.py:258
  56.4 106.4 %all-to-all-start = ((bf16[64,128,128]{2,1,0:T(8,128)(2,1)}), bf16[64,128,128]{2,1,0:T(8,128)(2,1)}, u32[]{:S(2)}, u32[]{:S(2)}) async-start(bf16[64,128,128]{2,1,0:T(8,128)(2,1)} %gather_fusion), calls=%async_computation | async-start | bytes 4194304 | tf_op jit(solution)/shard_map/all_to_all | solution.py:357
  63.0 1.3 copy-start.2
  77.4 85.4 %collective-permute-start.9 = (bf16[64,128,128]{2,1,0:T(8,128)(2,1)}, bf16[64,128,128]{2,1,0:T(8,128)(2,1)}, u32[]{:S(2)}, u32[]{:S(2)}) collective-permute-start(bf16[64,128,128]{2,1,0:T(8,128)(2,1)} %cross.1), channel_id=1, source_target_pairs={{0,2},{1,3},{2,0},{3,1},{4,6},{5,7},{6,4},{7,5},{8,10},{9,11},{10,... | collective-permute-start | bytes 6291464 | tf_op jit(solution)/shard_map/ppermute | solution.py:258
  120.8 41.9 %collective-permute-start.10 = (bf16[64,128,128]{2,1,0:T(8,128)(2,1)}, bf16[64,128,128]{2,1,0:T(8,128)(2,1)}, u32[]{:S(2)}, u32[]{:S(2)}) collective-permute-start(bf16[64,128,128]{2,1,0:T(8,128)(2,1)} %collective-permute-done.3.late), channel_id=1, source_target_pairs={{0,1},{1,0},{2,3},{3,2},{4,5},{5,4},{6,7},{7,6},{8,9},{9,8},{10,11... | collective-permute-start | bytes 6291464 | tf_op jit(solution)/shard_map/ppermute | solution.py:258
  162.8 13.4 %copy-start.1 = (bf16[64,128,128]{2,1,0:T(8,128)(2,1)S(1)}, bf16[64,128,128]{2,1,0:T(8,128)(2,1)}, u32[]{:S(2)}) copy-start(bf16[64,128,128]{2,1,0:T(8,128)(2,1)} %param.8) | copy-start | bytes 6291460

commit v4 on v3

--- a/solution.py
+++ b/solution.py
@@ -1,4 +1,5 @@
 import functools
+import math
 
 import jax
 import jax.numpy as jnp
@@ -25,8 +26,9 @@
 
 def gather_kernel(first, order_ref, tiles, *rest):
     outs, (held, sem) = rest[:-2], rest[-2:]
+    parts = len(outs)
     count = outs[0].shape[0]
-    for part in range(len(outs)):
+    for part in range(parts):
 
         def fetch(turn, carry):
             place = part * count + turn
@@ -40,14 +42,13 @@
     for part, out in enumerate(outs):
         block = held.at[pl.ds(part * count, count)]
         pltpu.make_async_copy(block, block, sem.at[part]).wait()
-        copies.append(pltpu.make_async_copy(block, out, sem.at[len(outs) + part]))
+        copies.append(pltpu.make_async_copy(block, out, sem.at[parts + part]))
         copies[-1].start()
     for copy in copies:
         copy.wait()
 
 
-def gather_tiles(order, tiles, first, parts, name):
-    count = tiles.shape[0] // 4
+def gather_tiles(order, tiles, first, parts, count, name):
     block = (count,) + tiles.shape[1:]
     return pl.pallas_call(
         functools.partial(gather_kernel, first),
@@ -58,8 +59,10 @@
             pltpu.VMEM((parts * count,) + tiles.shape[1:], tiles.dtype),
             pltpu.SemaphoreType.DMA((2 * parts,)),
         ],
-        compiler_params=params(60),
-        cost_estimate=cost(0, 8 * parts),
+        compiler_params=params(63),
+        cost_estimate=pl.CostEstimate(
+            flops=0, bytes_accessed=8 * parts * math.prod(block), transcendentals=0
+        ),
         name=name,
     )(order, tiles)
 
@@ -79,8 +82,8 @@
     pieces, (out, band, mine, theirs, acc, sem) = rest[:-6], rest[-6:]
     size = pieces[0].shape[0]
     loads = [
-        pltpu.make_async_copy(piece, band.at[pl.ds(place * size, size)], sem.at[0])
-        for place, piece in enumerate(pieces)
+        pltpu.make_async_copy(part, band.at[pl.ds(place * size, size)], sem.at[0])
+        for place, part in enumerate(pieces)
     ]
     loads.append(pltpu.make_async_copy(keep, mine, sem.at[1]))
     loads.append(pltpu.make_async_copy(recv, theirs, sem.at[2]))
@@ -130,32 +133,32 @@
             pltpu.VMEM(block, jnp.float32),
             pltpu.SemaphoreType.DMA((3,)),
         ],
-        compiler_params=params(60),
+        compiler_params=params(63),
         cost_estimate=cost(4 * keep.size * block[2], 24),
         name=name,
     )(meta_keep, meta_recv, bounds, keep, recv, *pieces)
 
 
-def final_kernel(
-    bits, meta_keep, meta_recv, bounds, places, early, other, keep, recv, late, beside, inbox, *rest
-):
-    near, out, acc, sent, band, mine, theirs, inverse, sem = rest
+def near_kernel(bits, meta_keep, meta_recv, bounds, early, other, keep, recv, late, beside, *rest):
+    near, acc, sent, band, mine, theirs, sem = rest
     count = keep.shape[0]
     size = late.shape[0]
     loads = [
         pltpu.make_async_copy(early, acc, sem.at[0]),
-        pltpu.make_async_copy(other, sent, sem.at[1]),
         pltpu.make_async_copy(late, band.at[pl.ds(0, size)], sem.at[2]),
         pltpu.make_async_copy(beside, band.at[pl.ds(size, size)], sem.at[3]),
-        pltpu.make_async_copy(inbox, inverse, sem.at[4]),
+        pltpu.make_async_copy(other, sent, sem.at[1]),
     ]
     for load in loads:
         load.start()
     sides = ((meta_keep, keep, mine), (meta_recv, recv, theirs))
 
     def chunk_copy(side, chunk):
-        piece = pl.ds(pl.multiple_of(chunk * CHUNK, CHUNK), CHUNK)
-        return pltpu.make_async_copy(sides[side][1].at[piece], sides[side][2].at[piece], sem.at[5 + side])
+        start = pl.multiple_of(chunk * CHUNK, CHUNK)
+        piece = pl.ds(start, CHUNK)
+        return pltpu.make_async_copy(
+            sides[side][1].at[piece], sides[side][2].at[piece], sem.at[4 + side]
+        )
 
     for side in (0, 1):
 
@@ -164,8 +167,6 @@
             return carry
 
         lax.fori_loop(bounds[side] // CHUNK, count // CHUNK, fetch, 0)
-    for load in loads[:4]:
-        load.wait()
     for side in (0, 1):
 
         def settle(chunk, carry):
@@ -173,6 +174,8 @@
             return carry
 
         lax.fori_loop(bounds[side] // CHUNK, count // CHUNK, settle, 0)
+    for load in loads:
+        load.wait()
     for side, (meta_ref, keep_ref, held) in enumerate(sides):
 
         def add(turn, carry):
@@ -191,41 +194,67 @@
         even = (first + 7) // 8
         lax.fori_loop(first, even * 8, add, 0)
         lax.fori_loop(even, count // 8, add_eight, 0)
-    loads[4].wait()
-
-    def apply(turn, carry):
-        block = (acc[turn] + sent[turn].astype(jnp.float32)).astype(jnp.bfloat16)
-        near[turn] = block
-        out[turn] = jnp.dot(
-            inverse[places[turn]], block, preferred_element_type=jnp.float32
-        ).astype(jnp.bfloat16)
-        return carry
-
-    lax.fori_loop(0, size, apply, 0, unroll=8)
-
-
-def final(bits, meta_keep, meta_recv, bounds, places, early, other, keep, recv, late, beside, inbox):
+    near[...] = (acc[...] + sent[...].astype(jnp.float32)).astype(jnp.bfloat16)
+
+
+def near_sums(bits, meta_keep, meta_recv, bounds, early, other, keep, recv, late, beside):
     block = late.shape
     held = pltpu.VMEM(keep.shape, keep.dtype)
-    result = jax.ShapeDtypeStruct(block, jnp.bfloat16)
     return pl.pallas_call(
-        functools.partial(final_kernel, bits),
-        out_shape=(result, result),
-        in_specs=[SMEM] * 4 + [HBM] * 7,
-        out_specs=(VMEM, VMEM),
+        functools.partial(near_kernel, bits),
+        out_shape=jax.ShapeDtypeStruct(block, jnp.bfloat16),
+        in_specs=[SMEM] * 3 + [HBM] * 6,
+        out_specs=VMEM,
         scratch_shapes=[
             pltpu.VMEM(block, jnp.float32),
             pltpu.VMEM(block, jnp.bfloat16),
             pltpu.VMEM((2 * block[0],) + block[1:], jnp.bfloat16),
             held,
             held,
-            pltpu.VMEM(inbox.shape, jnp.bfloat16),
-            pltpu.SemaphoreType.DMA((7,)),
+            pltpu.SemaphoreType.DMA((6,)),
         ],
-        compiler_params=params(60),
-        cost_estimate=cost(3 * keep.size * block[2], 20),
-        name="final",
-    )(meta_keep, meta_recv, bounds, places, early, other, keep, recv, late, beside, inbox)
+        compiler_params=params(63),
+        cost_estimate=cost(2 * keep.size * block[2], 18),
+        name="near",
+    )(meta_keep, meta_recv, bounds, early, other, keep, recv, late, beside)
+
+
+def apply_kernel(places, near, *rest):
+    inbox, (out, inverse, sem) = rest[:-3], rest[-3:]
+    loads = []
+    for place, part in enumerate(inbox):
+        count = part.shape[0]
+        loads.append(
+            pltpu.make_async_copy(part, inverse.at[pl.ds(place * count, count)], sem.at[place])
+        )
+        loads[-1].start()
+    for load in loads:
+        load.wait()
+
+    def apply(turn, carry):
+        out[turn] = jnp.dot(
+            inverse[places[turn]], near[turn], preferred_element_type=jnp.float32
+        ).astype(jnp.bfloat16)
+        return carry
+
+    lax.fori_loop(0, near.shape[0], apply, 0, unroll=16)
+
+
+def apply_inverses(places, near, inbox):
+    block = inbox[0].shape
+    return pl.pallas_call(
+        apply_kernel,
+        out_shape=jax.ShapeDtypeStruct(near.shape, jnp.bfloat16),
+        in_specs=[SMEM, VMEM] + [HBM] * len(inbox),
+        out_specs=VMEM,
+        scratch_shapes=[
+            pltpu.VMEM((len(inbox) * block[0],) + block[1:], jnp.bfloat16),
+            pltpu.SemaphoreType.DMA((len(inbox),)),
+        ],
+        compiler_params=params(63),
+        cost_estimate=cost(2 * near.size * near.shape[1], 6),
+        name="apply",
+    )(places, near, *inbox)
 
 
 def ranks_by(labels, key):
@@ -280,6 +309,21 @@
     other_chip = permute(blocks, across)
     halo_early = permute(blocks, early)
     own_beside = permute(blocks, beside)
+
+    capacity = -(-own // devices)
+    local = jnp.arange(own, dtype=jnp.int32)
+    source = pick(slot_cluster, myself * own + local) // own
+    places = ranks_by(source, local) * devices + source
+    held = lax.dynamic_slice_in_dim(slot_cluster, myself * own, own, 0)
+    target = held // own
+    place_held = ranks_by(target, held % own) * devices + target
+    outbox_order = pick(place_held, jnp.arange(devices * capacity, dtype=jnp.int32))
+    outbox = gather_tiles(outbox_order, inverses, 0, capacity, devices, "pack_inverses")
+
+    def exchange(value):
+        return lax.all_to_all(value, AXES, split_axis=0, concat_axis=0, tiled=True)
+
+    inbox = [exchange(outbox[0])]
 
     group = own * cols
     base = row * group
@@ -306,22 +350,19 @@
     bound_keep = jnp.sum((bucket == 1).astype(jnp.int32), keepdims=True)
     bound_send = jnp.sum((bucket == 4).astype(jnp.int32), keepdims=True)
     padding = jnp.zeros((127,), jnp.int32)
-    send_cross, send_own = gather_tiles(order, tiles, 2 * quarter_count, 2, "pack_send")
+    order, outbox = lax.optimization_barrier((order, outbox))
+    send_cross, send_own = gather_tiles(
+        order, tiles, 2 * quarter_count, 2, quarter_count, "pack_send"
+    )
     recv_cross = permute(send_cross, beside)
     recv_own = permute(send_own, beside)
     meta_recv = permute(
         jnp.concatenate([meta[2 * quarter_count :], bound_send, padding]), beside
     )
-    keep_cross, keep_own = gather_tiles(order, tiles, 0, 2, "pack_keep")
+    keep_cross, keep_own = gather_tiles(
+        order, tiles, 0, 2, quarter_count, "pack_keep"
+    )
     bounds = jnp.concatenate([bound_keep, meta_recv[2 * quarter_count : 2 * quarter_count + 1]])
-
-    capacity = -(-own // devices)
-    local = jnp.arange(own, dtype=jnp.int32)
-    source = pick(slot_cluster, myself * own + local) // own
-    places = source * capacity + ranks_by(source, local)
-    held = lax.dynamic_slice_in_dim(slot_cluster, myself * own, own, 0)
-    place_held = held // own * capacity + ranks_by(held // own, held % own)
-    outbox = inverses[pick(place_held, jnp.arange(devices * capacity, dtype=jnp.int32))]
 
     own_keep = meta[quarter_count : 2 * quarter_count]
     own_recv = meta_recv[quarter_count : 2 * quarter_count]
@@ -330,6 +371,7 @@
     (
         other_chip,
         halo_early,
+        inbox,
         keep_cross,
         keep_own,
         outbox,
@@ -343,6 +385,7 @@
         (
             other_chip,
             halo_early,
+            inbox,
             keep_cross,
             keep_own,
             outbox,
@@ -354,11 +397,11 @@
             places,
         )
     )
-    inbox = lax.all_to_all(outbox, AXES, split_axis=0, concat_axis=0, tiled=True)
 
     other_beside = permute(other_chip, beside)
     halo_late = permute(other_chip, late)
     early_beside = permute(halo_early, beside)
+    inbox += [exchange(part) for part in outbox[1:]]
     group_pieces = (blocks, own_beside, other_chip, other_beside)
     cross = sums(
         bits,
@@ -385,22 +428,21 @@
         group_pieces,
         "own",
     )
-    halo_late, early_sums = lax.optimization_barrier((halo_late, early_sums))
+    halo_late, early_sums, inbox = lax.optimization_barrier((halo_late, early_sums, inbox))
     late_beside = permute(halo_late, beside)
-    near, result = final(
+    near = near_sums(
         bits,
         own_keep,
         own_recv,
         bounds,
-        places,
         early_sums,
         other_sums,
         keep_own,
         recv_own,
         halo_late,
         late_beside,
-        inbox,
-    )
+    )
+    result = apply_inverses(places, near, inbox)
     return near.reshape(own * size, columns), result.reshape(own * size, columns)
 
 

time: 177 us -> 182 us (1.028)
  Pallas kernels: 53.9 us -> 59.8 us
  waiting for transfers between devices: 90.8 us -> 86.9 us
  local copies, waits for them, and re-layouts: 5.12 us -> 1.54 us
  starting transfers between devices: 19 us -> 22.3 us
  other arithmetic: 6.58 us -> 8.77 us
    ppermute x11, waiting for transfers between devices: 51.2 us -> 10.4 us  [permute(): return lax.ppermute(value, AXES, pairs)]
    all_to_all x1 -> x2, waiting for transfers between devices: 39.6 us -> 76.5 us  [exchange(): return lax.all_to_all(value, AXES, split_axis=0, concat_axis=0, tiled=True)]
    all_to_all x1 -> x2, starting transfers between devices: 6.57 us -> 13.4 us  [exchange(): return lax.all_to_all(value, AXES, split_axis=0, concat_axis=0, tiled=True)]
    ppermute x11, starting transfers between devices: 12.4 us -> 8.91 us  [permute(): return lax.ppermute(value, AXES, pairs)]
    pallas_call x2 -> x3, Pallas kernels: 13.9 us -> 17 us  [gather_tiles(): pl.pallas_call(functools.partial(gather_kernel, first), out_shape=(jax.Sh...]
    pallas_call x1 -> x2, Pallas kernels: 13.4 us -> 16.2 us  [the longest x1 10.6 us: near_sums(): pl.pallas_call(functools.partial(near_kernel, bits), out_shape=jax.ShapeD...]
    gather x1 -> x0, local copies, waits for them, and re-layouts: 2.16 us -> none  [per_device(): inverses[pick(place_held, jnp.arange(devices * capacity, dtype=jnp.int32))]]
  transfers between devices with their start and end apart: 12 -> 13, of which waited for: 4 -> 4; matrix products, arithmetic and copies ran while one was open for 6% -> 6% of each run, Pallas kernels for 23% -> 24%
where the time goes in v4:
time: 182 us; the launch traced here: 180 us
  waiting for transfers between devices  86.9 us (48%)
  Pallas kernels  59.8 us (33%)
  starting transfers between devices  22.3 us (12%)
  other arithmetic  8.77 us (5%)
    all_to_all x2, waiting for transfers between devices, exchange(): return lax.all_to_all(value, AXES, split_axis=0, concat_axis=0, tiled=True)  76.5 us
    pallas_call x2, Pallas kernels, sums(): pl.pallas_call(functools.partial(sums_kernel, bits, whole), out_shape=jax...  26.6 us
    pallas_call x3, Pallas kernels, gather_tiles(): pl.pallas_call(functools.partial(gather_kernel, first), out_shape=(jax.Sh...  17 us
    all_to_all x2, starting transfers between devices, exchange(): return lax.all_to_all(value, AXES, split_axis=0, concat_axis=0, tiled=True)  13.4 us
    pallas_call x1, Pallas kernels, near_sums(): pl.pallas_call(functools.partial(near_kernel, bits), out_shape=jax.ShapeD...  10.6 us
    ppermute x11, waiting for transfers between devices, permute(): return lax.ppermute(value, AXES, pairs)  10.4 us
    ppermute x11, starting transfers between devices, permute(): return lax.ppermute(value, AXES, pairs)  8.91 us
    pallas_call x1, Pallas kernels, apply_inverses(): pl.pallas_call(apply_kernel, out_shape=jax.ShapeDtypeStruct(near.shape, j...  5.65 us
  transfers between devices with their start and end apart: 13, of which 4 were waited for; matrix products, arithmetic and copies ran while one was open for 6% of the time, Pallas kernels for 24%

profile of v4, /device:TPU:7, one launch (start us, length us, event | category | flops | bytes accessed | tf_op | source)
XLA Modules:
  0.0 180.1 jit_solution(12703462482332395572)
XLA Ops:
  0.6 3.2 %collective-permute-start.1 = (bf16[64,128,128]{2,1,0:T(8,128)(2,1)}, bf16[64,128,128]{2,1,0:T(8,128)(2,1)}, u32[]{:S(2)}, u32[]{:S(2)}) collective-permute-start(bf16[64,128,128]{2,1,0:T(8,128)(2,1)} %bitcast.rest_0_), channel_id=1, source_target_pairs={{4,0},{8,4},{12,8},{16,12},{20,16},{24,20},{28,24},{5,1},{9,5},{13... | collective-permute-start | bytes 6291464 | tf_op jit(solution)/shard_map/ppermute | solution.py:287
  3.8 0.1 collective-permute-start
  3.9 0.8 and_select_fusion.7
  4.7 0.8 and_select_fusion.8
  5.4 0.2 convert_reduce_fusion.2
  5.6 0.8 iota_add_fusion.1
  6.5 0.7 convert_reduce_fusion.4
  7.2 0.2 convert_reduce_fusion
  7.5 1.0 select_reduce_fusion
  8.4 0.7 select_reduce_fusion.3.order_ref
  9.1 3.2 %pack_inverses.1 = (bf16[32,128,128]{2,1,0:T(8,128)(2,1)}, bf16[32,128,128]{2,1,0:T(8,128)(2,1)}) custom-call(s32[64]{0:T(128)} %select_reduce_fusion.3.order_ref, bf16[64,128,128]{2,1,0:T(8,128)(2,1)} %tiles.3), custom_call_target="tpu_custom_call" | custom-call | bytes 8388608 | tf_op jit(solution)/shard_map/pack_inverses/pallas_call | solution.py:53
  12.3 6.9 %pack_send.1 = (bf16[128,128,128]{2,1,0:T(8,128)(2,1)}, bf16[128,128,128]{2,1,0:T(8,128)(2,1)}) custom-call(s32[512]{0:T(512)} %get-tuple-element.28.order_ref, bf16[512,128,128]{2,1,0:T(8,128)(2,1)} %tiles.5), custom_call_target="tpu_custom_call" | custom-call | bytes 33554432 | tf_op jit(solution)/shard_map/pack_send/pallas_call | solution.py:53
  19.2 1.0 collective-permute-start.7
  20.2 6.6 %all-to-all-start = ((bf16[32,128,128]{2,1,0:T(8,128)(2,1)}), bf16[32,128,128]{2,1,0:T(8,128)(2,1)}, u32[]{:S(2)}, u32[]{:S(2)}) async-start(bf16[32,128,128]{2,1,0:T(8,128)(2,1)} %get-tuple-element.26), calls=%async_computation | async-start | bytes 2097152 | tf_op jit(solution)/shard_map/all_to_all | solution.py:324
  26.8 0.4 collective-permute-start.4
  27.2 0.7 pad_add_fusion
  27.9 0.0 copy-start
  27.9 0.2 collective-permute-start.2
  28.1 5.9 %collective-permute-done.2 = s32[384]{0:T(512)S(1)} collective-permute-done((s32[384]{0:T(512)S(1)}, s32[384]{0:T(512)S(1)}, u32[]{:S(2)}, u32[]{:S(2)}) %collective-permute-start.2) | collective-permute-done | bytes 1568 | tf_op jit(solution)/shard_map/ppermute | solution.py:287
  34.0 0.4 collective-permute-start.5
  34.4 6.9 %pack_keep.1 = (bf16[128,128,128]{2,1,0:T(8,128)(2,1)}, bf16[128,128,128]{2,1,0:T(8,128)(2,1)}) custom-call(s32[512]{0:T(512)} %get-tuple-element.28.order_ref, bf16[512,128,128]{2,1,0:T(8,128)(2,1)} %tiles.5), custom_call_target="tpu_custom_call" | custom-call | bytes 33554432 | tf_op jit(solution)/shard_map/pack_keep/pallas_call | solution.py:53
  41.3 0.0 copy-done
  41.3 0.2 select_reduce_fusion.2
  41.5 0.2 convert_reduce_fusion.1
  41.7 0.5 multiply_add_fusion.places
  42.2 0.5 fusion.17
  42.8 0.5 slice.27
  43.2 1.9 %pad_add_fusion.1.bounds = s32[2]{0:T(128)} fusion(s32[1]{0:T(128)} %slice.27, s32[1]{0:T(128)} %bitcast.4), kind=kLoop, calls=%fused_computation.99 | loop fusion | flops 2 | bytes 16 | tf_op jit(solution)/shard_map/concatenate | solution.py:365
  45.1 0.5 fusion.16
  45.7 32.5 %all-to-all-done.rest_0_ = bf16[32,128,128]{2,1,0:T(8,128)(2,1)} async-done(((bf16[32,128,128]{2,1,0:T(8,128)(2,1)}), bf16[32,128,128]{2,1,0:T(8,128)(2,1)}, u32[]{:S(2)}, u32[]{:S(2)}) %all-to-all-start) | async-done | bytes 1048608 | tf_op jit(solution)/shard_map/all_to_all | solution.py:324
  78.1 0.0 collective-permute-done.1.rest_4_
  78.1 0.0 collective-permute-done.rest_2_
  78.1 0.9 collective-permute-start.8
  79.1 0.1 collective-permute-start.6
  79.1 0.0 collective-permute-done.5.rest_1_
  79.1 2.4 %collective-permute-start.3 = (bf16[64,128,128]{2,1,0:T(8,128)(2,1)}, bf16[64,128,128]{2,1,0:T(8,128)(2,1)}, u32[]{:S(2)}, u32[]{:S(2)}) collective-permute-start(bf16[64,128,128]{2,1,0:T(8,128)(2,1)} %collective-permute-done.rest_2_), channel_id=1, source_target_pairs={{0,4},{4,8},{8,12},{12,16},{16,20},{20,24},{24,28},{1,5},{5,9},{9,... | collective-permute-start | bytes 6291464 | tf_op jit(solution)/shard_map/ppermute | solution.py:287
  81.5 6.8 %all-to-all-start.1 = ((bf16[32,128,128]{2,1,0:T(8,128)(2,1)}), bf16[32,128,128]{2,1,0:T(8,128)(2,1)}, u32[]{:S(2)}, u32[]{:S(2)}) async-start(bf16[32,128,128]{2,1,0:T(8,128)(2,1)} %get-tuple-element.39), calls=%async_computation.1 | async-start | bytes 2097152 | tf_op jit(solution)/shard_map/all_to_all | solution.py:324
  88.3 0.0 collective-permute-done.7.recv
  88.3 0.0 collective-permute-done.8.rest_5_
  88.3 0.0 collective-permute-done.6.rest_3_
  88.3 13.0 %cross.1 = bf16[64,128,128]{2,1,0:T(8,128)(2,1)} custom-call(s32[128]{0:T(128)} %get-tuple-element.41.meta_keep, s32[128]{0:T(128)} %get-tuple-element.42.meta_recv, s32[2]{0:T(128)} %pad_add_fusion.1.bounds, bf16[128,128,128]{2,1,0:T(8,128)(2,1)} %get-tuple-element.43.keep, bf16[128,128,128]{2,1,0:T(8,128)(2,1)} %collective-permute-done.7.recv, ...), custom_call_target="tpu_custom_call" | custom-call | flops 1073741824 | bytes 25165824 | tf_op jit(solution)/shard_map/cross/pallas_call | solution.py:124
  101.3 0.4 collective-permute-start.9
  101.7 0.0 collective-permute-done.4.recv
  101.7 13.6 %own.1.early = f32[64,128,128]{2,1,0:T(8,128)} custom-call(s32[128]{0:T(128)} %get-tuple-element.32.meta_keep, s32[128]{0:T(128)} %get-tuple-element.33.meta_recv, s32[2]{0:T(128)} %pad_add_fusion.1.bounds, bf16[128,128,128]{2,1,0:T(8,128)(2,1)} %get-tuple-element.36.keep, bf16[128,128,128]{2,1,0:T(8,128)(2,1)} %collective-permute-done.4.recv, ...), custom_call_target="tpu_custom_call" | custom-call | flops 1073741824 | bytes 25165824 | tf_op jit(solution)/shard_map/own/pallas_call | solution.py:124
  115.3 44.0 %all-to-all-done.1.rest_1_ = bf16[32,128,128]{2,1,0:T(8,128)(2,1)} async-done(((bf16[32,128,128]{2,1,0:T(8,128)(2,1)}), bf16[32,128,128]{2,1,0:T(8,128)(2,1)}, u32[]{:S(2)}, u32[]{:S(2)}) %all-to-all-start.1) | async-done | bytes 1048608 | tf_op jit(solution)/shard_map/all_to_all | solution.py:324
  159.3 0.0 collective-permute-done.3.late
  159.3 0.0 collective-permute-start.10
  159.3 0.0 collective-permute-done.9.other
  159.3 4.5 %collective-permute-done.10.beside = bf16[64,128,128]{2,1,0:T(8,128)(2,1)} collective-permute-done((bf16[64,128,128]{2,1,0:T(8,128)(2,1)}, bf16[64,128,128]{2,1,0:T(8,128)(2,1)}, u32[]{:S(2)}, u32[]{:S(2)}) %collective-permute-start.10) | collective-permute-done | bytes 2097184 | tf_op jit(solution)/shard_map/ppermute | solution.py:287
  163.8 10.6 %near.1 = bf16[64,128,128]{2,1,0:T(8,128)(2,1)} custom-call(s32[128]{0:T(128)} %get-tuple-element.32.meta_keep, s32[128]{0:T(128)} %get-tuple-element.33.meta_recv, s32[2]{0:T(128)} %pad_add_fusion.1.bounds, f32[64,128,128]{2,1,0:T(8,128)} %own.1.early, bf16[64,128,128]{2,1,0:T(8,128)(2,1)} %collective-permute-done.9.other, ...), custom_call_target="tpu_custom_call" | custom-call | flops 536870912 | bytes 18874368 | tf_op jit(solution)/shard_map/near/pallas_call | solution.py:203
  174.4 5.7 %apply.1 = bf16[64,128,128]{2,1,0:T(8,128)(2,1)} custom-call(s32[64]{0:T(128)} %multiply_add_fusion.places, bf16[64,128,128]{2,1,0:T(8,128)(2,1)} %near.1, bf16[32,128,128]{2,1,0:T(8,128)(2,1)} %all-to-all-done.rest_0_, bf16[32,128,128]{2,1,0:T(8,128)(2,1)} %all-to-all-done.1.rest_1_), custom_call_target="tpu_custom_call" | custom-call | flops 268435456 | bytes 6291456 | tf_op jit(solution)/shard_map/apply/pallas_call | solution.py:245
  (6 shorter events, 0.1 us)
Async XLA Ops:
  0.6 77.5 %collective-permute-start.1 = (bf16[64,128,128]{2,1,0:T(8,128)(2,1)}, bf16[64,128,128]{2,1,0:T(8,128)(2,1)}, u32[]{:S(2)}, u32[]{:S(2)}) collective-permute-start(bf16[64,128,128]{2,1,0:T(8,128)(2,1)} %bitcast.rest_0_), channel_id=1, source_target_pairs={{4,0},{8,4},{12,8},{16,12},{20,16},{24,20},{28,24},{5,1},{9,5},{13... | collective-permute-start | bytes 6291464 | tf_op jit(solution)/shard_map/ppermute | solution.py:287
  3.8 74.4 %collective-permute-start = (bf16[64,128,128]{2,1,0:T(8,128)(2,1)}, bf16[64,128,128]{2,1,0:T(8,128)(2,1)}, u32[]{:S(2)}, u32[]{:S(2)}) collective-permute-start(bf16[64,128,128]{2,1,0:T(8,128)(2,1)} %bitcast.rest_0_), channel_id=1, source_target_pairs={{0,2},{1,3},{2,0},{3,1},{4,6},{5,7},{6,4},{7,5},{8,10},{9,11},{10,... | collective-permute-start | bytes 6291464 | tf_op jit(solution)/shard_map/ppermute | solution.py:287
  19.2 69.1 %collective-permute-start.7 = (bf16[128,128,128]{2,1,0:T(8,128)(2,1)}, bf16[128,128,128]{2,1,0:T(8,128)(2,1)}, u32[]{:S(2)}, u32[]{:S(2)}) collective-permute-start(bf16[128,128,128]{2,1,0:T(8,128)(2,1)} %get-tuple-element.44), channel_id=1, source_target_pairs={{0,1},{1,0},{2,3},{3,2},{4,5},{5,4},{6,7},{7,6},{8,9},{9,8},{10,11... | collective-permute-start | bytes 12582920 | tf_op jit(solution)/shard_map/ppermute | solution.py:287
  20.2 58.0 %all-to-all-start = ((bf16[32,128,128]{2,1,0:T(8,128)(2,1)}), bf16[32,128,128]{2,1,0:T(8,128)(2,1)}, u32[]{:S(2)}, u32[]{:S(2)}) async-start(bf16[32,128,128]{2,1,0:T(8,128)(2,1)} %get-tuple-element.26), calls=%async_computation | async-start | bytes 2097152 | tf_op jit(solution)/shard_map/all_to_all | solution.py:324
  26.8 74.9 %collective-permute-start.4 = (bf16[128,128,128]{2,1,0:T(8,128)(2,1)}, bf16[128,128,128]{2,1,0:T(8,128)(2,1)}, u32[]{:S(2)}, u32[]{:S(2)}) collective-permute-start(bf16[128,128,128]{2,1,0:T(8,128)(2,1)} %get-tuple-element.37), channel_id=1, source_target_pairs={{0,1},{1,0},{2,3},{3,2},{4,5},{5,4},{6,7},{7,6},{8,9},{9,8},{10,11... | collective-permute-start | bytes 12582920 | tf_op jit(solution)/shard_map/ppermute | solution.py:287
  27.9 13.3 %copy-start = (s32[2048]{0:T(1024)S(1)}, s32[2048]{0:T(1024)}, u32[]{:S(2)}) copy-start(s32[2048]{0:T(1024)} %param.9) | copy-start | bytes 24580
  27.9 6.0 %collective-permute-start.2 = (s32[384]{0:T(512)S(1)}, s32[384]{0:T(512)S(1)}, u32[]{:S(2)}, u32[]{:S(2)}) collective-permute-start(s32[384]{0:T(512)S(1)} %pad_add_fusion), channel_id=1, source_target_pairs={{0,1},{1,0},{2,3},{3,2},{4,5},{5,4},{6,7},{7,6},{8,9},{9,8},{10,11... | collective-permute-start | bytes 4616 | tf_op jit(solution)/shard_map/ppermute | solution.py:287
  34.0 45.1 %collective-permute-start.5 = (bf16[64,128,128]{2,1,0:T(8,128)(2,1)}, bf16[64,128,128]{2,1,0:T(8,128)(2,1)}, u32[]{:S(2)}, u32[]{:S(2)}) collective-permute-start(bf16[64,128,128]{2,1,0:T(8,128)(2,1)} %bitcast.rest_0_), channel_id=1, source_target_pairs={{0,1},{1,0},{2,3},{3,2},{4,5},{5,4},{6,7},{7,6},{8,9},{9,8},{10,11... | collective-permute-start | bytes 6291464 | tf_op jit(solution)/shard_map/ppermute | solution.py:287
  78.1 10.2 %collective-permute-start.8 = (bf16[64,128,128]{2,1,0:T(8,128)(2,1)}, bf16[64,128,128]{2,1,0:T(8,128)(2,1)}, u32[]{:S(2)}, u32[]{:S(2)}) collective-permute-start(bf16[64,128,128]{2,1,0:T(8,128)(2,1)} %collective-permute-done.1.rest_4_), channel_id=1, source_target_pairs={{0,1},{1,0},{2,3},{3,2},{4,5},{5,4},{6,7},{7,6},{8,9},{9,8},{10,11... | collective-permute-start | bytes 6291464 | tf_op jit(solution)/shard_map/ppermute | solution.py:287
  79.1 9.3 %collective-permute-start.6 = (bf16[64,128,128]{2,1,0:T(8,128)(2,1)}, bf16[64,128,128]{2,1,0:T(8,128)(2,1)}, u32[]{:S(2)}, u32[]{:S(2)}) collective-permute-start(bf16[64,128,128]{2,1,0:T(8,128)(2,1)} %collective-permute-done.rest_2_), channel_id=1, source_target_pairs={{0,1},{1,0},{2,3},{3,2},{4,5},{5,4},{6,7},{7,6},{8,9},{9,8},{10,11... | collective-permute-start | bytes 6291464 | tf_op jit(solution)/shard_map/ppermute | solution.py:287
  79.1 80.2 %collective-permute-start.3 = (bf16[64,128,128]{2,1,0:T(8,128)(2,1)}, bf16[64,128,128]{2,1,0:T(8,128)(2,1)}, u32[]{:S(2)}, u32[]{:S(2)}) collective-permute-start(bf16[64,128,128]{2,1,0:T(8,128)(2,1)} %collective-permute-done.rest_2_), channel_id=1, source_target_pairs={{0,4},{4,8},{8,12},{12,16},{16,20},{20,24},{24,28},{1,5},{5,9},{9,... | collective-permute-start | bytes 6291464 | tf_op jit(solution)/shard_map/ppermute | solution.py:287
  81.5 77.8 %all-to-all-start.1 = ((bf16[32,128,128]{2,1,0:T(8,128)(2,1)}), bf16[32,128,128]{2,1,0:T(8,128)(2,1)}, u32[]{:S(2)}, u32[]{:S(2)}) async-start(bf16[32,128,128]{2,1,0:T(8,128)(2,1)} %get-tuple-element.39), calls=%async_computation.1 | async-start | bytes 2097152 | tf_op jit(solution)/shard_map/all_to_all | solution.py:324
  101.3 58.0 %collective-permute-start.9 = (bf16[64,128,128]{2,1,0:T(8,128)(2,1)}, bf16[64,128,128]{2,1,0:T(8,128)(2,1)}, u32[]{:S(2)}, u32[]{:S(2)}) collective-permute-start(bf16[64,128,128]{2,1,0:T(8,128)(2,1)} %cross.1), channel_id=1, source_target_pairs={{0,2},{1,3},{2,0},{3,1},{4,6},{5,7},{6,4},{7,5},{8,10},{9,11},{10,... | collective-permute-start | bytes 6291464 | tf_op jit(solution)/shard_map/ppermute | solution.py:287
  159.3 4.5 %collective-permute-start.10 = (bf16[64,128,128]{2,1,0:T(8,128)(2,1)}, bf16[64,128,128]{2,1,0:T(8,128)(2,1)}, u32[]{:S(2)}, u32[]{:S(2)}) collective-permute-start(bf16[64,128,128]{2,1,0:T(8,128)(2,1)} %collective-permute-done.3.late), channel_id=1, source_target_pairs={{0,1},{1,0},{2,3},{3,2},{4,5},{5,4},{6,7},{7,6},{8,9},{9,8},{10,11... | collective-permute-start | bytes 6291464 | tf_op jit(solution)/shard_map/ppermute | solution.py:287

commit v5 on v4

--- a/solution.py
+++ b/solution.py
@@ -313,17 +313,16 @@
     capacity = -(-own // devices)
     local = jnp.arange(own, dtype=jnp.int32)
     source = pick(slot_cluster, myself * own + local) // own
-    places = ranks_by(source, local) * devices + source
+    places = source * capacity + ranks_by(source, local)
     held = lax.dynamic_slice_in_dim(slot_cluster, myself * own, own, 0)
     target = held // own
-    place_held = ranks_by(target, held % own) * devices + target
+    place_held = target * capacity + ranks_by(target, held % own)
     outbox_order = pick(place_held, jnp.arange(devices * capacity, dtype=jnp.int32))
-    outbox = gather_tiles(outbox_order, inverses, 0, capacity, devices, "pack_inverses")
+    outbox = gather_tiles(outbox_order, inverses, 0, 1, devices * capacity, "pack_inverses")
 
     def exchange(value):
         return lax.all_to_all(value, AXES, split_axis=0, concat_axis=0, tiled=True)
 
-    inbox = [exchange(outbox[0])]
 
     group = own * cols
     base = row * group
@@ -371,7 +370,6 @@
     (
         other_chip,
         halo_early,
-        inbox,
         keep_cross,
         keep_own,
         outbox,
@@ -385,7 +383,6 @@
         (
             other_chip,
             halo_early,
-            inbox,
             keep_cross,
             keep_own,
             outbox,
@@ -401,7 +398,7 @@
     other_beside = permute(other_chip, beside)
     halo_late = permute(other_chip, late)
     early_beside = permute(halo_early, beside)
-    inbox += [exchange(part) for part in outbox[1:]]
+    inbox = [exchange(part) for part in outbox]
     group_pieces = (blocks, own_beside, other_chip, other_beside)
     cross = sums(
         bits,
@@ -428,7 +425,7 @@
         group_pieces,
         "own",
     )
-    halo_late, early_sums, inbox = lax.optimization_barrier((halo_late, early_sums, inbox))
+    halo_late, early_sums = lax.optimization_barrier((halo_late, early_sums))
     late_beside = permute(halo_late, beside)
     near = near_sums(
         bits,

time: 182 us -> 169 us (0.929)
  waiting for transfers between devices: 86.9 us -> 77.4 us
  starting transfers between devices: 22.3 us -> 19.7 us
    all_to_all x2 -> x1, waiting for transfers between devices: 76.5 us -> 19.9 us  [exchange(): return lax.all_to_all(value, AXES, split_axis=0, concat_axis=0, tiled=True)]
    ppermute x11, waiting for transfers between devices: 10.4 us -> 57.4 us  [permute(): return lax.ppermute(value, AXES, pairs)]
    all_to_all x2 -> x1, starting transfers between devices: 13.4 us -> 6.66 us  [exchange(): return lax.all_to_all(value, AXES, split_axis=0, concat_axis=0, tiled=True)]
    ppermute x11, starting transfers between devices: 8.91 us -> 13 us  [permute(): return lax.ppermute(value, AXES, pairs)]
  transfers between devices with their start and end apart: 13 -> 12, of which waited for: 4 -> 6; matrix products, arithmetic and copies ran while one was open for 6% -> 6% of each run, Pallas kernels for 24% -> 33%
where the time goes in v5:
time: 169 us; the launch traced here: 168 us
  waiting for transfers between devices  77.4 us (46%)
  Pallas kernels  60.2 us (36%)
  starting transfers between devices  19.7 us (12%)
  other arithmetic  7.96 us (5%)
    ppermute x11, waiting for transfers between devices, permute(): return lax.ppermute(value, AXES, pairs)  57.4 us
    pallas_call x2, Pallas kernels, sums(): pl.pallas_call(functools.partial(sums_kernel, bits, whole), out_shape=jax...  26.8 us
    all_to_all x1, waiting for transfers between devices, exchange(): return lax.all_to_all(value, AXES, split_axis=0, concat_axis=0, tiled=True)  19.9 us
    pallas_call x3, Pallas kernels, gather_tiles(): pl.pallas_call(functools.partial(gather_kernel, first), out_shape=(jax.Sh...  17.3 us
    ppermute x11, starting transfers between devices, permute(): return lax.ppermute(value, AXES, pairs)  13 us
    pallas_call x1, Pallas kernels, near_sums(): pl.pallas_call(functools.partial(near_kernel, bits), out_shape=jax.ShapeD...  10.4 us
    all_to_all x1, starting transfers between devices, exchange(): return lax.all_to_all(value, AXES, split_axis=0, concat_axis=0, tiled=True)  6.66 us
    pallas_call x1, Pallas kernels, apply_inverses(): pl.pallas_call(apply_kernel, out_shape=jax.ShapeDtypeStruct(near.shape, j...  5.69 us
  transfers between devices with their start and end apart: 12, of which 6 were waited for; matrix products, arithmetic and copies ran while one was open for 6% of the time, Pallas kernels for 33%

profile of v5, /device:TPU:7, one launch (start us, length us, event | category | flops | bytes accessed | tf_op | source)
XLA Modules:
  0.0 167.7 jit_solution(10959848182894581910)
XLA Ops:
  0.6 3.2 %collective-permute-start.1 = (bf16[64,128,128]{2,1,0:T(8,128)(2,1)}, bf16[64,128,128]{2,1,0:T(8,128)(2,1)}, u32[]{:S(2)}, u32[]{:S(2)}) collective-permute-start(bf16[64,128,128]{2,1,0:T(8,128)(2,1)} %bitcast.8), channel_id=1, source_target_pairs={{4,0},{8,4},{12,8},{16,12},{20,16},{24,20},{28,24},{5,1},{9,5},{13... | collective-permute-start | bytes 6291464 | tf_op jit(solution)/shard_map/ppermute | solution.py:287
  3.8 0.1 collective-permute-start
  3.9 0.8 and_select_fusion.8
  4.7 0.2 convert_reduce_fusion.2
  4.9 0.8 iota_add_fusion.1
  5.7 0.7 convert_reduce_fusion.4
  6.5 0.2 convert_reduce_fusion
  6.7 0.9 select_reduce_fusion
  7.7 0.7 select_reduce_fusion.3.order_ref
  8.3 3.6 %pack_inverses.1 = bf16[64,128,128]{2,1,0:T(8,128)(2,1)} custom-call(s32[64]{0:T(128)} %select_reduce_fusion.3.order_ref, bf16[64,128,128]{2,1,0:T(8,128)(2,1)} %tiles.3), custom_call_target="tpu_custom_call" | custom-call | bytes 8388608 | tf_op jit(solution)/shard_map/pack_inverses/pallas_call | solution.py:53
  11.9 6.9 %pack_send.1 = (bf16[128,128,128]{2,1,0:T(8,128)(2,1)}, bf16[128,128,128]{2,1,0:T(8,128)(2,1)}) custom-call(s32[512]{0:T(512)} %get-tuple-element.21.order_ref, bf16[512,128,128]{2,1,0:T(8,128)(2,1)} %tiles.5), custom_call_target="tpu_custom_call" | custom-call | bytes 33554432 | tf_op jit(solution)/shard_map/pack_send/pallas_call | solution.py:53
  18.8 1.0 collective-permute-start.7
  19.8 0.1 collective-permute-start.4
  19.9 0.7 pad_add_fusion
  20.6 0.0 copy-start
  20.6 0.4 collective-permute-start.2
  21.1 5.5 %collective-permute-done.2 = s32[384]{0:T(512)S(1)} collective-permute-done((s32[384]{0:T(512)S(1)}, s32[384]{0:T(512)S(1)}, u32[]{:S(2)}, u32[]{:S(2)}) %collective-permute-start.2) | collective-permute-done | bytes 1568 | tf_op jit(solution)/shard_map/ppermute | solution.py:287
  26.6 0.4 collective-permute-start.5
  26.9 6.9 %pack_keep.1 = (bf16[128,128,128]{2,1,0:T(8,128)(2,1)}, bf16[128,128,128]{2,1,0:T(8,128)(2,1)}) custom-call(s32[512]{0:T(512)} %get-tuple-element.21.order_ref, bf16[512,128,128]{2,1,0:T(8,128)(2,1)} %tiles.5), custom_call_target="tpu_custom_call" | custom-call | bytes 33554432 | tf_op jit(solution)/shard_map/pack_keep/pallas_call | solution.py:53
  33.9 0.0 copy-done
  33.9 0.2 select_reduce_fusion.2
  34.1 0.2 convert_reduce_fusion.1
  34.3 0.5 multiply_add_fusion.places
  34.8 0.6 fusion.17
  35.4 0.5 slice.27
  35.9 1.9 %pad_add_fusion.1.bounds = s32[2]{0:T(128)} fusion(s32[1]{0:T(128)} %slice.27, s32[1]{0:T(128)} %bitcast.4), kind=kLoop, calls=%fused_computation.99 | loop fusion | flops 2 | bytes 16 | tf_op jit(solution)/shard_map/concatenate | solution.py:364
  37.8 0.6 fusion.16
  38.4 11.0 %collective-permute-done.1.rest_4_ = bf16[64,128,128]{2,1,0:T(8,128)(2,1)} collective-permute-done((bf16[64,128,128]{2,1,0:T(8,128)(2,1)}, bf16[64,128,128]{2,1,0:T(8,128)(2,1)}, u32[]{:S(2)}, u32[]{:S(2)}) %collective-permute-start.1) | collective-permute-done | bytes 2097184 | tf_op jit(solution)/shard_map/ppermute | solution.py:287
  49.3 1.0 collective-permute-done.rest_2_
  50.3 1.9 %collective-permute-start.8 = (bf16[64,128,128]{2,1,0:T(8,128)(2,1)}, bf16[64,128,128]{2,1,0:T(8,128)(2,1)}, u32[]{:S(2)}, u32[]{:S(2)}) collective-permute-start(bf16[64,128,128]{2,1,0:T(8,128)(2,1)} %collective-permute-done.1.rest_4_), channel_id=1, source_target_pairs={{0,1},{1,0},{2,3},{3,2},{4,5},{5,4},{6,7},{7,6},{8,9},{9,8},{10,11... | collective-permute-start | bytes 6291464 | tf_op jit(solution)/shard_map/ppermute | solution.py:287
  52.2 0.0 collective-permute-start.6
  52.2 0.0 collective-permute-done.5.rest_1_
  52.2 3.4 %collective-permute-start.3 = (bf16[64,128,128]{2,1,0:T(8,128)(2,1)}, bf16[64,128,128]{2,1,0:T(8,128)(2,1)}, u32[]{:S(2)}, u32[]{:S(2)}) collective-permute-start(bf16[64,128,128]{2,1,0:T(8,128)(2,1)} %collective-permute-done.rest_2_), channel_id=1, source_target_pairs={{0,4},{4,8},{8,12},{12,16},{16,20},{20,24},{24,28},{1,5},{5,9},{9,... | collective-permute-start | bytes 6291464 | tf_op jit(solution)/shard_map/ppermute | solution.py:287
  55.6 6.7 %all-to-all-start = ((bf16[64,128,128]{2,1,0:T(8,128)(2,1)}), bf16[64,128,128]{2,1,0:T(8,128)(2,1)}, u32[]{:S(2)}, u32[]{:S(2)}) async-start(bf16[64,128,128]{2,1,0:T(8,128)(2,1)} %pack_inverses.1), calls=%async_computation | async-start | bytes 4194304 | tf_op jit(solution)/shard_map/all_to_all | solution.py:324
  62.3 0.0 collective-permute-done.7.recv
  62.3 0.0 collective-permute-done.8.rest_5_
  62.3 0.0 collective-permute-done.6.rest_3_
  62.3 13.0 %cross.1 = bf16[64,128,128]{2,1,0:T(8,128)(2,1)} custom-call(s32[128]{0:T(128)} %get-tuple-element.32.meta_keep, s32[128]{0:T(128)} %get-tuple-element.33.meta_recv, s32[2]{0:T(128)} %pad_add_fusion.1.bounds, bf16[128,128,128]{2,1,0:T(8,128)(2,1)} %get-tuple-element.34.keep, bf16[128,128,128]{2,1,0:T(8,128)(2,1)} %collective-permute-done.7.recv, ...), custom_call_target="tpu_custom_call" | custom-call | flops 1073741824 | bytes 25165824 | tf_op jit(solution)/shard_map/cross/pallas_call | solution.py:124
  75.3 0.3 collective-permute-start.9
  75.7 0.0 collective-permute-done.4.recv
  75.7 13.8 %own.1.early = f32[64,128,128]{2,1,0:T(8,128)} custom-call(s32[128]{0:T(128)} %get-tuple-element.25.meta_keep, s32[128]{0:T(128)} %get-tuple-element.26.meta_recv, s32[2]{0:T(128)} %pad_add_fusion.1.bounds, bf16[128,128,128]{2,1,0:T(8,128)(2,1)} %get-tuple-element.29.keep, bf16[128,128,128]{2,1,0:T(8,128)(2,1)} %collective-permute-done.4.recv, ...), custom_call_target="tpu_custom_call" | custom-call | flops 1073741824 | bytes 25165824 | tf_op jit(solution)/shard_map/own/pallas_call | solution.py:124
  89.5 30.6 %collective-permute-done.3.late = bf16[64,128,128]{2,1,0:T(8,128)(2,1)} collective-permute-done((bf16[64,128,128]{2,1,0:T(8,128)(2,1)}, bf16[64,128,128]{2,1,0:T(8,128)(2,1)}, u32[]{:S(2)}, u32[]{:S(2)}) %collective-permute-start.3) | collective-permute-done | bytes 2097184 | tf_op jit(solution)/shard_map/ppermute | solution.py:287
  120.0 2.3 %collective-permute-start.10 = (bf16[64,128,128]{2,1,0:T(8,128)(2,1)}, bf16[64,128,128]{2,1,0:T(8,128)(2,1)}, u32[]{:S(2)}, u32[]{:S(2)}) collective-permute-start(bf16[64,128,128]{2,1,0:T(8,128)(2,1)} %collective-permute-done.3.late), channel_id=1, source_target_pairs={{0,1},{1,0},{2,3},{3,2},{4,5},{5,4},{6,7},{7,6},{8,9},{9,8},{10,11... | collective-permute-start | bytes 6291464 | tf_op jit(solution)/shard_map/ppermute | solution.py:287
  122.4 9.3 %collective-permute-done.9.other = bf16[64,128,128]{2,1,0:T(8,128)(2,1)} collective-permute-done((bf16[64,128,128]{2,1,0:T(8,128)(2,1)}, bf16[64,128,128]{2,1,0:T(8,128)(2,1)}, u32[]{:S(2)}, u32[]{:S(2)}) %collective-permute-start.9) | collective-permute-done | bytes 2097184 | tf_op jit(solution)/shard_map/ppermute | solution.py:287
  131.7 0.0 collective-permute-done.10.beside
  131.7 10.4 %near.1 = bf16[64,128,128]{2,1,0:T(8,128)(2,1)} custom-call(s32[128]{0:T(128)} %get-tuple-element.25.meta_keep, s32[128]{0:T(128)} %get-tuple-element.26.meta_recv, s32[2]{0:T(128)} %pad_add_fusion.1.bounds, f32[64,128,128]{2,1,0:T(8,128)} %own.1.early, bf16[64,128,128]{2,1,0:T(8,128)(2,1)} %collective-permute-done.9.other, ...), custom_call_target="tpu_custom_call" | custom-call | flops 536870912 | bytes 18874368 | tf_op jit(solution)/shard_map/near/pallas_call | solution.py:203
  142.1 19.9 %all-to-all-done.rest_0_ = bf16[64,128,128]{2,1,0:T(8,128)(2,1)} async-done(((bf16[64,128,128]{2,1,0:T(8,128)(2,1)}), bf16[64,128,128]{2,1,0:T(8,128)(2,1)}, u32[]{:S(2)}, u32[]{:S(2)}) %all-to-all-start) | async-done | bytes 2097184 | tf_op jit(solution)/shard_map/all_to_all | solution.py:324
  162.0 5.7 %apply.1 = bf16[64,128,128]{2,1,0:T(8,128)(2,1)} custom-call(s32[64]{0:T(128)} %multiply_add_fusion.places, bf16[64,128,128]{2,1,0:T(8,128)(2,1)} %near.1, bf16[64,128,128]{2,1,0:T(8,128)(2,1)} %all-to-all-done.rest_0_), custom_call_target="tpu_custom_call" | custom-call | flops 268435456 | bytes 6291456 | tf_op jit(solution)/shard_map/apply/pallas_call | solution.py:245
  (7 shorter events, 0.1 us)
Async XLA Ops:
  0.6 48.7 %collective-permute-start.1 = (bf16[64,128,128]{2,1,0:T(8,128)(2,1)}, bf16[64,128,128]{2,1,0:T(8,128)(2,1)}, u32[]{:S(2)}, u32[]{:S(2)}) collective-permute-start(bf16[64,128,128]{2,1,0:T(8,128)(2,1)} %bitcast.8), channel_id=1, source_target_pairs={{4,0},{8,4},{12,8},{16,12},{20,16},{24,20},{28,24},{5,1},{9,5},{13... | collective-permute-start | bytes 6291464 | tf_op jit(solution)/shard_map/ppermute | solution.py:287
  3.8 46.6 %collective-permute-start = (bf16[64,128,128]{2,1,0:T(8,128)(2,1)}, bf16[64,128,128]{2,1,0:T(8,128)(2,1)}, u32[]{:S(2)}, u32[]{:S(2)}) collective-permute-start(bf16[64,128,128]{2,1,0:T(8,128)(2,1)} %bitcast.9), channel_id=1, source_target_pairs={{0,2},{1,3},{2,0},{3,1},{4,6},{5,7},{6,4},{7,5},{8,10},{9,11},{10,... | collective-permute-start | bytes 6291464 | tf_op jit(solution)/shard_map/ppermute | solution.py:287
  18.8 43.5 %collective-permute-start.7 = (bf16[128,128,128]{2,1,0:T(8,128)(2,1)}, bf16[128,128,128]{2,1,0:T(8,128)(2,1)}, u32[]{:S(2)}, u32[]{:S(2)}) collective-permute-start(bf16[128,128,128]{2,1,0:T(8,128)(2,1)} %get-tuple-element.35), channel_id=1, source_target_pairs={{0,1},{1,0},{2,3},{3,2},{4,5},{5,4},{6,7},{7,6},{8,9},{9,8},{10,11... | collective-permute-start | bytes 12582920 | tf_op jit(solution)/shard_map/ppermute | solution.py:287
  19.8 55.9 %collective-permute-start.4 = (bf16[128,128,128]{2,1,0:T(8,128)(2,1)}, bf16[128,128,128]{2,1,0:T(8,128)(2,1)}, u32[]{:S(2)}, u32[]{:S(2)}) collective-permute-start(bf16[128,128,128]{2,1,0:T(8,128)(2,1)} %get-tuple-element.30), channel_id=1, source_target_pairs={{0,1},{1,0},{2,3},{3,2},{4,5},{5,4},{6,7},{7,6},{8,9},{9,8},{10,11... | collective-permute-start | bytes 12582920 | tf_op jit(solution)/shard_map/ppermute | solution.py:287
  20.6 13.3 %copy-start = (s32[2048]{0:T(1024)S(1)}, s32[2048]{0:T(1024)}, u32[]{:S(2)}) copy-start(s32[2048]{0:T(1024)} %param.9) | copy-start | bytes 24580
  20.6 6.0 %collective-permute-start.2 = (s32[384]{0:T(512)S(1)}, s32[384]{0:T(512)S(1)}, u32[]{:S(2)}, u32[]{:S(2)}) collective-permute-start(s32[384]{0:T(512)S(1)} %pad_add_fusion), channel_id=1, source_target_pairs={{0,1},{1,0},{2,3},{3,2},{4,5},{5,4},{6,7},{7,6},{8,9},{9,8},{10,11... | collective-permute-start | bytes 4616 | tf_op jit(solution)/shard_map/ppermute | solution.py:287
  26.6 25.6 %collective-permute-start.5 = (bf16[64,128,128]{2,1,0:T(8,128)(2,1)}, bf16[64,128,128]{2,1,0:T(8,128)(2,1)}, u32[]{:S(2)}, u32[]{:S(2)}) collective-permute-start(bf16[64,128,128]{2,1,0:T(8,128)(2,1)} %bitcast.10), channel_id=1, source_target_pairs={{0,1},{1,0},{2,3},{3,2},{4,5},{5,4},{6,7},{7,6},{8,9},{9,8},{10,11... | collective-permute-start | bytes 6291464 | tf_op jit(solution)/shard_map/ppermute | solution.py:287
  50.3 11.9 %collective-permute-start.8 = (bf16[64,128,128]{2,1,0:T(8,128)(2,1)}, bf16[64,128,128]{2,1,0:T(8,128)(2,1)}, u32[]{:S(2)}, u32[]{:S(2)}) collective-permute-start(bf16[64,128,128]{2,1,0:T(8,128)(2,1)} %collective-permute-done.1.rest_4_), channel_id=1, source_target_pairs={{0,1},{1,0},{2,3},{3,2},{4,5},{5,4},{6,7},{7,6},{8,9},{9,8},{10,11... | collective-permute-start | bytes 6291464 | tf_op jit(solution)/shard_map/ppermute | solution.py:287
  52.2 10.1 %collective-permute-start.6 = (bf16[64,128,128]{2,1,0:T(8,128)(2,1)}, bf16[64,128,128]{2,1,0:T(8,128)(2,1)}, u32[]{:S(2)}, u32[]{:S(2)}) collective-permute-start(bf16[64,128,128]{2,1,0:T(8,128)(2,1)} %collective-permute-done.rest_2_), channel_id=1, source_target_pairs={{0,1},{1,0},{2,3},{3,2},{4,5},{5,4},{6,7},{7,6},{8,9},{9,8},{10,11... | collective-permute-start | bytes 6291464 | tf_op jit(solution)/shard_map/ppermute | solution.py:287
  52.2 67.8 %collective-permute-start.3 = (bf16[64,128,128]{2,1,0:T(8,128)(2,1)}, bf16[64,128,128]{2,1,0:T(8,128)(2,1)}, u32[]{:S(2)}, u32[]{:S(2)}) collective-permute-start(bf16[64,128,128]{2,1,0:T(8,128)(2,1)} %collective-permute-done.rest_2_), channel_id=1, source_target_pairs={{0,4},{4,8},{8,12},{12,16},{16,20},{20,24},{24,28},{1,5},{5,9},{9,... | collective-permute-start | bytes 6291464 | tf_op jit(solution)/shard_map/ppermute | solution.py:287
  55.6 106.4 %all-to-all-start = ((bf16[64,128,128]{2,1,0:T(8,128)(2,1)}), bf16[64,128,128]{2,1,0:T(8,128)(2,1)}, u32[]{:S(2)}, u32[]{:S(2)}) async-start(bf16[64,128,128]{2,1,0:T(8,128)(2,1)} %pack_inverses.1), calls=%async_computation | async-start | bytes 4194304 | tf_op jit(solution)/shard_map/all_to_all | solution.py:324
  75.3 56.4 %collective-permute-start.9 = (bf16[64,128,128]{2,1,0:T(8,128)(2,1)}, bf16[64,128,128]{2,1,0:T(8,128)(2,1)}, u32[]{:S(2)}, u32[]{:S(2)}) collective-permute-start(bf16[64,128,128]{2,1,0:T(8,128)(2,1)} %cross.1), channel_id=1, source_target_pairs={{0,2},{1,3},{2,0},{3,1},{4,6},{5,7},{6,4},{7,5},{8,10},{9,11},{10,... | collective-permute-start | bytes 6291464 | tf_op jit(solution)/shard_map/ppermute | solution.py:287
  120.0 11.7 %collective-permute-start.10 = (bf16[64,128,128]{2,1,0:T(8,128)(2,1)}, bf16[64,128,128]{2,1,0:T(8,128)(2,1)}, u32[]{:S(2)}, u32[]{:S(2)}) collective-permute-start(bf16[64,128,128]{2,1,0:T(8,128)(2,1)} %collective-permute-done.3.late), channel_id=1, source_target_pairs={{0,1},{1,0},{2,3},{3,2},{4,5},{5,4},{6,7},{7,6},{8,9},{9,8},{10,11... | collective-permute-start | bytes 6291464 | tf_op jit(solution)/shard_map/ppermute | solution.py:287

commit v6 on v5

--- a/solution.py
+++ b/solution.py
@@ -139,16 +139,19 @@
     )(meta_keep, meta_recv, bounds, keep, recv, *pieces)
 
 
-def near_kernel(bits, meta_keep, meta_recv, bounds, early, other, keep, recv, late, beside, *rest):
-    near, acc, sent, band, mine, theirs, sem = rest
+def near_kernel(bits, meta_keep, meta_recv, bounds, early, other, keep, recv, *rest):
+    pieces, (near, acc, sent, band, mine, theirs, sem) = rest[:-7], rest[-7:]
     count = keep.shape[0]
-    size = late.shape[0]
+    size = acc.shape[0]
     loads = [
         pltpu.make_async_copy(early, acc, sem.at[0]),
-        pltpu.make_async_copy(late, band.at[pl.ds(0, size)], sem.at[2]),
-        pltpu.make_async_copy(beside, band.at[pl.ds(size, size)], sem.at[3]),
         pltpu.make_async_copy(other, sent, sem.at[1]),
     ]
+    place = 0
+    for order, piece in enumerate(pieces):
+        part = band.at[pl.ds(place, piece.shape[0])]
+        loads.append(pltpu.make_async_copy(piece, part, sem.at[4 + order]))
+        place += piece.shape[0]
     for load in loads:
         load.start()
     sides = ((meta_keep, keep, mine), (meta_recv, recv, theirs))
@@ -157,7 +160,7 @@
         start = pl.multiple_of(chunk * CHUNK, CHUNK)
         piece = pl.ds(start, CHUNK)
         return pltpu.make_async_copy(
-            sides[side][1].at[piece], sides[side][2].at[piece], sem.at[4 + side]
+            sides[side][1].at[piece], sides[side][2].at[piece], sem.at[2 + side]
         )
 
     for side in (0, 1):
@@ -197,13 +200,13 @@
     near[...] = (acc[...] + sent[...].astype(jnp.float32)).astype(jnp.bfloat16)
 
 
-def near_sums(bits, meta_keep, meta_recv, bounds, early, other, keep, recv, late, beside):
-    block = late.shape
+def near_sums(bits, meta_keep, meta_recv, bounds, early, other, keep, recv, pieces):
+    block = early.shape
     held = pltpu.VMEM(keep.shape, keep.dtype)
     return pl.pallas_call(
         functools.partial(near_kernel, bits),
         out_shape=jax.ShapeDtypeStruct(block, jnp.bfloat16),
-        in_specs=[SMEM] * 3 + [HBM] * 6,
+        in_specs=[SMEM] * 3 + [HBM] * (4 + len(pieces)),
         out_specs=VMEM,
         scratch_shapes=[
             pltpu.VMEM(block, jnp.float32),
@@ -211,12 +214,12 @@
             pltpu.VMEM((2 * block[0],) + block[1:], jnp.bfloat16),
             held,
             held,
-            pltpu.SemaphoreType.DMA((6,)),
+            pltpu.SemaphoreType.DMA((4 + len(pieces),)),
         ],
         compiler_params=params(63),
         cost_estimate=cost(2 * keep.size * block[2], 18),
         name="near",
-    )(meta_keep, meta_recv, bounds, early, other, keep, recv, late, beside)
+    )(meta_keep, meta_recv, bounds, early, other, keep, recv, *pieces)
 
 
 def apply_kernel(places, near, *rest):
@@ -396,7 +399,9 @@
     )
 
     other_beside = permute(other_chip, beside)
-    halo_late = permute(other_chip, late)
+    cut = own - own // 4
+    halo_late = permute(other_chip[:cut], late)
+    halo_across = permute(halo_early[cut:], across)
     early_beside = permute(halo_early, beside)
     inbox = [exchange(part) for part in outbox]
     group_pieces = (blocks, own_beside, other_chip, other_beside)
@@ -413,6 +418,7 @@
         "cross",
     )
     other_sums = permute(cross, across)
+    own_keep, halo_across = lax.optimization_barrier((own_keep, halo_across))
     early_sums = sums(
         bits,
         False,
@@ -427,6 +433,7 @@
     )
     halo_late, early_sums = lax.optimization_barrier((halo_late, early_sums))
     late_beside = permute(halo_late, beside)
+    across_beside = permute(halo_across, beside)
     near = near_sums(
         bits,
         own_keep,
@@ -436,8 +443,7 @@
         other_sums,
         keep_own,
         recv_own,
-        halo_late,
-        late_beside,
+        (halo_late, halo_across, late_beside, across_beside),
     )
     result = apply_inverses(places, near, inbox)
     return near.reshape(own * size, columns), result.reshape(own * size, columns)

time: 169 us -> 161 us (0.953)
  the two profiles are of different devices: /device:TPU:7 before, /device:TPU:15 now
where the time goes in v6:
time: 161 us; the launch traced here: 160 us
  waiting for transfers between devices  65.8 us (41%)
  Pallas kernels  60.4 us (38%)
  starting transfers between devices  18.3 us (11%)
  other arithmetic  7.9 us (5%)
  local copies, waits for them, and re-layouts  7.14 us (4%)
    ppermute x13, waiting for transfers between devices, permute(): return lax.ppermute(value, AXES, pairs)  65.8 us
    pallas_call x2, Pallas kernels, sums(): pl.pallas_call(functools.partial(sums_kernel, bits, whole), out_shape=jax...  26.4 us
    pallas_call x3, Pallas kernels, gather_tiles(): pl.pallas_call(functools.partial(gather_kernel, first), out_shape=(jax.Sh...  17.5 us
    ppermute x13, starting transfers between devices, permute(): return lax.ppermute(value, AXES, pairs)  12.1 us
    pallas_call x1, Pallas kernels, near_sums(): pl.pallas_call(functools.partial(near_kernel, bits), out_shape=jax.ShapeD...  10.8 us
    all_to_all x1, starting transfers between devices, exchange(): return lax.all_to_all(value, AXES, split_axis=0, concat_axis=0, tiled=True)  6.16 us
    pallas_call x1, Pallas kernels, apply_inverses(): pl.pallas_call(apply_kernel, out_shape=jax.ShapeDtypeStruct(near.shape, j...  5.7 us
  transfers between devices with their start and end apart: 14, of which 6 were waited for; matrix products, arithmetic and copies ran while one was open for 9% of the time, Pallas kernels for 34%

profile of v6, /device:TPU:15, one launch (start us, length us, event | category | flops | bytes accessed | tf_op | source)
XLA Modules:
  0.0 160.2 jit_solution(9567073000277220485)
XLA Ops:
  0.6 0.3 collective-permute-start
  0.9 3.1 %collective-permute-start.1 = (bf16[64,128,128]{2,1,0:T(8,128)(2,1)}, bf16[64,128,128]{2,1,0:T(8,128)(2,1)}, u32[]{:S(2)}, u32[]{:S(2)}) collective-permute-start(bf16[64,128,128]{2,1,0:T(8,128)(2,1)} %bitcast.9), channel_id=1, source_target_pairs={{4,0},{8,4},{12,8},{16,12},{20,16},{24,20},{28,24},{5,1},{9,5},{13... | collective-permute-start | bytes 6291464 | tf_op jit(solution)/shard_map/ppermute | solution.py:290
  4.1 0.8 and_select_fusion.8
  4.9 0.2 convert_reduce_fusion.2
  5.1 0.6 select_reduce_fusion.3.order_ref
  5.7 0.8 iota_add_fusion.1
  6.5 0.7 convert_reduce_fusion.4
  7.3 0.2 convert_reduce_fusion
  7.5 0.9 select_reduce_fusion
  8.5 3.6 %pack_inverses.1 = bf16[64,128,128]{2,1,0:T(8,128)(2,1)} custom-call(s32[64]{0:T(128)} %select_reduce_fusion.3.order_ref, bf16[64,128,128]{2,1,0:T(8,128)(2,1)} %tiles.3), custom_call_target="tpu_custom_call" | custom-call | bytes 8388608 | tf_op jit(solution)/shard_map/pack_inverses/pallas_call | solution.py:53
  12.0 0.0 copy-start.2
  12.1 7.0 %pack_send.1 = (bf16[128,128,128]{2,1,0:T(8,128)(2,1)}, bf16[128,128,128]{2,1,0:T(8,128)(2,1)}) custom-call(s32[512]{0:T(512)} %get-tuple-element.23.order_ref, bf16[512,128,128]{2,1,0:T(8,128)(2,1)} %tiles.5), custom_call_target="tpu_custom_call" | custom-call | bytes 33554432 | tf_op jit(solution)/shard_map/pack_send/pallas_call | solution.py:53
  19.1 1.3 collective-permute-start.8
  20.4 0.1 collective-permute-start.5
  20.4 0.7 pad_add_fusion
  21.1 0.4 collective-permute-start.2
  21.6 0.0 copy-done.2
  21.6 0.2 select_reduce_fusion.2
  21.8 5.4 %collective-permute-done.2 = s32[384]{0:T(512)S(1)} collective-permute-done((s32[384]{0:T(512)S(1)}, s32[384]{0:T(512)S(1)}, u32[]{:S(2)}, u32[]{:S(2)}) %collective-permute-start.2) | collective-permute-done | bytes 1568 | tf_op jit(solution)/shard_map/ppermute | solution.py:290
  27.2 0.4 collective-permute-start.6
  27.5 6.9 %pack_keep.1 = (bf16[128,128,128]{2,1,0:T(8,128)(2,1)}, bf16[128,128,128]{2,1,0:T(8,128)(2,1)}) custom-call(s32[512]{0:T(512)} %get-tuple-element.23.order_ref, bf16[512,128,128]{2,1,0:T(8,128)(2,1)} %tiles.5), custom_call_target="tpu_custom_call" | custom-call | bytes 33554432 | tf_op jit(solution)/shard_map/pack_keep/pallas_call | solution.py:53
  34.4 0.2 convert_reduce_fusion.1
  34.6 0.6 multiply_add_fusion.places
  35.2 0.6 fusion.17
  35.8 0.5 slice.33
  36.3 1.9 %pad_add_fusion.1.bounds = s32[2]{0:T(128)} fusion(s32[1]{0:T(128)} %slice.33, s32[1]{0:T(128)} %bitcast.4), kind=kLoop, calls=%fused_computation.99 | loop fusion | flops 2 | bytes 16 | tf_op jit(solution)/shard_map/concatenate | solution.py:367
  38.2 0.6 fusion.16
  38.8 8.7 %collective-permute-done.rest_2_ = bf16[64,128,128]{2,1,0:T(8,128)(2,1)} collective-permute-done((bf16[64,128,128]{2,1,0:T(8,128)(2,1)}, bf16[64,128,128]{2,1,0:T(8,128)(2,1)}, u32[]{:S(2)}, u32[]{:S(2)}) %collective-permute-start) | collective-permute-done | bytes 2097184 | tf_op jit(solution)/shard_map/ppermute | solution.py:290
  47.5 1.8 %collective-permute-done.1.rest_4_ = bf16[64,128,128]{2,1,0:T(8,128)(2,1)} collective-permute-done((bf16[64,128,128]{2,1,0:T(8,128)(2,1)}, bf16[64,128,128]{2,1,0:T(8,128)(2,1)}, u32[]{:S(2)}, u32[]{:S(2)}) %collective-permute-start.1) | collective-permute-done | bytes 2097184 | tf_op jit(solution)/shard_map/ppermute | solution.py:290
  49.3 1.9 %collective-permute-start.7 = (bf16[64,128,128]{2,1,0:T(8,128)(2,1)}, bf16[64,128,128]{2,1,0:T(8,128)(2,1)}, u32[]{:S(2)}, u32[]{:S(2)}) collective-permute-start(bf16[64,128,128]{2,1,0:T(8,128)(2,1)} %collective-permute-done.rest_2_), channel_id=1, source_target_pairs={{0,1},{1,0},{2,3},{3,2},{4,5},{5,4},{6,7},{7,6},{8,9},{9,8},{10,11... | collective-permute-start | bytes 6291464 | tf_op jit(solution)/shard_map/ppermute | solution.py:290
  51.2 0.0 collective-permute-start.9
  51.2 6.2 %all-to-all-start = ((bf16[64,128,128]{2,1,0:T(8,128)(2,1)}), bf16[64,128,128]{2,1,0:T(8,128)(2,1)}, u32[]{:S(2)}, u32[]{:S(2)}) async-start(bf16[64,128,128]{2,1,0:T(8,128)(2,1)} %pack_inverses.1), calls=%async_computation | async-start | bytes 4194304 | tf_op jit(solution)/shard_map/all_to_all | solution.py:327
  57.4 2.7 %slice.39 = bf16[48,128,128]{2,1,0:T(8,128)(2,1)} slice(bf16[64,128,128]{2,1,0:T(8,128)(2,1)} %collective-permute-done.rest_2_), slice={[0:48], [0:128], [0:128]} | slice | bytes 3145728 | tf_op jit(solution)/shard_map/slice | solution.py:403
  60.1 0.0 collective-permute-done.6.rest_1_
  60.1 2.2 %collective-permute-start.4 = (bf16[48,128,128]{2,1,0:T(8,128)(2,1)}, bf16[48,128,128]{2,1,0:T(8,128)(2,1)}, u32[]{:S(2)}, u32[]{:S(2)}) collective-permute-start(bf16[48,128,128]{2,1,0:T(8,128)(2,1)} %slice.39), channel_id=1, source_target_pairs={{0,4},{4,8},{8,12},{12,16},{16,20},{20,24},{24,28},{1,5},{5,9},{9,... | collective-permute-start | bytes 4718600 | tf_op jit(solution)/shard_map/ppermute | solution.py:290
  62.3 1.9 %slice.38 = bf16[16,128,128]{2,1,0:T(8,128)(2,1)} slice(bf16[64,128,128]{2,1,0:T(8,128)(2,1)} %collective-permute-done.1.rest_4_), slice={[48:64], [0:128], [0:128]} | slice | bytes 1048576 | tf_op jit(solution)/shard_map/slice | solution.py:404
  64.2 0.0 collective-permute-done.8.recv
  64.2 1.2 collective-permute-start.3
  65.4 0.0 collective-permute-done.7.rest_3_
  65.4 0.0 collective-permute-done.9.rest_5_
  65.4 13.0 %cross.1 = bf16[64,128,128]{2,1,0:T(8,128)(2,1)} custom-call(s32[128]{0:T(128)} %get-tuple-element.36.meta_keep, s32[128]{0:T(128)} %get-tuple-element.37.meta_recv, s32[2]{0:T(128)} %pad_add_fusion.1.bounds, bf16[128,128,128]{2,1,0:T(8,128)(2,1)} %get-tuple-element.38.keep, bf16[128,128,128]{2,1,0:T(8,128)(2,1)} %collective-permute-done.8.recv, ...), custom_call_target="tpu_custom_call" | custom-call | flops 1073741824 | bytes 25165824 | tf_op jit(solution)/shard_map/cross/pallas_call | solution.py:124
  78.4 0.3 collective-permute-start.10
  78.7 10.5 %collective-permute-done.3.rest_1_ = bf16[16,128,128]{2,1,0:T(8,128)(2,1)S(1)} collective-permute-done((bf16[16,128,128]{2,1,0:T(8,128)(2,1)}, bf16[16,128,128]{2,1,0:T(8,128)(2,1)S(1)}, u32[]{:S(2)}, u32[]{:S(2)}) %collective-permute-start.3) | collective-permute-done | bytes 524320 | tf_op jit(solution)/shard_map/ppermute | solution.py:290
  89.3 0.0 copy-start
  89.3 0.0 collective-permute-done.5.recv
  89.3 13.4 %own.1.early = f32[64,128,128]{2,1,0:T(8,128)} custom-call(s32[128]{0:T(128)} %get-tuple-element.29.meta_keep, s32[128]{0:T(128)} %get-tuple-element.30.meta_recv, s32[2]{0:T(128)} %pad_add_fusion.1.bounds, bf16[128,128,128]{2,1,0:T(8,128)(2,1)} %get-tuple-element.33.keep, bf16[128,128,128]{2,1,0:T(8,128)(2,1)} %collective-permute-done.5.recv, ...), custom_call_target="tpu_custom_call" | custom-call | flops 1073741824 | bytes 25165824 | tf_op jit(solution)/shard_map/own/pallas_call | solution.py:124
  102.7 35.7 %collective-permute-done.4.rest_0_ = bf16[48,128,128]{2,1,0:T(8,128)(2,1)} collective-permute-done((bf16[48,128,128]{2,1,0:T(8,128)(2,1)}, bf16[48,128,128]{2,1,0:T(8,128)(2,1)}, u32[]{:S(2)}, u32[]{:S(2)}) %collective-permute-start.4) | collective-permute-done | bytes 1572896 | tf_op jit(solution)/shard_map/ppermute | solution.py:290
  138.4 0.9 collective-permute-start.11
  139.2 0.0 copy-done
  139.2 0.0 collective-permute-start.12
  139.3 3.6 %collective-permute-done.12.rest_3_ = bf16[16,128,128]{2,1,0:T(8,128)(2,1)S(1)} collective-permute-done((bf16[16,128,128]{2,1,0:T(8,128)(2,1)S(1)}, bf16[16,128,128]{2,1,0:T(8,128)(2,1)S(1)}, u32[]{:S(2)}, u32[]{:S(2)}) %collective-permute-start.12) | collective-permute-done | bytes 524320 | tf_op jit(solution)/shard_map/ppermute | solution.py:290
  142.9 0.0 copy-start.1
  142.9 0.8 copy-done.1
  143.7 0.0 collective-permute-done.11.rest_2_
  143.7 0.0 collective-permute-done.10.other
  143.7 10.8 %near.1 = bf16[64,128,128]{2,1,0:T(8,128)(2,1)} custom-call(s32[128]{0:T(128)} %get-tuple-element.29.meta_keep, s32[128]{0:T(128)} %get-tuple-element.30.meta_recv, s32[2]{0:T(128)} %pad_add_fusion.1.bounds, f32[64,128,128]{2,1,0:T(8,128)} %own.1.early, bf16[64,128,128]{2,1,0:T(8,128)(2,1)} %collective-permute-done.10.other, ...), custom_call_target="tpu_custom_call" | custom-call | flops 536870912 | bytes 18874368 | tf_op jit(solution)/shard_map/near/pallas_call | solution.py:206
  154.5 0.0 all-to-all-done.rest_0_
  154.5 5.7 %apply.1 = bf16[64,128,128]{2,1,0:T(8,128)(2,1)} custom-call(s32[64]{0:T(128)} %multiply_add_fusion.places, bf16[64,128,128]{2,1,0:T(8,128)(2,1)} %near.1, bf16[64,128,128]{2,1,0:T(8,128)(2,1)} %all-to-all-done.rest_0_), custom_call_target="tpu_custom_call" | custom-call | flops 268435456 | bytes 6291456 | tf_op jit(solution)/shard_map/apply/pallas_call | solution.py:248
  (7 shorter events, 0.1 us)
Async XLA Ops:
  0.6 46.9 %collective-permute-start = (bf16[64,128,128]{2,1,0:T(8,128)(2,1)}, bf16[64,128,128]{2,1,0:T(8,128)(2,1)}, u32[]{:S(2)}, u32[]{:S(2)}) collective-permute-start(bf16[64,128,128]{2,1,0:T(8,128)(2,1)} %bitcast.8), channel_id=1, source_target_pairs={{0,2},{1,3},{2,0},{3,1},{4,6},{5,7},{6,4},{7,5},{8,10},{9,11},{10,... | collective-permute-start | bytes 6291464 | tf_op jit(solution)/shard_map/ppermute | solution.py:290
  0.9 48.4 %collective-permute-start.1 = (bf16[64,128,128]{2,1,0:T(8,128)(2,1)}, bf16[64,128,128]{2,1,0:T(8,128)(2,1)}, u32[]{:S(2)}, u32[]{:S(2)}) collective-permute-start(bf16[64,128,128]{2,1,0:T(8,128)(2,1)} %bitcast.9), channel_id=1, source_target_pairs={{4,0},{8,4},{12,8},{16,12},{20,16},{24,20},{28,24},{5,1},{9,5},{13... | collective-permute-start | bytes 6291464 | tf_op jit(solution)/shard_map/ppermute | solution.py:290
  12.0 9.5 %copy-start.2 = (s32[2048]{0:T(1024)S(1)}, s32[2048]{0:T(1024)}, u32[]{:S(2)}) copy-start(s32[2048]{0:T(1024)} %param.9) | copy-start | bytes 24580
  19.1 45.1 %collective-permute-start.8 = (bf16[128,128,128]{2,1,0:T(8,128)(2,1)}, bf16[128,128,128]{2,1,0:T(8,128)(2,1)}, u32[]{:S(2)}, u32[]{:S(2)}) collective-permute-start(bf16[128,128,128]{2,1,0:T(8,128)(2,1)} %get-tuple-element.39), channel_id=1, source_target_pairs={{0,1},{1,0},{2,3},{3,2},{4,5},{5,4},{6,7},{7,6},{8,9},{9,8},{10,11... | collective-permute-start | bytes 12582920 | tf_op jit(solution)/shard_map/ppermute | solution.py:290
  20.4 68.9 %collective-permute-start.5 = (bf16[128,128,128]{2,1,0:T(8,128)(2,1)}, bf16[128,128,128]{2,1,0:T(8,128)(2,1)}, u32[]{:S(2)}, u32[]{:S(2)}) collective-permute-start(bf16[128,128,128]{2,1,0:T(8,128)(2,1)} %get-tuple-element.34), channel_id=1, source_target_pairs={{0,1},{1,0},{2,3},{3,2},{4,5},{5,4},{6,7},{7,6},{8,9},{9,8},{10,11... | collective-permute-start | bytes 12582920 | tf_op jit(solution)/shard_map/ppermute | solution.py:290
  21.1 6.0 %collective-permute-start.2 = (s32[384]{0:T(512)S(1)}, s32[384]{0:T(512)S(1)}, u32[]{:S(2)}, u32[]{:S(2)}) collective-permute-start(s32[384]{0:T(512)S(1)} %pad_add_fusion), channel_id=1, source_target_pairs={{0,1},{1,0},{2,3},{3,2},{4,5},{5,4},{6,7},{7,6},{8,9},{9,8},{10,11... | collective-permute-start | bytes 4616 | tf_op jit(solution)/shard_map/ppermute | solution.py:290
  27.2 32.9 %collective-permute-start.6 = (bf16[64,128,128]{2,1,0:T(8,128)(2,1)}, bf16[64,128,128]{2,1,0:T(8,128)(2,1)}, u32[]{:S(2)}, u32[]{:S(2)}) collective-permute-start(bf16[64,128,128]{2,1,0:T(8,128)(2,1)} %bitcast.10), channel_id=1, source_target_pairs={{0,1},{1,0},{2,3},{3,2},{4,5},{5,4},{6,7},{7,6},{8,9},{9,8},{10,11... | collective-permute-start | bytes 6291464 | tf_op jit(solution)/shard_map/ppermute | solution.py:290
  49.3 16.0 %collective-permute-start.7 = (bf16[64,128,128]{2,1,0:T(8,128)(2,1)}, bf16[64,128,128]{2,1,0:T(8,128)(2,1)}, u32[]{:S(2)}, u32[]{:S(2)}) collective-permute-start(bf16[64,128,128]{2,1,0:T(8,128)(2,1)} %collective-permute-done.rest_2_), channel_id=1, source_target_pairs={{0,1},{1,0},{2,3},{3,2},{4,5},{5,4},{6,7},{7,6},{8,9},{9,8},{10,11... | collective-permute-start | bytes 6291464 | tf_op jit(solution)/shard_map/ppermute | solution.py:290
  51.2 14.2 %collective-permute-start.9 = (bf16[64,128,128]{2,1,0:T(8,128)(2,1)}, bf16[64,128,128]{2,1,0:T(8,128)(2,1)}, u32[]{:S(2)}, u32[]{:S(2)}) collective-permute-start(bf16[64,128,128]{2,1,0:T(8,128)(2,1)} %collective-permute-done.1.rest_4_), channel_id=1, source_target_pairs={{0,1},{1,0},{2,3},{3,2},{4,5},{5,4},{6,7},{7,6},{8,9},{9,8},{10,11... | collective-permute-start | bytes 6291464 | tf_op jit(solution)/shard_map/ppermute | solution.py:290
  51.2 103.3 %all-to-all-start = ((bf16[64,128,128]{2,1,0:T(8,128)(2,1)}), bf16[64,128,128]{2,1,0:T(8,128)(2,1)}, u32[]{:S(2)}, u32[]{:S(2)}) async-start(bf16[64,128,128]{2,1,0:T(8,128)(2,1)} %pack_inverses.1), calls=%async_computation | async-start | bytes 4194304 | tf_op jit(solution)/shard_map/all_to_all | solution.py:327
  60.1 78.3 %collective-permute-start.4 = (bf16[48,128,128]{2,1,0:T(8,128)(2,1)}, bf16[48,128,128]{2,1,0:T(8,128)(2,1)}, u32[]{:S(2)}, u32[]{:S(2)}) collective-permute-start(bf16[48,128,128]{2,1,0:T(8,128)(2,1)} %slice.39), channel_id=1, source_target_pairs={{0,4},{4,8},{8,12},{12,16},{16,20},{20,24},{24,28},{1,5},{5,9},{9,... | collective-permute-start | bytes 4718600 | tf_op jit(solution)/shard_map/ppermute | solution.py:290
  64.2 25.1 %collective-permute-start.3 = (bf16[16,128,128]{2,1,0:T(8,128)(2,1)}, bf16[16,128,128]{2,1,0:T(8,128)(2,1)S(1)}, u32[]{:S(2)}, u32[]{:S(2)}) collective-permute-start(bf16[16,128,128]{2,1,0:T(8,128)(2,1)} %slice.38), channel_id=1, source_target_pairs={{0,2},{1,3},{2,0},{3,1},{4,6},{5,7},{6,4},{7,5},{8,10},{9,11},{10,... | collective-permute-start | bytes 1572872 | tf_op jit(solution)/shard_map/ppermute | solution.py:290
  78.4 65.3 %collective-permute-start.10 = (bf16[64,128,128]{2,1,0:T(8,128)(2,1)}, bf16[64,128,128]{2,1,0:T(8,128)(2,1)}, u32[]{:S(2)}, u32[]{:S(2)}) collective-permute-start(bf16[64,128,128]{2,1,0:T(8,128)(2,1)} %cross.1), channel_id=1, source_target_pairs={{0,2},{1,3},{2,0},{3,1},{4,6},{5,7},{6,4},{7,5},{8,10},{9,11},{10,... | collective-permute-start | bytes 6291464 | tf_op jit(solution)/shard_map/ppermute | solution.py:290
  89.3 50.0 %copy-start = (bf16[16,128,128]{2,1,0:T(8,128)(2,1)}, bf16[16,128,128]{2,1,0:T(8,128)(2,1)S(1)}, u32[]{:S(2)}) copy-start(bf16[16,128,128]{2,1,0:T(8,128)(2,1)S(1)} %collective-permute-done.3.rest_1_) | copy-start | bytes 1572868
  138.4 5.3 %collective-permute-start.11 = (bf16[48,128,128]{2,1,0:T(8,128)(2,1)}, bf16[48,128,128]{2,1,0:T(8,128)(2,1)}, u32[]{:S(2)}, u32[]{:S(2)}) collective-permute-start(bf16[48,128,128]{2,1,0:T(8,128)(2,1)} %collective-permute-done.4.rest_0_), channel_id=1, source_target_pairs={{0,1},{1,0},{2,3},{3,2},{4,5},{5,4},{6,7},{7,6},{8,9},{9,8},{10,11... | collective-permute-start | bytes 4718600 | tf_op jit(solution)/shard_map/ppermute | solution.py:290
  139.2 3.6 %collective-permute-start.12 = (bf16[16,128,128]{2,1,0:T(8,128)(2,1)S(1)}, bf16[16,128,128]{2,1,0:T(8,128)(2,1)S(1)}, u32[]{:S(2)}, u32[]{:S(2)}) collective-permute-start(bf16[16,128,128]{2,1,0:T(8,128)(2,1)S(1)} %collective-permute-done.3.rest_1_), channel_id=1, source_target_pairs={{0,1},{1,0},{2,3},{3,2},{4,5},{5,4},{6,7},{7,6},{8,9},{9,8},{10,11... | collective-permute-start | bytes 1572872 | tf_op jit(solution)/shard_map/ppermute | solution.py:290
  142.9 0.8 copy-start.1

commit v7 on v6

--- a/solution.py
+++ b/solution.py
@@ -65,6 +65,40 @@
         ),
         name=name,
     )(order, tiles)
+
+
+def split_kernel(cut, first, second, head, tail, held, sem):
+    rest = held.shape[0] - cut
+    parts = (
+        (first.at[pl.ds(0, cut)], held.at[pl.ds(0, cut)], head),
+        (second.at[pl.ds(cut, rest)], held.at[pl.ds(cut, rest)], tail),
+    )
+    loads = [pltpu.make_async_copy(a, b, sem.at[i]) for i, (a, b, c) in enumerate(parts)]
+    stores = [pltpu.make_async_copy(b, c, sem.at[2 + i]) for i, (a, b, c) in enumerate(parts)]
+    for load in loads:
+        load.start()
+    for load, store in zip(loads, stores):
+        load.wait()
+        store.start()
+    for store in stores:
+        store.wait()
+
+
+def split(cut, first, second):
+    tile = first.shape[1:]
+    return pl.pallas_call(
+        functools.partial(split_kernel, cut),
+        out_shape=(
+            jax.ShapeDtypeStruct((cut,) + tile, first.dtype),
+            jax.ShapeDtypeStruct((first.shape[0] - cut,) + tile, first.dtype),
+        ),
+        in_specs=[HBM, HBM],
+        out_specs=(HBM, HBM),
+        scratch_shapes=[pltpu.VMEM(first.shape, first.dtype), pltpu.SemaphoreType.DMA((4,))],
+        compiler_params=params(63),
+        cost_estimate=cost(0, 4),
+        name="split",
+    )(first, second)
 
 
 def add_tiles(meta_ref, place, count, tiles, start, band, acc, bits):
@@ -139,8 +173,10 @@
     )(meta_keep, meta_recv, bounds, keep, recv, *pieces)
 
 
-def near_kernel(bits, meta_keep, meta_recv, bounds, early, other, keep, recv, *rest):
-    pieces, (near, acc, sent, band, mine, theirs, sem) = rest[:-7], rest[-7:]
+def final_kernel(
+    bits, meta_keep, meta_recv, bounds, places, early, other, keep, recv, inbox, *rest
+):
+    pieces, (near, out, acc, sent, band, mine, theirs, inverse, sem) = rest[:-9], rest[-9:]
     count = keep.shape[0]
     size = acc.shape[0]
     loads = [
@@ -154,6 +190,7 @@
         place += piece.shape[0]
     for load in loads:
         load.start()
+    inverses = pltpu.make_async_copy(inbox, inverse, sem.at[4 + len(pieces)])
     sides = ((meta_keep, keep, mine), (meta_recv, recv, theirs))
 
     def chunk_copy(side, chunk):
@@ -170,6 +207,7 @@
             return carry
 
         lax.fori_loop(bounds[side] // CHUNK, count // CHUNK, fetch, 0)
+    inverses.start()
     for side in (0, 1):
 
         def settle(chunk, carry):
@@ -197,67 +235,42 @@
         even = (first + 7) // 8
         lax.fori_loop(first, even * 8, add, 0)
         lax.fori_loop(even, count // 8, add_eight, 0)
-    near[...] = (acc[...] + sent[...].astype(jnp.float32)).astype(jnp.bfloat16)
-
-
-def near_sums(bits, meta_keep, meta_recv, bounds, early, other, keep, recv, pieces):
+    inverses.wait()
+
+    def apply(turn, carry):
+        block = (acc[turn] + sent[turn].astype(jnp.float32)).astype(jnp.bfloat16)
+        near[turn] = block
+        out[turn] = jnp.dot(
+            inverse[places[turn]], block, preferred_element_type=jnp.float32
+        ).astype(jnp.bfloat16)
+        return carry
+
+    lax.fori_loop(0, size, apply, 0, unroll=16)
+
+
+def final(
+    bits, meta_keep, meta_recv, bounds, places, early, other, keep, recv, inbox, pieces
+):
     block = early.shape
     held = pltpu.VMEM(keep.shape, keep.dtype)
     return pl.pallas_call(
-        functools.partial(near_kernel, bits),
-        out_shape=jax.ShapeDtypeStruct(block, jnp.bfloat16),
-        in_specs=[SMEM] * 3 + [HBM] * (4 + len(pieces)),
-        out_specs=VMEM,
+        functools.partial(final_kernel, bits),
+        out_shape=(jax.ShapeDtypeStruct(block, jnp.bfloat16),) * 2,
+        in_specs=[SMEM] * 4 + [HBM] * (5 + len(pieces)),
+        out_specs=(VMEM, VMEM),
         scratch_shapes=[
             pltpu.VMEM(block, jnp.float32),
             pltpu.VMEM(block, jnp.bfloat16),
             pltpu.VMEM((2 * block[0],) + block[1:], jnp.bfloat16),
             held,
             held,
-            pltpu.SemaphoreType.DMA((4 + len(pieces),)),
+            pltpu.VMEM(inbox.shape, jnp.bfloat16),
+            pltpu.SemaphoreType.DMA((5 + len(pieces),)),
         ],
         compiler_params=params(63),
-        cost_estimate=cost(2 * keep.size * block[2], 18),
-        name="near",
-    )(meta_keep, meta_recv, bounds, early, other, keep, recv, *pieces)
-
-
-def apply_kernel(places, near, *rest):
-    inbox, (out, inverse, sem) = rest[:-3], rest[-3:]
-    loads = []
-    for place, part in enumerate(inbox):
-        count = part.shape[0]
-        loads.append(
-            pltpu.make_async_copy(part, inverse.at[pl.ds(place * count, count)], sem.at[place])
-        )
-        loads[-1].start()
-    for load in loads:
-        load.wait()
-
-    def apply(turn, carry):
-        out[turn] = jnp.dot(
-            inverse[places[turn]], near[turn], preferred_element_type=jnp.float32
-        ).astype(jnp.bfloat16)
-        return carry
-
-    lax.fori_loop(0, near.shape[0], apply, 0, unroll=16)
-
-
-def apply_inverses(places, near, inbox):
-    block = inbox[0].shape
-    return pl.pallas_call(
-        apply_kernel,
-        out_shape=jax.ShapeDtypeStruct(near.shape, jnp.bfloat16),
-        in_specs=[SMEM, VMEM] + [HBM] * len(inbox),
-        out_specs=VMEM,
-        scratch_shapes=[
-            pltpu.VMEM((len(inbox) * block[0],) + block[1:], jnp.bfloat16),
-            pltpu.SemaphoreType.DMA((len(inbox),)),
-        ],
-        compiler_params=params(63),
-        cost_estimate=cost(2 * near.size * near.shape[1], 6),
-        name="apply",
-    )(places, near, *inbox)
+        cost_estimate=cost(3 * keep.size * block[2], 22),
+        name="final",
+    )(meta_keep, meta_recv, bounds, places, early, other, keep, recv, inbox, *pieces)
 
 
 def ranks_by(labels, key):
@@ -321,7 +334,7 @@
     target = held // own
     place_held = target * capacity + ranks_by(target, held % own)
     outbox_order = pick(place_held, jnp.arange(devices * capacity, dtype=jnp.int32))
-    outbox = gather_tiles(outbox_order, inverses, 0, 1, devices * capacity, "pack_inverses")
+    (outbox,) = gather_tiles(outbox_order, inverses, 0, 1, devices * capacity, "pack_inverses")
 
     def exchange(value):
         return lax.all_to_all(value, AXES, split_axis=0, concat_axis=0, tiled=True)
@@ -400,10 +413,11 @@
 
     other_beside = permute(other_chip, beside)
     cut = own - own // 4
-    halo_late = permute(other_chip[:cut], late)
-    halo_across = permute(halo_early[cut:], across)
+    late_part, across_part = split(cut, other_chip, halo_early)
+    halo_late = permute(late_part, late)
+    halo_across = permute(across_part, across)
+    inbox = exchange(outbox)
     early_beside = permute(halo_early, beside)
-    inbox = [exchange(part) for part in outbox]
     group_pieces = (blocks, own_beside, other_chip, other_beside)
     cross = sums(
         bits,
@@ -434,18 +448,19 @@
     halo_late, early_sums = lax.optimization_barrier((halo_late, early_sums))
     late_beside = permute(halo_late, beside)
     across_beside = permute(halo_across, beside)
-    near = near_sums(
+    near, result = final(
         bits,
         own_keep,
         own_recv,
         bounds,
+        places,
         early_sums,
         other_sums,
         keep_own,
         recv_own,
+        inbox,
         (halo_late, halo_across, late_beside, across_beside),
     )
-    result = apply_inverses(places, near, inbox)
     return near.reshape(own * size, columns), result.reshape(own * size, columns)
 
 

time: 161 us -> 156 us (0.969)
  local copies, waits for them, and re-layouts: 7.14 us -> 2.5 us
  Pallas kernels: 60.4 us -> 57.8 us
  waiting for transfers between devices: 65.8 us -> 68 us
    slice x2 -> x0, local copies, waits for them, and re-layouts: 4.63 us -> none  [the longest x1 2.73 us: per_device(): halo_late = permute(other_chip[:cut], late)]
    ppermute x13, waiting for transfers between devices: 65.8 us -> 68 us  [permute(): return lax.ppermute(value, AXES, pairs)]
    pallas_call x2, Pallas kernels: 16.5 us -> 14.6 us  [the longest x1 11.8 us: final(): pl.pallas_call(functools.partial(final_kernel, bits), out_shape=(jax.Shap...]
  transfers between devices with their start and end apart: 14 -> 14, of which waited for: 6 -> 6; matrix products, arithmetic and copies ran while one was open for 9% -> 6% of each run, Pallas kernels for 34% -> 30%
where the time goes in v7:
time: 156 us
  waiting for transfers between devices  68 us (44%)
  Pallas kernels  57.8 us (37%)
  starting transfers between devices  18.4 us (12%)
  other arithmetic  8.04 us (5%)
  local copies, waits for them, and re-layouts  2.5 us (2%)
    ppermute x13, waiting for transfers between devices, permute(): return lax.ppermute(value, AXES, pairs)  68 us
    pallas_call x2, Pallas kernels, sums(): pl.pallas_call(functools.partial(sums_kernel, bits, whole), out_shape=jax...  25.9 us
    pallas_call x3, Pallas kernels, gather_tiles(): pl.pallas_call(functools.partial(gather_kernel, first), out_shape=(jax.Sh...  17.4 us
    ppermute x13, starting transfers between devices, permute(): return lax.ppermute(value, AXES, pairs)  12.2 us
    pallas_call x1, Pallas kernels, final(): pl.pallas_call(functools.partial(final_kernel, bits), out_shape=(jax.Shap...  11.8 us
    all_to_all x1, starting transfers between devices, exchange(): return lax.all_to_all(value, AXES, split_axis=0, concat_axis=0, tiled=True)  6.16 us
  transfers between devices with their start and end apart: 14, of which 6 were waited for; matrix products, arithmetic and copies ran while one was open for 6% of the time, Pallas kernels for 30%

profile of v7, /device:TPU:15, one launch (start us, length us, event | category | flops | bytes accessed | tf_op | source)
XLA Modules:
  0.0 155.5 jit_solution(5055717875239112044)
XLA Ops:
  0.6 0.3 collective-permute-start
  0.9 3.1 %collective-permute-start.1 = (bf16[64,128,128]{2,1,0:T(8,128)(2,1)}, bf16[64,128,128]{2,1,0:T(8,128)(2,1)}, u32[]{:S(2)}, u32[]{:S(2)}) collective-permute-start(bf16[64,128,128]{2,1,0:T(8,128)(2,1)} %bitcast.9), channel_id=1, source_target_pairs={{4,0},{8,4},{12,8},{16,12},{20,16},{24,20},{28,24},{5,1},{9,5},{13... | collective-permute-start | bytes 6291464 | tf_op jit(solution)/shard_map/ppermute | solution.py:303
  4.1 0.8 and_select_fusion.8
  4.9 0.2 convert_reduce_fusion.2
  5.1 0.7 select_reduce_fusion.3.order_ref
  5.8 0.8 iota_add_fusion.1
  6.6 0.7 convert_reduce_fusion.4
  7.4 0.2 convert_reduce_fusion
  7.6 0.9 select_reduce_fusion
  8.6 3.5 %pack_inverses.1 = bf16[64,128,128]{2,1,0:T(8,128)(2,1)} custom-call(s32[64]{0:T(128)} %select_reduce_fusion.3.order_ref, bf16[64,128,128]{2,1,0:T(8,128)(2,1)} %tiles.3), custom_call_target="tpu_custom_call" | custom-call | bytes 8388608 | tf_op jit(solution)/shard_map/pack_inverses/pallas_call | solution.py:53
  12.1 0.0 copy-start.2
  12.1 7.0 %pack_send.1 = (bf16[128,128,128]{2,1,0:T(8,128)(2,1)}, bf16[128,128,128]{2,1,0:T(8,128)(2,1)}) custom-call(s32[512]{0:T(512)} %get-tuple-element.27.order_ref, bf16[512,128,128]{2,1,0:T(8,128)(2,1)} %tiles.5), custom_call_target="tpu_custom_call" | custom-call | bytes 33554432 | tf_op jit(solution)/shard_map/pack_send/pallas_call | solution.py:53
  19.1 1.3 collective-permute-start.8
  20.4 0.1 collective-permute-start.5
  20.5 0.6 pad_add_fusion
  21.1 0.4 collective-permute-start.2
  21.6 0.0 copy-done.2
  21.6 0.2 select_reduce_fusion.2
  21.8 5.4 %collective-permute-done.2 = s32[384]{0:T(512)S(1)} collective-permute-done((s32[384]{0:T(512)S(1)}, s32[384]{0:T(512)S(1)}, u32[]{:S(2)}, u32[]{:S(2)}) %collective-permute-start.2) | collective-permute-done | bytes 1568 | tf_op jit(solution)/shard_map/ppermute | solution.py:303
  27.2 0.4 collective-permute-start.6
  27.6 6.9 %pack_keep.1 = (bf16[128,128,128]{2,1,0:T(8,128)(2,1)}, bf16[128,128,128]{2,1,0:T(8,128)(2,1)}) custom-call(s32[512]{0:T(512)} %get-tuple-element.27.order_ref, bf16[512,128,128]{2,1,0:T(8,128)(2,1)} %tiles.5), custom_call_target="tpu_custom_call" | custom-call | bytes 33554432 | tf_op jit(solution)/shard_map/pack_keep/pallas_call | solution.py:53
  34.5 0.2 convert_reduce_fusion.1
  34.7 0.6 multiply_add_fusion.places
  35.3 0.6 fusion.17
  35.9 0.5 slice.27
  36.4 1.9 %pad_add_fusion.1.bounds = s32[2]{0:T(128)} fusion(s32[1]{0:T(128)} %slice.27, s32[1]{0:T(128)} %bitcast.4), kind=kLoop, calls=%fused_computation.99 | loop fusion | flops 2 | bytes 16 | tf_op jit(solution)/shard_map/concatenate | solution.py:380
  38.3 0.6 fusion.16
  38.9 8.6 %collective-permute-done.first.rest_2_ = bf16[64,128,128]{2,1,0:T(8,128)(2,1)} collective-permute-done((bf16[64,128,128]{2,1,0:T(8,128)(2,1)}, bf16[64,128,128]{2,1,0:T(8,128)(2,1)}, u32[]{:S(2)}, u32[]{:S(2)}) %collective-permute-start) | collective-permute-done | bytes 2097184 | tf_op jit(solution)/shard_map/ppermute | solution.py:303
  47.5 1.8 %collective-permute-done.1.second.rest_4_ = bf16[64,128,128]{2,1,0:T(8,128)(2,1)} collective-permute-done((bf16[64,128,128]{2,1,0:T(8,128)(2,1)}, bf16[64,128,128]{2,1,0:T(8,128)(2,1)}, u32[]{:S(2)}, u32[]{:S(2)}) %collective-permute-start.1) | collective-permute-done | bytes 2097184 | tf_op jit(solution)/shard_map/ppermute | solution.py:303
  49.3 1.9 %collective-permute-start.7 = (bf16[64,128,128]{2,1,0:T(8,128)(2,1)}, bf16[64,128,128]{2,1,0:T(8,128)(2,1)}, u32[]{:S(2)}, u32[]{:S(2)}) collective-permute-start(bf16[64,128,128]{2,1,0:T(8,128)(2,1)} %collective-permute-done.first.rest_2_), channel_id=1, source_target_pairs={{0,1},{1,0},{2,3},{3,2},{4,5},{5,4},{6,7},{7,6},{8,9},{9,8},{10,11... | collective-permute-start | bytes 6291464 | tf_op jit(solution)/shard_map/ppermute | solution.py:303
  51.2 0.0 collective-permute-start.9
  51.2 6.2 %all-to-all-start = ((bf16[64,128,128]{2,1,0:T(8,128)(2,1)}), bf16[64,128,128]{2,1,0:T(8,128)(2,1)}, u32[]{:S(2)}, u32[]{:S(2)}) async-start(bf16[64,128,128]{2,1,0:T(8,128)(2,1)} %pack_inverses.1), calls=%async_computation | async-start | bytes 4194304 | tf_op jit(solution)/shard_map/all_to_all | solution.py:340
  57.4 2.7 %split.1 = (bf16[48,128,128]{2,1,0:T(8,128)(2,1)}, bf16[16,128,128]{2,1,0:T(8,128)(2,1)}) custom-call(bf16[64,128,128]{2,1,0:T(8,128)(2,1)} %collective-permute-done.first.rest_2_, bf16[64,128,128]{2,1,0:T(8,128)(2,1)} %collective-permute-done.1.second.rest_4_), custom_call_target="tpu_custom_call" | custom-call | bytes 4194304 | tf_op jit(solution)/shard_map/split/pallas_call | solution.py:89
  60.1 0.0 collective-permute-done.6.rest_1_
  60.1 2.2 %collective-permute-start.4 = (bf16[48,128,128]{2,1,0:T(8,128)(2,1)}, bf16[48,128,128]{2,1,0:T(8,128)(2,1)}, u32[]{:S(2)}, u32[]{:S(2)}) collective-permute-start(bf16[48,128,128]{2,1,0:T(8,128)(2,1)} %get-tuple-element.39), channel_id=1, source_target_pairs={{0,4},{4,8},{8,12},{12,16},{16,20},{20,24},{24,28},{1,5},{5,9},{9,... | collective-permute-start | bytes 4718600 | tf_op jit(solution)/shard_map/ppermute | solution.py:303
  62.3 0.0 collective-permute-done.8.recv
  62.3 1.3 collective-permute-start.3
  63.6 0.0 collective-permute-done.7.rest_3_
  63.6 0.0 collective-permute-done.9.rest_5_
  63.6 13.0 %cross.1 = bf16[64,128,128]{2,1,0:T(8,128)(2,1)} custom-call(s32[128]{0:T(128)} %get-tuple-element.43.meta_keep, s32[128]{0:T(128)} %get-tuple-element.44.meta_recv, s32[2]{0:T(128)} %pad_add_fusion.1.bounds, bf16[128,128,128]{2,1,0:T(8,128)(2,1)} %get-tuple-element.45.keep, bf16[128,128,128]{2,1,0:T(8,128)(2,1)} %collective-permute-done.8.recv, ...), custom_call_target="tpu_custom_call" | custom-call | flops 1073741824 | bytes 25165824 | tf_op jit(solution)/shard_map/cross/pallas_call | solution.py:158
  76.6 0.4 collective-permute-start.10
  77.0 12.3 %collective-permute-done.3.rest_1_ = bf16[16,128,128]{2,1,0:T(8,128)(2,1)S(1)} collective-permute-done((bf16[16,128,128]{2,1,0:T(8,128)(2,1)}, bf16[16,128,128]{2,1,0:T(8,128)(2,1)S(1)}, u32[]{:S(2)}, u32[]{:S(2)}) %collective-permute-start.3) | collective-permute-done | bytes 524320 | tf_op jit(solution)/shard_map/ppermute | solution.py:303
  89.3 0.0 copy-start
  89.3 0.0 collective-permute-done.5.recv
  89.3 12.9 %own.1.early = f32[64,128,128]{2,1,0:T(8,128)} custom-call(s32[128]{0:T(128)} %get-tuple-element.35.meta_keep, s32[128]{0:T(128)} %get-tuple-element.36.meta_recv, s32[2]{0:T(128)} %pad_add_fusion.1.bounds, bf16[128,128,128]{2,1,0:T(8,128)(2,1)} %get-tuple-element.40.keep, bf16[128,128,128]{2,1,0:T(8,128)(2,1)} %collective-permute-done.5.recv, ...), custom_call_target="tpu_custom_call" | custom-call | flops 1073741824 | bytes 25165824 | tf_op jit(solution)/shard_map/own/pallas_call | solution.py:158
  102.2 36.1 %collective-permute-done.4.rest_0_ = bf16[48,128,128]{2,1,0:T(8,128)(2,1)} collective-permute-done((bf16[48,128,128]{2,1,0:T(8,128)(2,1)}, bf16[48,128,128]{2,1,0:T(8,128)(2,1)}, u32[]{:S(2)}, u32[]{:S(2)}) %collective-permute-start.4) | collective-permute-done | bytes 1572896 | tf_op jit(solution)/shard_map/ppermute | solution.py:303
  138.4 0.9 collective-permute-start.11
  139.3 0.0 copy-done
  139.3 0.0 collective-permute-start.12
  139.3 3.6 %collective-permute-done.12.rest_3_ = bf16[16,128,128]{2,1,0:T(8,128)(2,1)S(1)} collective-permute-done((bf16[16,128,128]{2,1,0:T(8,128)(2,1)S(1)}, bf16[16,128,128]{2,1,0:T(8,128)(2,1)S(1)}, u32[]{:S(2)}, u32[]{:S(2)}) %collective-permute-start.12) | collective-permute-done | bytes 524320 | tf_op jit(solution)/shard_map/ppermute | solution.py:303
  142.9 0.0 copy-start.1
  142.9 0.8 copy-done.1
  143.7 0.0 collective-permute-done.11.rest_2_
  143.7 0.0 all-to-all-done.inbox
  143.7 0.0 collective-permute-done.10.other
  143.7 11.8 %final.1 = (bf16[64,128,128]{2,1,0:T(8,128)(2,1)}, bf16[64,128,128]{2,1,0:T(8,128)(2,1)}) custom-call(s32[128]{0:T(128)} %get-tuple-element.35.meta_keep, s32[128]{0:T(128)} %get-tuple-element.36.meta_recv, s32[2]{0:T(128)} %pad_add_fusion.1.bounds, s32[64]{0:T(128)} %multiply_add_fusion.places, f32[64,128,128]{2,1,0:T(8,128)} %own.1.early, ...), custom_call_target="tpu_custom_call" | custom-call | flops 805306368 | bytes 23068672 | tf_op jit(solution)/shard_map/final/pallas_call | solution.py:256
  (7 shorter events, 0.1 us)
Async XLA Ops:
  0.6 46.9 %collective-permute-start = (bf16[64,128,128]{2,1,0:T(8,128)(2,1)}, bf16[64,128,128]{2,1,0:T(8,128)(2,1)}, u32[]{:S(2)}, u32[]{:S(2)}) collective-permute-start(bf16[64,128,128]{2,1,0:T(8,128)(2,1)} %bitcast.8), channel_id=1, source_target_pairs={{0,2},{1,3},{2,0},{3,1},{4,6},{5,7},{6,4},{7,5},{8,10},{9,11},{10,... | collective-permute-start | bytes 6291464 | tf_op jit(solution)/shard_map/ppermute | solution.py:303
  0.9 48.4 %collective-permute-start.1 = (bf16[64,128,128]{2,1,0:T(8,128)(2,1)}, bf16[64,128,128]{2,1,0:T(8,128)(2,1)}, u32[]{:S(2)}, u32[]{:S(2)}) collective-permute-start(bf16[64,128,128]{2,1,0:T(8,128)(2,1)} %bitcast.9), channel_id=1, source_target_pairs={{4,0},{8,4},{12,8},{16,12},{20,16},{24,20},{28,24},{5,1},{9,5},{13... | collective-permute-start | bytes 6291464 | tf_op jit(solution)/shard_map/ppermute | solution.py:303
  12.1 9.5 %copy-start.2 = (s32[2048]{0:T(1024)S(1)}, s32[2048]{0:T(1024)}, u32[]{:S(2)}) copy-start(s32[2048]{0:T(1024)} %param.9) | copy-start | bytes 24580
  19.1 43.2 %collective-permute-start.8 = (bf16[128,128,128]{2,1,0:T(8,128)(2,1)}, bf16[128,128,128]{2,1,0:T(8,128)(2,1)}, u32[]{:S(2)}, u32[]{:S(2)}) collective-permute-start(bf16[128,128,128]{2,1,0:T(8,128)(2,1)} %get-tuple-element.46), channel_id=1, source_target_pairs={{0,1},{1,0},{2,3},{3,2},{4,5},{5,4},{6,7},{7,6},{8,9},{9,8},{10,11... | collective-permute-start | bytes 12582920 | tf_op jit(solution)/shard_map/ppermute | solution.py:303
  20.4 68.9 %collective-permute-start.5 = (bf16[128,128,128]{2,1,0:T(8,128)(2,1)}, bf16[128,128,128]{2,1,0:T(8,128)(2,1)}, u32[]{:S(2)}, u32[]{:S(2)}) collective-permute-start(bf16[128,128,128]{2,1,0:T(8,128)(2,1)} %get-tuple-element.41), channel_id=1, source_target_pairs={{0,1},{1,0},{2,3},{3,2},{4,5},{5,4},{6,7},{7,6},{8,9},{9,8},{10,11... | collective-permute-start | bytes 12582920 | tf_op jit(solution)/shard_map/ppermute | solution.py:303
  21.1 6.1 %collective-permute-start.2 = (s32[384]{0:T(512)S(1)}, s32[384]{0:T(512)S(1)}, u32[]{:S(2)}, u32[]{:S(2)}) collective-permute-start(s32[384]{0:T(512)S(1)} %pad_add_fusion), channel_id=1, source_target_pairs={{0,1},{1,0},{2,3},{3,2},{4,5},{5,4},{6,7},{7,6},{8,9},{9,8},{10,11... | collective-permute-start | bytes 4616 | tf_op jit(solution)/shard_map/ppermute | solution.py:303
  27.2 32.9 %collective-permute-start.6 = (bf16[64,128,128]{2,1,0:T(8,128)(2,1)}, bf16[64,128,128]{2,1,0:T(8,128)(2,1)}, u32[]{:S(2)}, u32[]{:S(2)}) collective-permute-start(bf16[64,128,128]{2,1,0:T(8,128)(2,1)} %bitcast.10), channel_id=1, source_target_pairs={{0,1},{1,0},{2,3},{3,2},{4,5},{5,4},{6,7},{7,6},{8,9},{9,8},{10,11... | collective-permute-start | bytes 6291464 | tf_op jit(solution)/shard_map/ppermute | solution.py:303
  49.3 14.3 %collective-permute-start.7 = (bf16[64,128,128]{2,1,0:T(8,128)(2,1)}, bf16[64,128,128]{2,1,0:T(8,128)(2,1)}, u32[]{:S(2)}, u32[]{:S(2)}) collective-permute-start(bf16[64,128,128]{2,1,0:T(8,128)(2,1)} %collective-permute-done.first.rest_2_), channel_id=1, source_target_pairs={{0,1},{1,0},{2,3},{3,2},{4,5},{5,4},{6,7},{7,6},{8,9},{9,8},{10,11... | collective-permute-start | bytes 6291464 | tf_op jit(solution)/shard_map/ppermute | solution.py:303
  51.2 12.4 %collective-permute-start.9 = (bf16[64,128,128]{2,1,0:T(8,128)(2,1)}, bf16[64,128,128]{2,1,0:T(8,128)(2,1)}, u32[]{:S(2)}, u32[]{:S(2)}) collective-permute-start(bf16[64,128,128]{2,1,0:T(8,128)(2,1)} %collective-permute-done.1.second.rest_4_), channel_id=1, source_target_pairs={{0,1},{1,0},{2,3},{3,2},{4,5},{5,4},{6,7},{7,6},{8,9},{9,8},{10,11... | collective-permute-start | bytes 6291464 | tf_op jit(solution)/shard_map/ppermute | solution.py:303
  51.2 92.5 %all-to-all-start = ((bf16[64,128,128]{2,1,0:T(8,128)(2,1)}), bf16[64,128,128]{2,1,0:T(8,128)(2,1)}, u32[]{:S(2)}, u32[]{:S(2)}) async-start(bf16[64,128,128]{2,1,0:T(8,128)(2,1)} %pack_inverses.1), calls=%async_computation | async-start | bytes 4194304 | tf_op jit(solution)/shard_map/all_to_all | solution.py:340
  60.1 78.2 %collective-permute-start.4 = (bf16[48,128,128]{2,1,0:T(8,128)(2,1)}, bf16[48,128,128]{2,1,0:T(8,128)(2,1)}, u32[]{:S(2)}, u32[]{:S(2)}) collective-permute-start(bf16[48,128,128]{2,1,0:T(8,128)(2,1)} %get-tuple-element.39), channel_id=1, source_target_pairs={{0,4},{4,8},{8,12},{12,16},{16,20},{20,24},{24,28},{1,5},{5,9},{9,... | collective-permute-start | bytes 4718600 | tf_op jit(solution)/shard_map/ppermute | solution.py:303
  62.3 26.9 %collective-permute-start.3 = (bf16[16,128,128]{2,1,0:T(8,128)(2,1)}, bf16[16,128,128]{2,1,0:T(8,128)(2,1)S(1)}, u32[]{:S(2)}, u32[]{:S(2)}) collective-permute-start(bf16[16,128,128]{2,1,0:T(8,128)(2,1)} %get-tuple-element.34), channel_id=1, source_target_pairs={{0,2},{1,3},{2,0},{3,1},{4,6},{5,7},{6,4},{7,5},{8,10},{9,11},{10,... | collective-permute-start | bytes 1572872 | tf_op jit(solution)/shard_map/ppermute | solution.py:303
  76.6 67.1 %collective-permute-start.10 = (bf16[64,128,128]{2,1,0:T(8,128)(2,1)}, bf16[64,128,128]{2,1,0:T(8,128)(2,1)}, u32[]{:S(2)}, u32[]{:S(2)}) collective-permute-start(bf16[64,128,128]{2,1,0:T(8,128)(2,1)} %cross.1), channel_id=1, source_target_pairs={{0,2},{1,3},{2,0},{3,1},{4,6},{5,7},{6,4},{7,5},{8,10},{9,11},{10,... | collective-permute-start | bytes 6291464 | tf_op jit(solution)/shard_map/ppermute | solution.py:303
  89.3 50.0 %copy-start = (bf16[16,128,128]{2,1,0:T(8,128)(2,1)}, bf16[16,128,128]{2,1,0:T(8,128)(2,1)S(1)}, u32[]{:S(2)}) copy-start(bf16[16,128,128]{2,1,0:T(8,128)(2,1)S(1)} %collective-permute-done.3.rest_1_) | copy-start | bytes 1572868
  138.4 5.3 %collective-permute-start.11 = (bf16[48,128,128]{2,1,0:T(8,128)(2,1)}, bf16[48,128,128]{2,1,0:T(8,128)(2,1)}, u32[]{:S(2)}, u32[]{:S(2)}) collective-permute-start(bf16[48,128,128]{2,1,0:T(8,128)(2,1)} %collective-permute-done.4.rest_0_), channel_id=1, source_target_pairs={{0,1},{1,0},{2,3},{3,2},{4,5},{5,4},{6,7},{7,6},{8,9},{9,8},{10,11... | collective-permute-start | bytes 4718600 | tf_op jit(solution)/shard_map/ppermute | solution.py:303
  139.3 3.6 %collective-permute-start.12 = (bf16[16,128,128]{2,1,0:T(8,128)(2,1)S(1)}, bf16[16,128,128]{2,1,0:T(8,128)(2,1)S(1)}, u32[]{:S(2)}, u32[]{:S(2)}) collective-permute-start(bf16[16,128,128]{2,1,0:T(8,128)(2,1)S(1)} %collective-permute-done.3.rest_1_), channel_id=1, source_target_pairs={{0,1},{1,0},{2,3},{3,2},{4,5},{5,4},{6,7},{7,6},{8,9},{9,8},{10,11... | collective-permute-start | bytes 1572872 | tf_op jit(solution)/shard_map/ppermute | solution.py:303
  142.9 0.8 copy-start.1

commit v8 on v7

--- a/solution.py
+++ b/solution.py
@@ -176,13 +176,13 @@
 def final_kernel(
     bits, meta_keep, meta_recv, bounds, places, early, other, keep, recv, inbox, *rest
 ):
-    pieces, (near, out, acc, sent, band, mine, theirs, inverse, sem) = rest[:-9], rest[-9:]
+    pieces, (near, out, acc, sent, band, mine, theirs, inverse, held_near, held_out, sem, done) = (
+        rest[:-12],
+        rest[-12:],
+    )
     count = keep.shape[0]
     size = acc.shape[0]
-    loads = [
-        pltpu.make_async_copy(early, acc, sem.at[0]),
-        pltpu.make_async_copy(other, sent, sem.at[1]),
-    ]
+    loads = [pltpu.make_async_copy(early, acc, sem.at[0])]
     place = 0
     for order, piece in enumerate(pieces):
         part = band.at[pl.ds(place, piece.shape[0])]
@@ -190,7 +190,10 @@
         place += piece.shape[0]
     for load in loads:
         load.start()
-    inverses = pltpu.make_async_copy(inbox, inverse, sem.at[4 + len(pieces)])
+    others = [
+        pltpu.make_async_copy(other, sent, sem.at[1]),
+        pltpu.make_async_copy(inbox, inverse, sem.at[4 + len(pieces)]),
+    ]
     sides = ((meta_keep, keep, mine), (meta_recv, recv, theirs))
 
     def chunk_copy(side, chunk):
@@ -207,17 +210,17 @@
             return carry
 
         lax.fori_loop(bounds[side] // CHUNK, count // CHUNK, fetch, 0)
-    inverses.start()
-    for side in (0, 1):
+    for load in others:
+        load.start()
+    for load in loads:
+        load.wait()
+    for side, (meta_ref, keep_ref, held) in enumerate(sides):
 
         def settle(chunk, carry):
             chunk_copy(side, chunk).wait()
             return carry
 
         lax.fori_loop(bounds[side] // CHUNK, count // CHUNK, settle, 0)
-    for load in loads:
-        load.wait()
-    for side, (meta_ref, keep_ref, held) in enumerate(sides):
 
         def add(turn, carry):
             meta = meta_ref[turn]
@@ -235,17 +238,29 @@
         even = (first + 7) // 8
         lax.fori_loop(first, even * 8, add, 0)
         lax.fori_loop(even, count // 8, add_eight, 0)
-    inverses.wait()
+    for load in others:
+        load.wait()
 
     def apply(turn, carry):
         block = (acc[turn] + sent[turn].astype(jnp.float32)).astype(jnp.bfloat16)
-        near[turn] = block
-        out[turn] = jnp.dot(
+        held_near[turn] = block
+        held_out[turn] = jnp.dot(
             inverse[places[turn]], block, preferred_element_type=jnp.float32
         ).astype(jnp.bfloat16)
         return carry
 
-    lax.fori_loop(0, size, apply, 0, unroll=16)
+    stores = []
+    share = math.gcd(size, CHUNK)
+    for order, start in enumerate(range(0, size, share)):
+        lax.fori_loop(start, start + share, apply, 0, unroll=True)
+        part = pl.ds(start, share)
+        for side, (held, whole) in enumerate(((held_near, near), (held_out, out))):
+            stores.append(
+                pltpu.make_async_copy(held.at[part], whole.at[part], done.at[2 * order + side])
+            )
+            stores[-1].start()
+    for store in stores:
+        store.wait()
 
 
 def final(
@@ -257,7 +272,7 @@
         functools.partial(final_kernel, bits),
         out_shape=(jax.ShapeDtypeStruct(block, jnp.bfloat16),) * 2,
         in_specs=[SMEM] * 4 + [HBM] * (5 + len(pieces)),
-        out_specs=(VMEM, VMEM),
+        out_specs=(HBM, HBM),
         scratch_shapes=[
             pltpu.VMEM(block, jnp.float32),
             pltpu.VMEM(block, jnp.bfloat16),
@@ -265,7 +280,10 @@
             held,
             held,
             pltpu.VMEM(inbox.shape, jnp.bfloat16),
+            pltpu.VMEM(block, jnp.bfloat16),
+            pltpu.VMEM(block, jnp.bfloat16),
             pltpu.SemaphoreType.DMA((5 + len(pieces),)),
+            pltpu.SemaphoreType.DMA((2 * block[0] // math.gcd(block[0], CHUNK),)),
         ],
         compiler_params=params(63),
         cost_estimate=cost(3 * keep.size * block[2], 22),

time: 156 us -> 155 us (level)
  no operation moved by 1% of the time
where the time goes in v8:
time: 155 us
  waiting for transfers between devices  67.9 us (44%)
  Pallas kernels  56.9 us (37%)
  starting transfers between devices  18.4 us (12%)
  other arithmetic  8.04 us (5%)
  local copies, waits for them, and re-layouts  2.5 us (2%)
    ppermute x13, waiting for transfers between devices, permute(): return lax.ppermute(value, AXES, pairs)  67.9 us
    pallas_call x2, Pallas kernels, sums(): pl.pallas_call(functools.partial(sums_kernel, bits, whole), out_shape=jax...  26 us
    pallas_call x3, Pallas kernels, gather_tiles(): pl.pallas_call(functools.partial(gather_kernel, first), out_shape=(jax.Sh...  17.4 us
    ppermute x13, starting transfers between devices, permute(): return lax.ppermute(value, AXES, pairs)  12.2 us
    pallas_call x1, Pallas kernels, final(): pl.pallas_call(functools.partial(final_kernel, bits), out_shape=(jax.Shap...  10.8 us
    all_to_all x1, starting transfers between devices, exchange(): return lax.all_to_all(value, AXES, split_axis=0, concat_axis=0, tiled=True)  6.16 us
  transfers between devices with their start and end apart: 14, of which 6 were waited for; matrix products, arithmetic and copies ran while one was open for 6% of the time, Pallas kernels for 30%

profile of v8, /device:TPU:15, one launch (start us, length us, event | category | flops | bytes accessed | tf_op | source)
XLA Modules:
  0.0 154.5 jit_solution(14939641598048811035)
XLA Ops:
  0.6 0.3 collective-permute-start
  0.9 3.1 %collective-permute-start.1 = (bf16[64,128,128]{2,1,0:T(8,128)(2,1)}, bf16[64,128,128]{2,1,0:T(8,128)(2,1)}, u32[]{:S(2)}, u32[]{:S(2)}) collective-permute-start(bf16[64,128,128]{2,1,0:T(8,128)(2,1)} %bitcast.9), channel_id=1, source_target_pairs={{4,0},{8,4},{12,8},{16,12},{20,16},{24,20},{28,24},{5,1},{9,5},{13... | collective-permute-start | bytes 6291464 | tf_op jit(solution)/shard_map/ppermute | solution.py:321
  4.1 0.8 and_select_fusion.8
  4.9 0.2 convert_reduce_fusion.2
  5.1 0.7 select_reduce_fusion.3.order_ref
  5.8 0.8 iota_add_fusion.1
  6.6 0.7 convert_reduce_fusion.4
  7.4 0.2 convert_reduce_fusion
  7.6 0.9 select_reduce_fusion
  8.6 3.5 %pack_inverses.1 = bf16[64,128,128]{2,1,0:T(8,128)(2,1)} custom-call(s32[64]{0:T(128)} %select_reduce_fusion.3.order_ref, bf16[64,128,128]{2,1,0:T(8,128)(2,1)} %tiles.3), custom_call_target="tpu_custom_call" | custom-call | bytes 8388608 | tf_op jit(solution)/shard_map/pack_inverses/pallas_call | solution.py:53
  12.1 0.0 copy-start.2
  12.1 7.0 %pack_send.1 = (bf16[128,128,128]{2,1,0:T(8,128)(2,1)}, bf16[128,128,128]{2,1,0:T(8,128)(2,1)}) custom-call(s32[512]{0:T(512)} %get-tuple-element.27.order_ref, bf16[512,128,128]{2,1,0:T(8,128)(2,1)} %tiles.5), custom_call_target="tpu_custom_call" | custom-call | bytes 33554432 | tf_op jit(solution)/shard_map/pack_send/pallas_call | solution.py:53
  19.1 1.3 collective-permute-start.8
  20.4 0.1 collective-permute-start.5
  20.5 0.6 pad_add_fusion
  21.1 0.4 collective-permute-start.2
  21.6 0.0 copy-done.2
  21.6 0.2 select_reduce_fusion.2
  21.8 5.4 %collective-permute-done.2 = s32[384]{0:T(512)S(1)} collective-permute-done((s32[384]{0:T(512)S(1)}, s32[384]{0:T(512)S(1)}, u32[]{:S(2)}, u32[]{:S(2)}) %collective-permute-start.2) | collective-permute-done | bytes 1568 | tf_op jit(solution)/shard_map/ppermute | solution.py:321
  27.2 0.4 collective-permute-start.6
  27.6 6.9 %pack_keep.1 = (bf16[128,128,128]{2,1,0:T(8,128)(2,1)}, bf16[128,128,128]{2,1,0:T(8,128)(2,1)}) custom-call(s32[512]{0:T(512)} %get-tuple-element.27.order_ref, bf16[512,128,128]{2,1,0:T(8,128)(2,1)} %tiles.5), custom_call_target="tpu_custom_call" | custom-call | bytes 33554432 | tf_op jit(solution)/shard_map/pack_keep/pallas_call | solution.py:53
  34.5 0.2 convert_reduce_fusion.1
  34.7 0.6 multiply_add_fusion.places
  35.3 0.6 fusion.17
  35.9 0.5 slice.27
  36.4 1.9 %pad_add_fusion.1.bounds = s32[2]{0:T(128)} fusion(s32[1]{0:T(128)} %slice.27, s32[1]{0:T(128)} %bitcast.4), kind=kLoop, calls=%fused_computation.99 | loop fusion | flops 2 | bytes 16 | tf_op jit(solution)/shard_map/concatenate | solution.py:398
  38.3 0.6 fusion.16
  38.9 8.6 %collective-permute-done.first.rest_2_ = bf16[64,128,128]{2,1,0:T(8,128)(2,1)} collective-permute-done((bf16[64,128,128]{2,1,0:T(8,128)(2,1)}, bf16[64,128,128]{2,1,0:T(8,128)(2,1)}, u32[]{:S(2)}, u32[]{:S(2)}) %collective-permute-start) | collective-permute-done | bytes 2097184 | tf_op jit(solution)/shard_map/ppermute | solution.py:321
  47.5 1.8 %collective-permute-done.1.second.rest_4_ = bf16[64,128,128]{2,1,0:T(8,128)(2,1)} collective-permute-done((bf16[64,128,128]{2,1,0:T(8,128)(2,1)}, bf16[64,128,128]{2,1,0:T(8,128)(2,1)}, u32[]{:S(2)}, u32[]{:S(2)}) %collective-permute-start.1) | collective-permute-done | bytes 2097184 | tf_op jit(solution)/shard_map/ppermute | solution.py:321
  49.3 1.9 %collective-permute-start.7 = (bf16[64,128,128]{2,1,0:T(8,128)(2,1)}, bf16[64,128,128]{2,1,0:T(8,128)(2,1)}, u32[]{:S(2)}, u32[]{:S(2)}) collective-permute-start(bf16[64,128,128]{2,1,0:T(8,128)(2,1)} %collective-permute-done.first.rest_2_), channel_id=1, source_target_pairs={{0,1},{1,0},{2,3},{3,2},{4,5},{5,4},{6,7},{7,6},{8,9},{9,8},{10,11... | collective-permute-start | bytes 6291464 | tf_op jit(solution)/shard_map/ppermute | solution.py:321
  51.2 0.0 collective-permute-start.9
  51.2 6.2 %all-to-all-start = ((bf16[64,128,128]{2,1,0:T(8,128)(2,1)}), bf16[64,128,128]{2,1,0:T(8,128)(2,1)}, u32[]{:S(2)}, u32[]{:S(2)}) async-start(bf16[64,128,128]{2,1,0:T(8,128)(2,1)} %pack_inverses.1), calls=%async_computation | async-start | bytes 4194304 | tf_op jit(solution)/shard_map/all_to_all | solution.py:358
  57.4 2.7 %split.1 = (bf16[48,128,128]{2,1,0:T(8,128)(2,1)}, bf16[16,128,128]{2,1,0:T(8,128)(2,1)}) custom-call(bf16[64,128,128]{2,1,0:T(8,128)(2,1)} %collective-permute-done.first.rest_2_, bf16[64,128,128]{2,1,0:T(8,128)(2,1)} %collective-permute-done.1.second.rest_4_), custom_call_target="tpu_custom_call" | custom-call | bytes 4194304 | tf_op jit(solution)/shard_map/split/pallas_call | solution.py:89
  60.1 0.0 collective-permute-done.6.rest_1_
  60.1 2.2 %collective-permute-start.4 = (bf16[48,128,128]{2,1,0:T(8,128)(2,1)}, bf16[48,128,128]{2,1,0:T(8,128)(2,1)}, u32[]{:S(2)}, u32[]{:S(2)}) collective-permute-start(bf16[48,128,128]{2,1,0:T(8,128)(2,1)} %get-tuple-element.39), channel_id=1, source_target_pairs={{0,4},{4,8},{8,12},{12,16},{16,20},{20,24},{24,28},{1,5},{5,9},{9,... | collective-permute-start | bytes 4718600 | tf_op jit(solution)/shard_map/ppermute | solution.py:321
  62.3 0.0 collective-permute-done.8.recv
  62.3 1.3 collective-permute-start.3
  63.6 0.0 collective-permute-done.7.rest_3_
  63.6 0.0 collective-permute-done.9.rest_5_
  63.6 13.0 %cross.1 = bf16[64,128,128]{2,1,0:T(8,128)(2,1)} custom-call(s32[128]{0:T(128)} %get-tuple-element.43.meta_keep, s32[128]{0:T(128)} %get-tuple-element.44.meta_recv, s32[2]{0:T(128)} %pad_add_fusion.1.bounds, bf16[128,128,128]{2,1,0:T(8,128)(2,1)} %get-tuple-element.45.keep, bf16[128,128,128]{2,1,0:T(8,128)(2,1)} %collective-permute-done.8.recv, ...), custom_call_target="tpu_custom_call" | custom-call | flops 1073741824 | bytes 25165824 | tf_op jit(solution)/shard_map/cross/pallas_call | solution.py:158
  76.6 0.4 collective-permute-start.10
  77.0 12.3 %collective-permute-done.3.rest_1_ = bf16[16,128,128]{2,1,0:T(8,128)(2,1)S(1)} collective-permute-done((bf16[16,128,128]{2,1,0:T(8,128)(2,1)}, bf16[16,128,128]{2,1,0:T(8,128)(2,1)S(1)}, u32[]{:S(2)}, u32[]{:S(2)}) %collective-permute-start.3) | collective-permute-done | bytes 524320 | tf_op jit(solution)/shard_map/ppermute | solution.py:321
  89.3 0.0 copy-start
  89.3 0.0 collective-permute-done.5.recv
  89.3 13.0 %own.1.early = f32[64,128,128]{2,1,0:T(8,128)} custom-call(s32[128]{0:T(128)} %get-tuple-element.35.meta_keep, s32[128]{0:T(128)} %get-tuple-element.36.meta_recv, s32[2]{0:T(128)} %pad_add_fusion.1.bounds, bf16[128,128,128]{2,1,0:T(8,128)(2,1)} %get-tuple-element.40.keep, bf16[128,128,128]{2,1,0:T(8,128)(2,1)} %collective-permute-done.5.recv, ...), custom_call_target="tpu_custom_call" | custom-call | flops 1073741824 | bytes 25165824 | tf_op jit(solution)/shard_map/own/pallas_call | solution.py:158
  102.3 36.1 %collective-permute-done.4.rest_0_ = bf16[48,128,128]{2,1,0:T(8,128)(2,1)} collective-permute-done((bf16[48,128,128]{2,1,0:T(8,128)(2,1)}, bf16[48,128,128]{2,1,0:T(8,128)(2,1)}, u32[]{:S(2)}, u32[]{:S(2)}) %collective-permute-start.4) | collective-permute-done | bytes 1572896 | tf_op jit(solution)/shard_map/ppermute | solution.py:321
  138.4 0.9 collective-permute-start.11
  139.3 0.0 copy-done
  139.3 0.0 collective-permute-start.12
  139.3 3.6 %collective-permute-done.12.rest_3_ = bf16[16,128,128]{2,1,0:T(8,128)(2,1)S(1)} collective-permute-done((bf16[16,128,128]{2,1,0:T(8,128)(2,1)S(1)}, bf16[16,128,128]{2,1,0:T(8,128)(2,1)S(1)}, u32[]{:S(2)}, u32[]{:S(2)}) %collective-permute-start.12) | collective-permute-done | bytes 524320 | tf_op jit(solution)/shard_map/ppermute | solution.py:321
  142.9 0.0 copy-start.1
  142.9 0.8 copy-done.1
  143.7 0.0 collective-permute-done.11.rest_2_
  143.7 0.0 all-to-all-done.inbox
  143.7 0.0 collective-permute-done.10.other
  143.7 10.8 %final.1 = (bf16[64,128,128]{2,1,0:T(8,128)(2,1)}, bf16[64,128,128]{2,1,0:T(8,128)(2,1)}) custom-call(s32[128]{0:T(128)} %get-tuple-element.35.meta_keep, s32[128]{0:T(128)} %get-tuple-element.36.meta_recv, s32[2]{0:T(128)} %pad_add_fusion.1.bounds, s32[64]{0:T(128)} %multiply_add_fusion.places, f32[64,128,128]{2,1,0:T(8,128)} %own.1.early, ...), custom_call_target="tpu_custom_call" | custom-call | flops 805306368 | bytes 23068672 | tf_op jit(solution)/shard_map/final/pallas_call | solution.py:271
  (7 shorter events, 0.1 us)
Async XLA Ops:
  0.6 46.9 %collective-permute-start = (bf16[64,128,128]{2,1,0:T(8,128)(2,1)}, bf16[64,128,128]{2,1,0:T(8,128)(2,1)}, u32[]{:S(2)}, u32[]{:S(2)}) collective-permute-start(bf16[64,128,128]{2,1,0:T(8,128)(2,1)} %bitcast.8), channel_id=1, source_target_pairs={{0,2},{1,3},{2,0},{3,1},{4,6},{5,7},{6,4},{7,5},{8,10},{9,11},{10,... | collective-permute-start | bytes 6291464 | tf_op jit(solution)/shard_map/ppermute | solution.py:321
  0.9 48.4 %collective-permute-start.1 = (bf16[64,128,128]{2,1,0:T(8,128)(2,1)}, bf16[64,128,128]{2,1,0:T(8,128)(2,1)}, u32[]{:S(2)}, u32[]{:S(2)}) collective-permute-start(bf16[64,128,128]{2,1,0:T(8,128)(2,1)} %bitcast.9), channel_id=1, source_target_pairs={{4,0},{8,4},{12,8},{16,12},{20,16},{24,20},{28,24},{5,1},{9,5},{13... | collective-permute-start | bytes 6291464 | tf_op jit(solution)/shard_map/ppermute | solution.py:321
  12.1 9.5 %copy-start.2 = (s32[2048]{0:T(1024)S(1)}, s32[2048]{0:T(1024)}, u32[]{:S(2)}) copy-start(s32[2048]{0:T(1024)} %param.9) | copy-start | bytes 24580
  19.1 43.2 %collective-permute-start.8 = (bf16[128,128,128]{2,1,0:T(8,128)(2,1)}, bf16[128,128,128]{2,1,0:T(8,128)(2,1)}, u32[]{:S(2)}, u32[]{:S(2)}) collective-permute-start(bf16[128,128,128]{2,1,0:T(8,128)(2,1)} %get-tuple-element.46), channel_id=1, source_target_pairs={{0,1},{1,0},{2,3},{3,2},{4,5},{5,4},{6,7},{7,6},{8,9},{9,8},{10,11... | collective-permute-start | bytes 12582920 | tf_op jit(solution)/shard_map/ppermute | solution.py:321
  20.4 68.9 %collective-permute-start.5 = (bf16[128,128,128]{2,1,0:T(8,128)(2,1)}, bf16[128,128,128]{2,1,0:T(8,128)(2,1)}, u32[]{:S(2)}, u32[]{:S(2)}) collective-permute-start(bf16[128,128,128]{2,1,0:T(8,128)(2,1)} %get-tuple-element.41), channel_id=1, source_target_pairs={{0,1},{1,0},{2,3},{3,2},{4,5},{5,4},{6,7},{7,6},{8,9},{9,8},{10,11... | collective-permute-start | bytes 12582920 | tf_op jit(solution)/shard_map/ppermute | solution.py:321
  21.1 6.1 %collective-permute-start.2 = (s32[384]{0:T(512)S(1)}, s32[384]{0:T(512)S(1)}, u32[]{:S(2)}, u32[]{:S(2)}) collective-permute-start(s32[384]{0:T(512)S(1)} %pad_add_fusion), channel_id=1, source_target_pairs={{0,1},{1,0},{2,3},{3,2},{4,5},{5,4},{6,7},{7,6},{8,9},{9,8},{10,11... | collective-permute-start | bytes 4616 | tf_op jit(solution)/shard_map/ppermute | solution.py:321
  27.2 32.9 %collective-permute-start.6 = (bf16[64,128,128]{2,1,0:T(8,128)(2,1)}, bf16[64,128,128]{2,1,0:T(8,128)(2,1)}, u32[]{:S(2)}, u32[]{:S(2)}) collective-permute-start(bf16[64,128,128]{2,1,0:T(8,128)(2,1)} %bitcast.10), channel_id=1, source_target_pairs={{0,1},{1,0},{2,3},{3,2},{4,5},{5,4},{6,7},{7,6},{8,9},{9,8},{10,11... | collective-permute-start | bytes 6291464 | tf_op jit(solution)/shard_map/ppermute | solution.py:321
  49.3 14.3 %collective-permute-start.7 = (bf16[64,128,128]{2,1,0:T(8,128)(2,1)}, bf16[64,128,128]{2,1,0:T(8,128)(2,1)}, u32[]{:S(2)}, u32[]{:S(2)}) collective-permute-start(bf16[64,128,128]{2,1,0:T(8,128)(2,1)} %collective-permute-done.first.rest_2_), channel_id=1, source_target_pairs={{0,1},{1,0},{2,3},{3,2},{4,5},{5,4},{6,7},{7,6},{8,9},{9,8},{10,11... | collective-permute-start | bytes 6291464 | tf_op jit(solution)/shard_map/ppermute | solution.py:321
  51.2 12.4 %collective-permute-start.9 = (bf16[64,128,128]{2,1,0:T(8,128)(2,1)}, bf16[64,128,128]{2,1,0:T(8,128)(2,1)}, u32[]{:S(2)}, u32[]{:S(2)}) collective-permute-start(bf16[64,128,128]{2,1,0:T(8,128)(2,1)} %collective-permute-done.1.second.rest_4_), channel_id=1, source_target_pairs={{0,1},{1,0},{2,3},{3,2},{4,5},{5,4},{6,7},{7,6},{8,9},{9,8},{10,11... | collective-permute-start | bytes 6291464 | tf_op jit(solution)/shard_map/ppermute | solution.py:321
  51.2 92.5 %all-to-all-start = ((bf16[64,128,128]{2,1,0:T(8,128)(2,1)}), bf16[64,128,128]{2,1,0:T(8,128)(2,1)}, u32[]{:S(2)}, u32[]{:S(2)}) async-start(bf16[64,128,128]{2,1,0:T(8,128)(2,1)} %pack_inverses.1), calls=%async_computation | async-start | bytes 4194304 | tf_op jit(solution)/shard_map/all_to_all | solution.py:358
  60.1 78.2 %collective-permute-start.4 = (bf16[48,128,128]{2,1,0:T(8,128)(2,1)}, bf16[48,128,128]{2,1,0:T(8,128)(2,1)}, u32[]{:S(2)}, u32[]{:S(2)}) collective-permute-start(bf16[48,128,128]{2,1,0:T(8,128)(2,1)} %get-tuple-element.39), channel_id=1, source_target_pairs={{0,4},{4,8},{8,12},{12,16},{16,20},{20,24},{24,28},{1,5},{5,9},{9,... | collective-permute-start | bytes 4718600 | tf_op jit(solution)/shard_map/ppermute | solution.py:321
  62.3 26.9 %collective-permute-start.3 = (bf16[16,128,128]{2,1,0:T(8,128)(2,1)}, bf16[16,128,128]{2,1,0:T(8,128)(2,1)S(1)}, u32[]{:S(2)}, u32[]{:S(2)}) collective-permute-start(bf16[16,128,128]{2,1,0:T(8,128)(2,1)} %get-tuple-element.34), channel_id=1, source_target_pairs={{0,2},{1,3},{2,0},{3,1},{4,6},{5,7},{6,4},{7,5},{8,10},{9,11},{10,... | collective-permute-start | bytes 1572872 | tf_op jit(solution)/shard_map/ppermute | solution.py:321
  76.6 67.1 %collective-permute-start.10 = (bf16[64,128,128]{2,1,0:T(8,128)(2,1)}, bf16[64,128,128]{2,1,0:T(8,128)(2,1)}, u32[]{:S(2)}, u32[]{:S(2)}) collective-permute-start(bf16[64,128,128]{2,1,0:T(8,128)(2,1)} %cross.1), channel_id=1, source_target_pairs={{0,2},{1,3},{2,0},{3,1},{4,6},{5,7},{6,4},{7,5},{8,10},{9,11},{10,... | collective-permute-start | bytes 6291464 | tf_op jit(solution)/shard_map/ppermute | solution.py:321
  89.3 50.0 %copy-start = (bf16[16,128,128]{2,1,0:T(8,128)(2,1)}, bf16[16,128,128]{2,1,0:T(8,128)(2,1)S(1)}, u32[]{:S(2)}) copy-start(bf16[16,128,128]{2,1,0:T(8,128)(2,1)S(1)} %collective-permute-done.3.rest_1_) | copy-start | bytes 1572868
  138.4 5.3 %collective-permute-start.11 = (bf16[48,128,128]{2,1,0:T(8,128)(2,1)}, bf16[48,128,128]{2,1,0:T(8,128)(2,1)}, u32[]{:S(2)}, u32[]{:S(2)}) collective-permute-start(bf16[48,128,128]{2,1,0:T(8,128)(2,1)} %collective-permute-done.4.rest_0_), channel_id=1, source_target_pairs={{0,1},{1,0},{2,3},{3,2},{4,5},{5,4},{6,7},{7,6},{8,9},{9,8},{10,11... | collective-permute-start | bytes 4718600 | tf_op jit(solution)/shard_map/ppermute | solution.py:321
  139.3 3.6 %collective-permute-start.12 = (bf16[16,128,128]{2,1,0:T(8,128)(2,1)S(1)}, bf16[16,128,128]{2,1,0:T(8,128)(2,1)S(1)}, u32[]{:S(2)}, u32[]{:S(2)}) collective-permute-start(bf16[16,128,128]{2,1,0:T(8,128)(2,1)S(1)} %collective-permute-done.3.rest_1_), channel_id=1, source_target_pairs={{0,1},{1,0},{2,3},{3,2},{4,5},{5,4},{6,7},{7,6},{8,9},{9,8},{10,11... | collective-permute-start | bytes 1572872 | tf_op jit(solution)/shard_map/ppermute | solution.py:321
  142.9 0.8 copy-start.1

commit v9 on v8

--- a/solution.py
+++ b/solution.py
@@ -430,7 +430,7 @@
     )
 
     other_beside = permute(other_chip, beside)
-    cut = own - own // 4
+    cut = own - 3 * own // 8
     late_part, across_part = split(cut, other_chip, halo_early)
     halo_late = permute(late_part, late)
     halo_across = permute(across_part, across)

time: 155 us -> 155 us (level)
  the two profiles are of different devices: /device:TPU:15 before, /device:TPU:7 now
where the time goes in v9:
time: 155 us; the launch traced here: 153 us
  waiting for transfers between devices  66.5 us (43%)
  Pallas kernels  56.8 us (37%)
  starting transfers between devices  18.5 us (12%)
  other arithmetic  7.93 us (5%)
  local copies, waits for them, and re-layouts  2.56 us (2%)
    ppermute x13, waiting for transfers between devices, permute(): return lax.ppermute(value, AXES, pairs)  66.5 us
    pallas_call x2, Pallas kernels, sums(): pl.pallas_call(functools.partial(sums_kernel, bits, whole), out_shape=jax...  26.7 us
    pallas_call x3, Pallas kernels, gather_tiles(): pl.pallas_call(functools.partial(gather_kernel, first), out_shape=(jax.Sh...  17.4 us
    ppermute x13, starting transfers between devices, permute(): return lax.ppermute(value, AXES, pairs)  12.2 us
    pallas_call x1, Pallas kernels, final(): pl.pallas_call(functools.partial(final_kernel, bits), out_shape=(jax.Shap...  10 us
    all_to_all x1, starting transfers between devices, exchange(): return lax.all_to_all(value, AXES, split_axis=0, concat_axis=0, tiled=True)  6.27 us
  transfers between devices with their start and end apart: 14, of which 7 were waited for; matrix products, arithmetic and copies ran while one was open for 6% of the time, Pallas kernels for 31%

profile of v9, /device:TPU:7, one launch (start us, length us, event | category | flops | bytes accessed | tf_op | source)
XLA Modules:
  0.0 153.0 jit_solution(8668965956846038457)
XLA Ops:
  0.6 0.3 collective-permute-start
  0.9 3.1 %collective-permute-start.1 = (bf16[64,128,128]{2,1,0:T(8,128)(2,1)}, bf16[64,128,128]{2,1,0:T(8,128)(2,1)}, u32[]{:S(2)}, u32[]{:S(2)}) collective-permute-start(bf16[64,128,128]{2,1,0:T(8,128)(2,1)} %bitcast.9), channel_id=1, source_target_pairs={{4,0},{8,4},{12,8},{16,12},{20,16},{24,20},{28,24},{5,1},{9,5},{13... | collective-permute-start | bytes 6291464 | tf_op jit(solution)/shard_map/ppermute | solution.py:321
  4.1 0.8 and_select_fusion.8
  4.9 0.2 convert_reduce_fusion.2
  5.1 0.7 select_reduce_fusion.3.order_ref
  5.8 0.8 iota_add_fusion.1
  6.6 0.7 convert_reduce_fusion.4
  7.4 0.2 convert_reduce_fusion
  7.6 0.9 select_reduce_fusion
  8.6 3.5 %pack_inverses.1 = bf16[64,128,128]{2,1,0:T(8,128)(2,1)} custom-call(s32[64]{0:T(128)} %select_reduce_fusion.3.order_ref, bf16[64,128,128]{2,1,0:T(8,128)(2,1)} %tiles.3), custom_call_target="tpu_custom_call" | custom-call | bytes 8388608 | tf_op jit(solution)/shard_map/pack_inverses/pallas_call | solution.py:53
  12.1 0.0 copy-start.2
  12.1 7.0 %pack_send.1 = (bf16[128,128,128]{2,1,0:T(8,128)(2,1)}, bf16[128,128,128]{2,1,0:T(8,128)(2,1)}) custom-call(s32[512]{0:T(512)} %get-tuple-element.27.order_ref, bf16[512,128,128]{2,1,0:T(8,128)(2,1)} %tiles.5), custom_call_target="tpu_custom_call" | custom-call | bytes 33554432 | tf_op jit(solution)/shard_map/pack_send/pallas_call | solution.py:53
  19.1 1.3 collective-permute-start.8
  20.4 0.7 pad_add_fusion
  21.1 0.0 collective-permute-start.2
  21.2 0.5 collective-permute-start.5
  21.7 0.0 copy-done.2
  21.7 0.2 select_reduce_fusion.2
  21.9 0.5 fusion.17
  22.4 0.2 convert_reduce_fusion.1
  22.6 4.6 %collective-permute-done.2 = s32[384]{0:T(512)S(1)} collective-permute-done((s32[384]{0:T(512)S(1)}, s32[384]{0:T(512)S(1)}, u32[]{:S(2)}, u32[]{:S(2)}) %collective-permute-start.2) | collective-permute-done | bytes 1568 | tf_op jit(solution)/shard_map/ppermute | solution.py:321
  27.2 0.4 collective-permute-start.6
  27.5 0.5 multiply_add_fusion.places
  28.1 6.9 %pack_keep.1 = (bf16[128,128,128]{2,1,0:T(8,128)(2,1)}, bf16[128,128,128]{2,1,0:T(8,128)(2,1)}) custom-call(s32[512]{0:T(512)} %get-tuple-element.27.order_ref, bf16[512,128,128]{2,1,0:T(8,128)(2,1)} %tiles.5), custom_call_target="tpu_custom_call" | custom-call | bytes 33554432 | tf_op jit(solution)/shard_map/pack_keep/pallas_call | solution.py:53
  35.0 0.5 slice.27
  35.5 1.8 %pad_add_fusion.1.bounds = s32[2]{0:T(128)} fusion(s32[1]{0:T(128)} %slice.27, s32[1]{0:T(128)} %bitcast.4), kind=kLoop, calls=%fused_computation.99 | loop fusion | flops 2 | bytes 16 | tf_op jit(solution)/shard_map/concatenate | solution.py:398
  37.3 0.6 fusion.16
  37.9 9.6 %collective-permute-done.first.rest_2_ = bf16[64,128,128]{2,1,0:T(8,128)(2,1)} collective-permute-done((bf16[64,128,128]{2,1,0:T(8,128)(2,1)}, bf16[64,128,128]{2,1,0:T(8,128)(2,1)}, u32[]{:S(2)}, u32[]{:S(2)}) %collective-permute-start) | collective-permute-done | bytes 2097184 | tf_op jit(solution)/shard_map/ppermute | solution.py:321
  47.5 1.8 %collective-permute-done.1.second.rest_4_ = bf16[64,128,128]{2,1,0:T(8,128)(2,1)} collective-permute-done((bf16[64,128,128]{2,1,0:T(8,128)(2,1)}, bf16[64,128,128]{2,1,0:T(8,128)(2,1)}, u32[]{:S(2)}, u32[]{:S(2)}) %collective-permute-start.1) | collective-permute-done | bytes 2097184 | tf_op jit(solution)/shard_map/ppermute | solution.py:321
  49.3 1.9 %collective-permute-start.7 = (bf16[64,128,128]{2,1,0:T(8,128)(2,1)}, bf16[64,128,128]{2,1,0:T(8,128)(2,1)}, u32[]{:S(2)}, u32[]{:S(2)}) collective-permute-start(bf16[64,128,128]{2,1,0:T(8,128)(2,1)} %collective-permute-done.first.rest_2_), channel_id=1, source_target_pairs={{0,1},{1,0},{2,3},{3,2},{4,5},{5,4},{6,7},{7,6},{8,9},{9,8},{10,11... | collective-permute-start | bytes 6291464 | tf_op jit(solution)/shard_map/ppermute | solution.py:321
  51.2 0.0 collective-permute-start.9
  51.2 6.3 %all-to-all-start = ((bf16[64,128,128]{2,1,0:T(8,128)(2,1)}), bf16[64,128,128]{2,1,0:T(8,128)(2,1)}, u32[]{:S(2)}, u32[]{:S(2)}) async-start(bf16[64,128,128]{2,1,0:T(8,128)(2,1)} %pack_inverses.1), calls=%async_computation | async-start | bytes 4194304 | tf_op jit(solution)/shard_map/all_to_all | solution.py:358
  57.5 2.7 %split.1 = (bf16[40,128,128]{2,1,0:T(8,128)(2,1)}, bf16[24,128,128]{2,1,0:T(8,128)(2,1)}) custom-call(bf16[64,128,128]{2,1,0:T(8,128)(2,1)} %collective-permute-done.first.rest_2_, bf16[64,128,128]{2,1,0:T(8,128)(2,1)} %collective-permute-done.1.second.rest_4_), custom_call_target="tpu_custom_call" | custom-call | bytes 4194304 | tf_op jit(solution)/shard_map/split/pallas_call | solution.py:89
  60.1 0.0 collective-permute-done.6.rest_1_
  60.2 2.2 %collective-permute-start.4 = (bf16[40,128,128]{2,1,0:T(8,128)(2,1)}, bf16[40,128,128]{2,1,0:T(8,128)(2,1)}, u32[]{:S(2)}, u32[]{:S(2)}) collective-permute-start(bf16[40,128,128]{2,1,0:T(8,128)(2,1)} %get-tuple-element.39), channel_id=1, source_target_pairs={{0,4},{4,8},{8,12},{12,16},{16,20},{20,24},{24,28},{1,5},{5,9},{9,... | collective-permute-start | bytes 3932168 | tf_op jit(solution)/shard_map/ppermute | solution.py:321
  62.4 0.0 collective-permute-done.8.recv
  62.4 1.3 collective-permute-start.3
  63.6 0.0 collective-permute-done.7.rest_3_
  63.6 0.0 collective-permute-done.9.rest_5_
  63.6 13.0 %cross.1 = bf16[64,128,128]{2,1,0:T(8,128)(2,1)} custom-call(s32[128]{0:T(128)} %get-tuple-element.43.meta_keep, s32[128]{0:T(128)} %get-tuple-element.44.meta_recv, s32[2]{0:T(128)} %pad_add_fusion.1.bounds, bf16[128,128,128]{2,1,0:T(8,128)(2,1)} %get-tuple-element.45.keep, bf16[128,128,128]{2,1,0:T(8,128)(2,1)} %collective-permute-done.8.recv, ...), custom_call_target="tpu_custom_call" | custom-call | flops 1073741824 | bytes 25165824 | tf_op jit(solution)/shard_map/cross/pallas_call | solution.py:158
  76.6 0.4 collective-permute-start.10
  77.0 18.2 %collective-permute-done.3.rest_1_ = bf16[24,128,128]{2,1,0:T(8,128)(2,1)S(1)} collective-permute-done((bf16[24,128,128]{2,1,0:T(8,128)(2,1)}, bf16[24,128,128]{2,1,0:T(8,128)(2,1)S(1)}, u32[]{:S(2)}, u32[]{:S(2)}) %collective-permute-start.3) | collective-permute-done | bytes 786464 | tf_op jit(solution)/shard_map/ppermute | solution.py:321
  95.2 0.0 copy-start
  95.2 0.0 collective-permute-done.5.recv
  95.2 13.7 %own.1.early = f32[64,128,128]{2,1,0:T(8,128)} custom-call(s32[128]{0:T(128)} %get-tuple-element.35.meta_keep, s32[128]{0:T(128)} %get-tuple-element.36.meta_recv, s32[2]{0:T(128)} %pad_add_fusion.1.bounds, bf16[128,128,128]{2,1,0:T(8,128)(2,1)} %get-tuple-element.40.keep, bf16[128,128,128]{2,1,0:T(8,128)(2,1)} %collective-permute-done.5.recv, ...), custom_call_target="tpu_custom_call" | custom-call | flops 1073741824 | bytes 25165824 | tf_op jit(solution)/shard_map/own/pallas_call | solution.py:158
  108.9 13.8 %collective-permute-done.4.rest_0_ = bf16[40,128,128]{2,1,0:T(8,128)(2,1)} collective-permute-done((bf16[40,128,128]{2,1,0:T(8,128)(2,1)}, bf16[40,128,128]{2,1,0:T(8,128)(2,1)}, u32[]{:S(2)}, u32[]{:S(2)}) %collective-permute-start.4) | collective-permute-done | bytes 1310752 | tf_op jit(solution)/shard_map/ppermute | solution.py:321
  122.7 0.9 collective-permute-start.11
  123.6 0.0 copy-done
  123.6 0.0 collective-permute-start.12
  123.6 3.6 %collective-permute-done.12.rest_3_ = bf16[24,128,128]{2,1,0:T(8,128)(2,1)S(1)} collective-permute-done((bf16[24,128,128]{2,1,0:T(8,128)(2,1)S(1)}, bf16[24,128,128]{2,1,0:T(8,128)(2,1)S(1)}, u32[]{:S(2)}, u32[]{:S(2)}) %collective-permute-start.12) | collective-permute-done | bytes 786464 | tf_op jit(solution)/shard_map/ppermute | solution.py:321
  127.3 0.0 copy-start.1
  127.3 0.9 copy-done.1
  128.2 0.0 collective-permute-done.11.rest_2_
  128.2 0.0 all-to-all-done.inbox
  128.2 14.8 %collective-permute-done.10.other = bf16[64,128,128]{2,1,0:T(8,128)(2,1)} collective-permute-done((bf16[64,128,128]{2,1,0:T(8,128)(2,1)}, bf16[64,128,128]{2,1,0:T(8,128)(2,1)}, u32[]{:S(2)}, u32[]{:S(2)}) %collective-permute-start.10) | collective-permute-done | bytes 2097184 | tf_op jit(solution)/shard_map/ppermute | solution.py:321
  142.9 10.0 %final.1 = (bf16[64,128,128]{2,1,0:T(8,128)(2,1)}, bf16[64,128,128]{2,1,0:T(8,128)(2,1)}) custom-call(s32[128]{0:T(128)} %get-tuple-element.35.meta_keep, s32[128]{0:T(128)} %get-tuple-element.36.meta_recv, s32[2]{0:T(128)} %pad_add_fusion.1.bounds, s32[64]{0:T(128)} %multiply_add_fusion.places, f32[64,128,128]{2,1,0:T(8,128)} %own.1.early, ...), custom_call_target="tpu_custom_call" | custom-call | flops 805306368 | bytes 23068672 | tf_op jit(solution)/shard_map/final/pallas_call | solution.py:271
  (7 shorter events, 0.1 us)
Async XLA Ops:
  0.6 46.9 %collective-permute-start = (bf16[64,128,128]{2,1,0:T(8,128)(2,1)}, bf16[64,128,128]{2,1,0:T(8,128)(2,1)}, u32[]{:S(2)}, u32[]{:S(2)}) collective-permute-start(bf16[64,128,128]{2,1,0:T(8,128)(2,1)} %bitcast.8), channel_id=1, source_target_pairs={{0,2},{1,3},{2,0},{3,1},{4,6},{5,7},{6,4},{7,5},{8,10},{9,11},{10,... | collective-permute-start | bytes 6291464 | tf_op jit(solution)/shard_map/ppermute | solution.py:321
  0.9 48.4 %collective-permute-start.1 = (bf16[64,128,128]{2,1,0:T(8,128)(2,1)}, bf16[64,128,128]{2,1,0:T(8,128)(2,1)}, u32[]{:S(2)}, u32[]{:S(2)}) collective-permute-start(bf16[64,128,128]{2,1,0:T(8,128)(2,1)} %bitcast.9), channel_id=1, source_target_pairs={{4,0},{8,4},{12,8},{16,12},{20,16},{24,20},{28,24},{5,1},{9,5},{13... | collective-permute-start | bytes 6291464 | tf_op jit(solution)/shard_map/ppermute | solution.py:321
  12.1 9.6 %copy-start.2 = (s32[2048]{0:T(1024)S(1)}, s32[2048]{0:T(1024)}, u32[]{:S(2)}) copy-start(s32[2048]{0:T(1024)} %param.9) | copy-start | bytes 24580
  19.1 43.3 %collective-permute-start.8 = (bf16[128,128,128]{2,1,0:T(8,128)(2,1)}, bf16[128,128,128]{2,1,0:T(8,128)(2,1)}, u32[]{:S(2)}, u32[]{:S(2)}) collective-permute-start(bf16[128,128,128]{2,1,0:T(8,128)(2,1)} %get-tuple-element.46), channel_id=1, source_target_pairs={{0,1},{1,0},{2,3},{3,2},{4,5},{5,4},{6,7},{7,6},{8,9},{9,8},{10,11... | collective-permute-start | bytes 12582920 | tf_op jit(solution)/shard_map/ppermute | solution.py:321
  21.1 6.0 %collective-permute-start.2 = (s32[384]{0:T(512)S(1)}, s32[384]{0:T(512)S(1)}, u32[]{:S(2)}, u32[]{:S(2)}) collective-permute-start(s32[384]{0:T(512)S(1)} %pad_add_fusion), channel_id=1, source_target_pairs={{0,1},{1,0},{2,3},{3,2},{4,5},{5,4},{6,7},{7,6},{8,9},{9,8},{10,11... | collective-permute-start | bytes 4616 | tf_op jit(solution)/shard_map/ppermute | solution.py:321
  21.2 74.0 %collective-permute-start.5 = (bf16[128,128,128]{2,1,0:T(8,128)(2,1)}, bf16[128,128,128]{2,1,0:T(8,128)(2,1)}, u32[]{:S(2)}, u32[]{:S(2)}) collective-permute-start(bf16[128,128,128]{2,1,0:T(8,128)(2,1)} %get-tuple-element.41), channel_id=1, source_target_pairs={{0,1},{1,0},{2,3},{3,2},{4,5},{5,4},{6,7},{7,6},{8,9},{9,8},{10,11... | collective-permute-start | bytes 12582920 | tf_op jit(solution)/shard_map/ppermute | solution.py:321
  27.2 33.0 %collective-permute-start.6 = (bf16[64,128,128]{2,1,0:T(8,128)(2,1)}, bf16[64,128,128]{2,1,0:T(8,128)(2,1)}, u32[]{:S(2)}, u32[]{:S(2)}) collective-permute-start(bf16[64,128,128]{2,1,0:T(8,128)(2,1)} %bitcast.10), channel_id=1, source_target_pairs={{0,1},{1,0},{2,3},{3,2},{4,5},{5,4},{6,7},{7,6},{8,9},{9,8},{10,11... | collective-permute-start | bytes 6291464 | tf_op jit(solution)/shard_map/ppermute | solution.py:321
  49.3 14.3 %collective-permute-start.7 = (bf16[64,128,128]{2,1,0:T(8,128)(2,1)}, bf16[64,128,128]{2,1,0:T(8,128)(2,1)}, u32[]{:S(2)}, u32[]{:S(2)}) collective-permute-start(bf16[64,128,128]{2,1,0:T(8,128)(2,1)} %collective-permute-done.first.rest_2_), channel_id=1, source_target_pairs={{0,1},{1,0},{2,3},{3,2},{4,5},{5,4},{6,7},{7,6},{8,9},{9,8},{10,11... | collective-permute-start | bytes 6291464 | tf_op jit(solution)/shard_map/ppermute | solution.py:321
  51.2 12.4 %collective-permute-start.9 = (bf16[64,128,128]{2,1,0:T(8,128)(2,1)}, bf16[64,128,128]{2,1,0:T(8,128)(2,1)}, u32[]{:S(2)}, u32[]{:S(2)}) collective-permute-start(bf16[64,128,128]{2,1,0:T(8,128)(2,1)} %collective-permute-done.1.second.rest_4_), channel_id=1, source_target_pairs={{0,1},{1,0},{2,3},{3,2},{4,5},{5,4},{6,7},{7,6},{8,9},{9,8},{10,11... | collective-permute-start | bytes 6291464 | tf_op jit(solution)/shard_map/ppermute | solution.py:321
  51.2 77.0 %all-to-all-start = ((bf16[64,128,128]{2,1,0:T(8,128)(2,1)}), bf16[64,128,128]{2,1,0:T(8,128)(2,1)}, u32[]{:S(2)}, u32[]{:S(2)}) async-start(bf16[64,128,128]{2,1,0:T(8,128)(2,1)} %pack_inverses.1), calls=%async_computation | async-start | bytes 4194304 | tf_op jit(solution)/shard_map/all_to_all | solution.py:358
  60.2 62.6 %collective-permute-start.4 = (bf16[40,128,128]{2,1,0:T(8,128)(2,1)}, bf16[40,128,128]{2,1,0:T(8,128)(2,1)}, u32[]{:S(2)}, u32[]{:S(2)}) collective-permute-start(bf16[40,128,128]{2,1,0:T(8,128)(2,1)} %get-tuple-element.39), channel_id=1, source_target_pairs={{0,4},{4,8},{8,12},{12,16},{16,20},{20,24},{24,28},{1,5},{5,9},{9,... | collective-permute-start | bytes 3932168 | tf_op jit(solution)/shard_map/ppermute | solution.py:321
  62.4 32.8 %collective-permute-start.3 = (bf16[24,128,128]{2,1,0:T(8,128)(2,1)}, bf16[24,128,128]{2,1,0:T(8,128)(2,1)S(1)}, u32[]{:S(2)}, u32[]{:S(2)}) collective-permute-start(bf16[24,128,128]{2,1,0:T(8,128)(2,1)} %get-tuple-element.34), channel_id=1, source_target_pairs={{0,2},{1,3},{2,0},{3,1},{4,6},{5,7},{6,4},{7,5},{8,10},{9,11},{10,... | collective-permute-start | bytes 2359304 | tf_op jit(solution)/shard_map/ppermute | solution.py:321
  76.6 66.3 %collective-permute-start.10 = (bf16[64,128,128]{2,1,0:T(8,128)(2,1)}, bf16[64,128,128]{2,1,0:T(8,128)(2,1)}, u32[]{:S(2)}, u32[]{:S(2)}) collective-permute-start(bf16[64,128,128]{2,1,0:T(8,128)(2,1)} %cross.1), channel_id=1, source_target_pairs={{0,2},{1,3},{2,0},{3,1},{4,6},{5,7},{6,4},{7,5},{8,10},{9,11},{10,... | collective-permute-start | bytes 6291464 | tf_op jit(solution)/shard_map/ppermute | solution.py:321
  95.2 28.4 %copy-start = (bf16[24,128,128]{2,1,0:T(8,128)(2,1)}, bf16[24,128,128]{2,1,0:T(8,128)(2,1)S(1)}, u32[]{:S(2)}) copy-start(bf16[24,128,128]{2,1,0:T(8,128)(2,1)S(1)} %collective-permute-done.3.rest_1_) | copy-start | bytes 2359300
  122.7 5.4 %collective-permute-start.11 = (bf16[40,128,128]{2,1,0:T(8,128)(2,1)}, bf16[40,128,128]{2,1,0:T(8,128)(2,1)}, u32[]{:S(2)}, u32[]{:S(2)}) collective-permute-start(bf16[40,128,128]{2,1,0:T(8,128)(2,1)} %collective-permute-done.4.rest_0_), channel_id=1, source_target_pairs={{0,1},{1,0},{2,3},{3,2},{4,5},{5,4},{6,7},{7,6},{8,9},{9,8},{10,11... | collective-permute-start | bytes 3932168 | tf_op jit(solution)/shard_map/ppermute | solution.py:321
  123.6 3.6 %collective-permute-start.12 = (bf16[24,128,128]{2,1,0:T(8,128)(2,1)S(1)}, bf16[24,128,128]{2,1,0:T(8,128)(2,1)S(1)}, u32[]{:S(2)}, u32[]{:S(2)}) collective-permute-start(bf16[24,128,128]{2,1,0:T(8,128)(2,1)S(1)} %collective-permute-done.3.rest_1_), channel_id=1, source_target_pairs={{0,1},{1,0},{2,3},{3,2},{4,5},{5,4},{6,7},{7,6},{8,9},{9,8},{10,11... | collective-permute-start | bytes 2359304 | tf_op jit(solution)/shard_map/ppermute | solution.py:321
  127.3 0.9 copy-start.1
